TPU v7x, 512 devices: a whole 4x8x8 slice. The times are simulated.
512 devices in a mesh: image: 8 (over x, core), slab: 64 (over z, y).
Axes of the slice: x: 4, y: 8, z: 8, core: 2. Of those that a mesh axis runs over, the one named last changes fastest.
Arguments:
- string: float32 [16, 2048, 4096], P('image', 'slab'), may hold values from -1.2 to 1.2
- tilt: float32 [2048, 4096], P('slab'), may hold values from -0.5 to 0.5
- source_pair: int32 [16], replicated, may hold values from 0 to 14, as said below
Outputs:
- new_string: float32 [16, 2048, 4096], P('image', 'slab')
Inputs may be any that keep to these rules, and one draw needn't show every extreme that they name: source_pair[j] lies between j - 2 and j; the first entry is 0 and the last is 14.
All inputs are finite; a program needn't handle non-finite values.
Results may differ from a plain program's by a relative error of at most 0.00012.
Values sent between devices are 32-bit elements; how exact they have to be, the bound alone decides.
No kernel may reach another device: no remote copies, remote signals or barrier semaphores. Data moves between devices by JAX's collectives and lax.ppermute only.
A program may use at most 64 MiB of HBM per device.

v0:
```python
import jax
import jax.numpy as jnp
from jax import lax
from jax.sharding import PartitionSpec as P

SUBSTEPS = 8


DT = 0.1
EPS = 1e-06


def padded_2(block, sides, width):
    for axis, dim in sides:
        count = lax.axis_size(axis)
        forward = [(i, i + 1) for i in range(count - 1)]
        forward.append((count - 1, 0))
        backward = [(target, source) for source, target in forward]
        low = lax.ppermute(
            lax.slice_in_dim(block, block.shape[dim] - width, None, axis=dim), axis, forward
        )
        high = lax.ppermute(lax.slice_in_dim(block, 0, width, axis=dim), axis, backward)
        block = jnp.concatenate([low, block, high], axis=dim)
    return block


def shifted(block, axis, distance):
    devices = range(lax.axis_size(axis))
    route = [(i - distance, i) for i in devices if i - distance in devices]
    return lax.ppermute(block, axis, route)


def flow(padded, tilt_part):
    middle = padded[:, 1:-1]
    lap = (
        padded[:, 2:]
        + padded[:, :-2]
        + jnp.roll(middle, 1, 2)
        + jnp.roll(middle, -1, 2)
        - 4.0 * middle
    )
    return middle + DT * (lap + middle - middle * middle * middle + tilt_part[None])


def body(string, tilt, source_pair):
    count = string.shape[0]
    depth = string.shape[1]
    field = string
    for step in range(SUBSTEPS):
        padded = padded_2(field, (("slab", 1),), 1)
        field = flow(padded, tilt)
    rank = lax.axis_index("image")
    images_all = count * lax.axis_size("image")
    lower = shifted(field, "image", 1)
    upper = shifted(field, "image", -1)
    n_low = lower.shape[0]
    extended = jnp.concatenate([lower, field, upper], axis=0)
    base = rank * count - n_low
    diffs = extended[n_low + 1 : n_low + count + 1] - extended[n_low : n_low + count]
    partial_sq = jnp.sum(diffs * diffs, axis=(1, 2))
    summed = lax.psum(partial_sq, "slab")
    squares = lax.all_gather(summed, "image", axis=0, tiled=True)
    cells = depth * lax.axis_size("slab") * string.shape[2]
    seg = jnp.sqrt(squares / cells + EPS)
    index_all = jnp.arange(images_all, dtype=jnp.int32)
    seg = jnp.where(index_all < images_all - 1, seg, jnp.float32(0.0))
    arc = jnp.concatenate([jnp.zeros((1,), jnp.float32), jnp.cumsum(seg[:-1])])
    total = arc[images_all - 1]
    first = rank * count
    targets = first + jnp.arange(count, dtype=jnp.int32)
    sources = lax.dynamic_slice_in_dim(source_pair, first, count)
    picker = (sources[:, None] == index_all[None, :]).astype(jnp.float32)
    arc_src = jnp.sum(picker * arc[None, :], axis=1)
    seg_src = jnp.sum(picker * seg[None, :], axis=1)
    ratio = targets.astype(jnp.float32) / (images_all - 1)
    weight = (ratio * total - arc_src) / seg_src
    local = sources - base
    slots = jnp.arange(extended.shape[0], dtype=jnp.int32)
    pick_low = (local[:, None] == slots[None, :]).astype(jnp.float32)
    pick_high = ((local + 1)[:, None] == slots[None, :]).astype(jnp.float32)
    low_img = jnp.einsum("tm,myx->tyx", pick_low, extended, precision=lax.Precision.HIGHEST)
    high_img = jnp.einsum("tm,myx->tyx", pick_high, extended, precision=lax.Precision.HIGHEST)
    weight = weight[:, None, None]
    return (1.0 - weight) * low_img + weight * high_img


def solution(mesh):
    placed = (P("image", "slab", None), P("slab", None), P())
    return jax.shard_map(
        body, mesh=mesh, in_specs=placed, out_specs=P("image", "slab", None), check_vma=False
    )
```

profile of v0, /device:TPU:1, one launch (start us, length us, event | category | flops | bytes accessed | tf_op | source)
XLA Modules:
  0.0 340.4 jit_solution(13387661797103866002)
XLA Ops:
  0.0 2.0 copy.32
  2.1 14.4 %collective-permute-start = (f32[2,1,4096]{2,0,1:T(2,128)S(1)}, f32[2,1,4096]{2,0,1:T(2,128)S(1)}, u32[]{:S(2)}, u32[]{:S(2)}) collective-permute-start(f32[2,1,4096]{2,0,1:T(2,128)S(1)} %get-tuple-element.58), channel_id=1, source_target_pairs={{1,0},{2,1},{3,2},{4,3},{5,4},{6,5},{7,6},{8,7},{9,8},{10,9},{11,1... | collective-permute-start | bytes 98312 | tf_op jit(solution)/shard_map/ppermute | solution.py:22
  16.5 2.1 collective-permute-start.1
  18.5 1.2 fusion.107
  19.7 0.1 fusion.108
  19.9 4.7 %collective-permute-done.1 = f32[2,1,4096]{2,0,1:T(2,128)S(1)} collective-permute-done((f32[2,1,4096]{2,0,1:T(2,128)S(1)}, f32[2,1,4096]{2,0,1:T(2,128)S(1)}, u32[]{:S(2)}, u32[]{:S(2)}) %collective-permute-start.1) | collective-permute-done | bytes 32800 | tf_op jit(solution)/shard_map/ppermute | solution.py:19
  24.6 6.3 %fusion.4 = f32[2,32,4096]{2,0,1:T(2,128)S(1)} fusion(f32[2,32,4096]{2,0,1:T(2,128)S(1)} %copy.32, f32[2,1,4096]{2,0,1:T(2,128)S(1)} %collective-permute-done.1, f32[2,1,4096]{2,0,1:T(2,128)S(1)} %collective-permute-done, f32[2,32,4095]{2,0,1:T(2,128)S(1)} %get-tuple-element.55, f32[2,32,1]{2,0,1:T(2,128)S(1)} %get-tuple-element.57, ...), kind=kLoop, calls=%fused_computation.15 | loop fusion | flops 4194304 | bytes 4784128 | tf_op jit(solution)/shard_map/add | solution.py:42
  30.9 1.2 fusion.104
  32.1 2.0 collective-permute-start.2
  34.1 3.3 collective-permute-start.3
  37.4 0.1 fusion.105
  37.5 4.6 %collective-permute-done.3 = f32[2,1,4096]{2,0,1:T(2,128)S(1)} collective-permute-done((f32[2,1,4096]{2,0,1:T(2,128)S(1)}, f32[2,1,4096]{2,0,1:T(2,128)S(1)}, u32[]{:S(2)}, u32[]{:S(2)}) %collective-permute-start.3) | collective-permute-done | bytes 32800 | tf_op jit(solution)/shard_map/ppermute | solution.py:19
  42.1 6.3 %fusion.8 = f32[2,32,4096]{2,0,1:T(2,128)S(1)} fusion(f32[2,32,4096]{2,0,1:T(2,128)S(1)} %fusion.4, f32[2,1,4096]{2,0,1:T(2,128)S(1)} %collective-permute-done.3, f32[2,1,4096]{2,0,1:T(2,128)S(1)} %collective-permute-done.2, f32[2,32,4095]{2,0,1:T(2,128)S(1)} %get-tuple-element.49, f32[2,32,1]{2,0,1:T(2,128)S(1)} %get-tuple-element.51, ...), kind=kLoop, calls=%fused_computation.19 | loop fusion | flops 4194304 | bytes 4784128 | tf_op jit(solution)/shard_map/add | solution.py:42
  48.4 1.2 fusion.101
  49.7 1.9 collective-permute-start.4
  51.6 3.4 collective-permute-start.5
  55.0 0.1 fusion.102
  55.1 4.5 %collective-permute-done.5 = f32[2,1,4096]{2,0,1:T(2,128)S(1)} collective-permute-done((f32[2,1,4096]{2,0,1:T(2,128)S(1)}, f32[2,1,4096]{2,0,1:T(2,128)S(1)}, u32[]{:S(2)}, u32[]{:S(2)}) %collective-permute-start.5) | collective-permute-done | bytes 32800 | tf_op jit(solution)/shard_map/ppermute | solution.py:19
  59.6 6.3 %fusion.12 = f32[2,32,4096]{2,0,1:T(2,128)S(1)} fusion(f32[2,32,4096]{2,0,1:T(2,128)S(1)} %fusion.8, f32[2,1,4096]{2,0,1:T(2,128)S(1)} %collective-permute-done.5, f32[2,1,4096]{2,0,1:T(2,128)S(1)} %collective-permute-done.4, f32[2,32,4095]{2,0,1:T(2,128)S(1)} %get-tuple-element.43, f32[2,32,1]{2,0,1:T(2,128)S(1)} %get-tuple-element.45, ...), kind=kLoop, calls=%fused_computation.23 | loop fusion | flops 4194304 | bytes 4784128 | tf_op jit(solution)/shard_map/add | solution.py:42
  65.9 1.2 fusion.98
  67.1 1.9 collective-permute-start.6
  69.0 3.5 %collective-permute-start.7 = (f32[2,1,4096]{2,0,1:T(2,128)S(1)}, f32[2,1,4096]{2,0,1:T(2,128)S(1)}, u32[]{:S(2)}, u32[]{:S(2)}) collective-permute-start(f32[2,1,4096]{2,0,1:T(2,128)S(1)} %get-tuple-element.41), channel_id=1, source_target_pairs={{0,1},{1,2},{2,3},{3,4},{4,5},{5,6},{6,7},{7,8},{8,9},{9,10},{10,1... | collective-permute-start | bytes 98312 | tf_op jit(solution)/shard_map/ppermute | solution.py:19
  72.6 0.1 fusion.99
  72.7 4.3 %collective-permute-done.7 = f32[2,1,4096]{2,0,1:T(2,128)S(1)} collective-permute-done((f32[2,1,4096]{2,0,1:T(2,128)S(1)}, f32[2,1,4096]{2,0,1:T(2,128)S(1)}, u32[]{:S(2)}, u32[]{:S(2)}) %collective-permute-start.7) | collective-permute-done | bytes 32800 | tf_op jit(solution)/shard_map/ppermute | solution.py:19
  77.0 6.3 %fusion.16 = f32[2,32,4096]{2,0,1:T(2,128)S(1)} fusion(f32[2,32,4096]{2,0,1:T(2,128)S(1)} %fusion.12, f32[2,1,4096]{2,0,1:T(2,128)S(1)} %collective-permute-done.7, f32[2,1,4096]{2,0,1:T(2,128)S(1)} %collective-permute-done.6, f32[2,32,4095]{2,0,1:T(2,128)S(1)} %get-tuple-element.37, f32[2,32,1]{2,0,1:T(2,128)S(1)} %get-tuple-element.39, ...), kind=kLoop, calls=%fused_computation.27 | loop fusion | flops 4194304 | bytes 4784128 | tf_op jit(solution)/shard_map/add | solution.py:42
  83.4 1.2 fusion.95
  84.6 1.9 collective-permute-start.8
  86.5 3.4 collective-permute-start.9
  89.9 0.1 fusion.96
  90.0 4.5 %collective-permute-done.9 = f32[2,1,4096]{2,0,1:T(2,128)S(1)} collective-permute-done((f32[2,1,4096]{2,0,1:T(2,128)S(1)}, f32[2,1,4096]{2,0,1:T(2,128)S(1)}, u32[]{:S(2)}, u32[]{:S(2)}) %collective-permute-start.9) | collective-permute-done | bytes 32800 | tf_op jit(solution)/shard_map/ppermute | solution.py:19
  94.5 6.3 %fusion.20 = f32[2,32,4096]{2,0,1:T(2,128)S(1)} fusion(f32[2,32,4096]{2,0,1:T(2,128)S(1)} %fusion.16, f32[2,1,4096]{2,0,1:T(2,128)S(1)} %collective-permute-done.9, f32[2,1,4096]{2,0,1:T(2,128)S(1)} %collective-permute-done.8, f32[2,32,4095]{2,0,1:T(2,128)S(1)} %get-tuple-element.31, f32[2,32,1]{2,0,1:T(2,128)S(1)} %get-tuple-element.33, ...), kind=kLoop, calls=%fused_computation.31 | loop fusion | flops 4194304 | bytes 4784128 | tf_op jit(solution)/shard_map/add | solution.py:42
  100.8 1.2 fusion.92
  102.0 1.9 collective-permute-start.10
  104.0 3.4 collective-permute-start.11
  107.3 0.1 fusion.93
  107.4 4.5 %collective-permute-done.11 = f32[2,1,4096]{2,0,1:T(2,128)S(1)} collective-permute-done((f32[2,1,4096]{2,0,1:T(2,128)S(1)}, f32[2,1,4096]{2,0,1:T(2,128)S(1)}, u32[]{:S(2)}, u32[]{:S(2)}) %collective-permute-start.11) | collective-permute-done | bytes 32800 | tf_op jit(solution)/shard_map/ppermute | solution.py:19
  111.9 6.3 %fusion.24 = f32[2,32,4096]{2,0,1:T(2,128)S(1)} fusion(f32[2,32,4096]{2,0,1:T(2,128)S(1)} %fusion.20, f32[2,1,4096]{2,0,1:T(2,128)S(1)} %collective-permute-done.11, f32[2,1,4096]{2,0,1:T(2,128)S(1)} %collective-permute-done.10, f32[2,32,4095]{2,0,1:T(2,128)S(1)} %get-tuple-element.25, f32[2,32,1]{2,0,1:T(2,128)S(1)} %get-tuple-element.27, ...), kind=kLoop, calls=%fused_computation.35 | loop fusion | flops 4194304 | bytes 4784128 | tf_op jit(solution)/shard_map/add | solution.py:42
  118.3 1.2 fusion.89
  119.5 1.9 collective-permute-start.12
  121.4 3.4 collective-permute-start.13
  124.8 0.1 fusion.90
  124.9 4.5 %collective-permute-done.13 = f32[2,1,4096]{2,0,1:T(2,128)S(1)} collective-permute-done((f32[2,1,4096]{2,0,1:T(2,128)S(1)}, f32[2,1,4096]{2,0,1:T(2,128)S(1)}, u32[]{:S(2)}, u32[]{:S(2)}) %collective-permute-start.13) | collective-permute-done | bytes 32800 | tf_op jit(solution)/shard_map/ppermute | solution.py:19
  129.4 6.3 %fusion.28 = f32[2,32,4096]{2,0,1:T(2,128)S(1)} fusion(f32[2,32,4096]{2,0,1:T(2,128)S(1)} %fusion.24, f32[2,1,4096]{2,0,1:T(2,128)S(1)} %collective-permute-done.13, f32[2,1,4096]{2,0,1:T(2,128)S(1)} %collective-permute-done.12, f32[2,32,4095]{2,0,1:T(2,128)S(1)} %get-tuple-element.19, f32[2,32,1]{2,0,1:T(2,128)S(1)} %get-tuple-element.21, ...), kind=kLoop, calls=%fused_computation.39 | loop fusion | flops 4194304 | bytes 4784128 | tf_op jit(solution)/shard_map/add | solution.py:42
  135.7 1.2 fusion.86
  136.9 2.1 collective-permute-start.14
  139.1 3.4 collective-permute-start.15
  142.5 0.1 fusion.87
  142.6 4.5 %collective-permute-done.15 = f32[2,1,4096]{2,0,1:T(2,128)S(1)} collective-permute-done((f32[2,1,4096]{2,0,1:T(2,128)S(1)}, f32[2,1,4096]{2,0,1:T(2,128)S(1)}, u32[]{:S(2)}, u32[]{:S(2)}) %collective-permute-start.15) | collective-permute-done | bytes 32800 | tf_op jit(solution)/shard_map/ppermute | solution.py:19
  147.1 6.3 %fusion.32 = f32[2,32,4096]{2,0,1:T(2,128)S(1)} fusion(f32[2,32,4096]{2,0,1:T(2,128)S(1)} %fusion.28, f32[2,1,4096]{2,0,1:T(2,128)S(1)} %collective-permute-done.15, f32[2,1,4096]{2,0,1:T(2,128)S(1)} %collective-permute-done.14, f32[2,32,4095]{2,0,1:T(2,128)S(1)} %get-tuple-element.13, f32[2,32,1]{2,0,1:T(2,128)S(1)} %get-tuple-element.15, ...), kind=kLoop, calls=%fused_computation.43 | loop fusion | flops 4194304 | bytes 4784128 | tf_op jit(solution)/shard_map/add | solution.py:42
  153.4 12.0 %collective-permute-start.16 = (f32[2,32,4096]{2,0,1:T(2,128)S(1)}, f32[2,32,4096]{2,0,1:T(2,128)S(1)}, u32[]{:S(2)}, u32[]{:S(2)}) collective-permute-start(f32[2,32,4096]{2,0,1:T(2,128)S(1)} %fusion.32), channel_id=1, source_target_pairs={{64,0},{128,64},{192,128},{256,192},{320,256},{384,320},{448,384},... | collective-permute-start | bytes 3145736 | tf_op jit(solution)/shard_map/ppermute | solution.py:30
  165.4 1.3 dynamic-slice
  166.7 3.0 collective-permute-start.17
  169.8 9.5 %collective-permute-done.16 = f32[2,32,4096]{2,0,1:T(2,128)S(1)} collective-permute-done((f32[2,32,4096]{2,0,1:T(2,128)S(1)}, f32[2,32,4096]{2,0,1:T(2,128)S(1)}, u32[]{:S(2)}, u32[]{:S(2)}) %collective-permute-start.16) | collective-permute-done | bytes 1048608 | tf_op jit(solution)/shard_map/ppermute | solution.py:30
  179.2 1.6 fusion.75
  181.5 110.5 %psum.7 = f32[2]{0:T(128)S(1)} all-reduce(f32[2]{0:T(128)S(1)} %fusion.75), channel_id=1, replica_groups=mesh['image'=8,'slab'=64] {'slab'}, use_global_device_ids=true, to_apply=%region_1.2 | all-reduce | flops 2 | bytes 16 | tf_op jit(solution)/shard_map/psum | solution.py:61
  292.0 0.2 dynamic-update-slice
  292.3 37.6 %all-reduce = f32[16]{0:T(128)S(1)} all-reduce(f32[16]{0:T(128)S(1)} %dynamic-update-slice), channel_id=1, replica_groups=mesh['image'=8,'slab'=64] {'image'}, use_global_device_ids=true, to_apply=%add | all-reduce | flops 16 | bytes 128
  329.8 0.2 reduce-window.4
  330.0 0.6 slice.289
  331.3 0.1 pad_maximum_fusion.20
  331.3 0.2 select_reduce_fusion.1
  331.5 3.4 %convolution_multiply_fusion = f32[2,32,4096]{2,0,1:T(2,128)S(1)} fusion(f32[2,32,4096]{2,0,1:T(2,128)S(1)} %collective-permute-done.16, f32[2,32,4096]{2,0,1:T(2,128)S(1)} %fusion.32, f32[2,32,4096]{2,0,1:T(2,128)S(1)} %collective-permute-done.17, f32[2]{0:T(128)S(1)} %get-tuple-element.8, s32[2]{0:T(128)S(1)} %get-tuple-element.9), kind=kOutput, calls=%fused_computation | convolution fusion | flops 20709388 | bytes 4194320 | tf_op jit(solution)/shard_map/tm,myx->tyx/dot_general | solution.py:82
  335.0 3.8 %fusion = f32[2,32,4096]{2,0,1:T(2,128)S(1)} fusion(f32[2,32,4096]{2,0,1:T(2,128)S(1)} %convolution_multiply_fusion, f32[2,32,4096]{2,0,1:T(2,128)S(1)} %collective-permute-done.16, f32[2,32,4096]{2,0,1:T(2,128)S(1)} %fusion.32, f32[2,32,4096]{2,0,1:T(2,128)S(1)} %collective-permute-done.17, f32[2]{0:T(128)S(1)} %get-tuple-element.7, s32[2]{0:T(128)S(1)} %get-tuple-element.10), kind=kOutput, calls=%fused_computation.2 | convolution fusion | flops 20971532 | bytes 5242896 | tf_op jit(solution)/shard_map/tm,myx->tyx/dot_general | solution.py:81
  338.8 1.6 copy.33
  (26 shorter events, 0.2 us)
Async XLA Ops:
  2.1 17.8 %collective-permute-start = (f32[2,1,4096]{2,0,1:T(2,128)S(1)}, f32[2,1,4096]{2,0,1:T(2,128)S(1)}, u32[]{:S(2)}, u32[]{:S(2)}) collective-permute-start(f32[2,1,4096]{2,0,1:T(2,128)S(1)} %get-tuple-element.58), channel_id=1, source_target_pairs={{1,0},{2,1},{3,2},{4,3},{5,4},{6,5},{7,6},{8,7},{9,8},{10,9},{11,1... | collective-permute-start | bytes 98312 | tf_op jit(solution)/shard_map/ppermute | solution.py:22
  16.5 8.1 %copy-start = (f32[32,4096]{1,0:T(8,128)S(1)}, f32[32,4096]{1,0:T(8,128)}, u32[]{:S(2)}) copy-start(f32[32,4096]{1,0:T(8,128)} %param.4) | copy-start | bytes 1572868
  16.5 8.1 %collective-permute-start.1 = (f32[2,1,4096]{2,0,1:T(2,128)S(1)}, f32[2,1,4096]{2,0,1:T(2,128)S(1)}, u32[]{:S(2)}, u32[]{:S(2)}) collective-permute-start(f32[2,1,4096]{2,0,1:T(2,128)S(1)} %get-tuple-element.59), channel_id=1, source_target_pairs={{0,1},{1,2},{2,3},{3,4},{4,5},{5,6},{6,7},{7,8},{8,9},{9,10},{10,1... | collective-permute-start | bytes 98312 | tf_op jit(solution)/shard_map/ppermute | solution.py:19
  32.1 5.4 %collective-permute-start.2 = (f32[2,1,4096]{2,0,1:T(2,128)S(1)}, f32[2,1,4096]{2,0,1:T(2,128)S(1)}, u32[]{:S(2)}, u32[]{:S(2)}) collective-permute-start(f32[2,1,4096]{2,0,1:T(2,128)S(1)} %get-tuple-element.52), channel_id=1, source_target_pairs={{1,0},{2,1},{3,2},{4,3},{5,4},{6,5},{7,6},{8,7},{9,8},{10,9},{11,1... | collective-permute-start | bytes 98312 | tf_op jit(solution)/shard_map/ppermute | solution.py:22
  34.1 8.0 %collective-permute-start.3 = (f32[2,1,4096]{2,0,1:T(2,128)S(1)}, f32[2,1,4096]{2,0,1:T(2,128)S(1)}, u32[]{:S(2)}, u32[]{:S(2)}) collective-permute-start(f32[2,1,4096]{2,0,1:T(2,128)S(1)} %get-tuple-element.53), channel_id=1, source_target_pairs={{0,1},{1,2},{2,3},{3,4},{4,5},{5,6},{6,7},{7,8},{8,9},{9,10},{10,1... | collective-permute-start | bytes 98312 | tf_op jit(solution)/shard_map/ppermute | solution.py:19
  49.7 5.4 %collective-permute-start.4 = (f32[2,1,4096]{2,0,1:T(2,128)S(1)}, f32[2,1,4096]{2,0,1:T(2,128)S(1)}, u32[]{:S(2)}, u32[]{:S(2)}) collective-permute-start(f32[2,1,4096]{2,0,1:T(2,128)S(1)} %get-tuple-element.46), channel_id=1, source_target_pairs={{1,0},{2,1},{3,2},{4,3},{5,4},{6,5},{7,6},{8,7},{9,8},{10,9},{11,1... | collective-permute-start | bytes 98312 | tf_op jit(solution)/shard_map/ppermute | solution.py:22
  51.6 8.0 %collective-permute-start.5 = (f32[2,1,4096]{2,0,1:T(2,128)S(1)}, f32[2,1,4096]{2,0,1:T(2,128)S(1)}, u32[]{:S(2)}, u32[]{:S(2)}) collective-permute-start(f32[2,1,4096]{2,0,1:T(2,128)S(1)} %get-tuple-element.47), channel_id=1, source_target_pairs={{0,1},{1,2},{2,3},{3,4},{4,5},{5,6},{6,7},{7,8},{8,9},{9,10},{10,1... | collective-permute-start | bytes 98312 | tf_op jit(solution)/shard_map/ppermute | solution.py:19
  67.1 5.6 %collective-permute-start.6 = (f32[2,1,4096]{2,0,1:T(2,128)S(1)}, f32[2,1,4096]{2,0,1:T(2,128)S(1)}, u32[]{:S(2)}, u32[]{:S(2)}) collective-permute-start(f32[2,1,4096]{2,0,1:T(2,128)S(1)} %get-tuple-element.40), channel_id=1, source_target_pairs={{1,0},{2,1},{3,2},{4,3},{5,4},{6,5},{7,6},{8,7},{9,8},{10,9},{11,1... | collective-permute-start | bytes 98312 | tf_op jit(solution)/shard_map/ppermute | solution.py:22
  69.0 8.0 %collective-permute-start.7 = (f32[2,1,4096]{2,0,1:T(2,128)S(1)}, f32[2,1,4096]{2,0,1:T(2,128)S(1)}, u32[]{:S(2)}, u32[]{:S(2)}) collective-permute-start(f32[2,1,4096]{2,0,1:T(2,128)S(1)} %get-tuple-element.41), channel_id=1, source_target_pairs={{0,1},{1,2},{2,3},{3,4},{4,5},{5,6},{6,7},{7,8},{8,9},{9,10},{10,1... | collective-permute-start | bytes 98312 | tf_op jit(solution)/shard_map/ppermute | solution.py:19
  84.6 5.4 %collective-permute-start.8 = (f32[2,1,4096]{2,0,1:T(2,128)S(1)}, f32[2,1,4096]{2,0,1:T(2,128)S(1)}, u32[]{:S(2)}, u32[]{:S(2)}) collective-permute-start(f32[2,1,4096]{2,0,1:T(2,128)S(1)} %get-tuple-element.34), channel_id=1, source_target_pairs={{1,0},{2,1},{3,2},{4,3},{5,4},{6,5},{7,6},{8,7},{9,8},{10,9},{11,1... | collective-permute-start | bytes 98312 | tf_op jit(solution)/shard_map/ppermute | solution.py:22
  86.5 8.0 %collective-permute-start.9 = (f32[2,1,4096]{2,0,1:T(2,128)S(1)}, f32[2,1,4096]{2,0,1:T(2,128)S(1)}, u32[]{:S(2)}, u32[]{:S(2)}) collective-permute-start(f32[2,1,4096]{2,0,1:T(2,128)S(1)} %get-tuple-element.35), channel_id=1, source_target_pairs={{0,1},{1,2},{2,3},{3,4},{4,5},{5,6},{6,7},{7,8},{8,9},{9,10},{10,1... | collective-permute-start | bytes 98312 | tf_op jit(solution)/shard_map/ppermute | solution.py:19
  102.0 5.4 %collective-permute-start.10 = (f32[2,1,4096]{2,0,1:T(2,128)S(1)}, f32[2,1,4096]{2,0,1:T(2,128)S(1)}, u32[]{:S(2)}, u32[]{:S(2)}) collective-permute-start(f32[2,1,4096]{2,0,1:T(2,128)S(1)} %get-tuple-element.28), channel_id=1, source_target_pairs={{1,0},{2,1},{3,2},{4,3},{5,4},{6,5},{7,6},{8,7},{9,8},{10,9},{11,1... | collective-permute-start | bytes 98312 | tf_op jit(solution)/shard_map/ppermute | solution.py:22
  104.0 8.0 %collective-permute-start.11 = (f32[2,1,4096]{2,0,1:T(2,128)S(1)}, f32[2,1,4096]{2,0,1:T(2,128)S(1)}, u32[]{:S(2)}, u32[]{:S(2)}) collective-permute-start(f32[2,1,4096]{2,0,1:T(2,128)S(1)} %get-tuple-element.29), channel_id=1, source_target_pairs={{0,1},{1,2},{2,3},{3,4},{4,5},{5,6},{6,7},{7,8},{8,9},{9,10},{10,1... | collective-permute-start | bytes 98312 | tf_op jit(solution)/shard_map/ppermute | solution.py:19
  119.5 5.4 %collective-permute-start.12 = (f32[2,1,4096]{2,0,1:T(2,128)S(1)}, f32[2,1,4096]{2,0,1:T(2,128)S(1)}, u32[]{:S(2)}, u32[]{:S(2)}) collective-permute-start(f32[2,1,4096]{2,0,1:T(2,128)S(1)} %get-tuple-element.22), channel_id=1, source_target_pairs={{1,0},{2,1},{3,2},{4,3},{5,4},{6,5},{7,6},{8,7},{9,8},{10,9},{11,1... | collective-permute-start | bytes 98312 | tf_op jit(solution)/shard_map/ppermute | solution.py:22
  121.4 8.0 %collective-permute-start.13 = (f32[2,1,4096]{2,0,1:T(2,128)S(1)}, f32[2,1,4096]{2,0,1:T(2,128)S(1)}, u32[]{:S(2)}, u32[]{:S(2)}) collective-permute-start(f32[2,1,4096]{2,0,1:T(2,128)S(1)} %get-tuple-element.23), channel_id=1, source_target_pairs={{0,1},{1,2},{2,3},{3,4},{4,5},{5,6},{6,7},{7,8},{8,9},{9,10},{10,1... | collective-permute-start | bytes 98312 | tf_op jit(solution)/shard_map/ppermute | solution.py:19
  136.9 5.6 %collective-permute-start.14 = (f32[2,1,4096]{2,0,1:T(2,128)S(1)}, f32[2,1,4096]{2,0,1:T(2,128)S(1)}, u32[]{:S(2)}, u32[]{:S(2)}) collective-permute-start(f32[2,1,4096]{2,0,1:T(2,128)S(1)} %get-tuple-element.16), channel_id=1, source_target_pairs={{1,0},{2,1},{3,2},{4,3},{5,4},{6,5},{7,6},{8,7},{9,8},{10,9},{11,1... | collective-permute-start | bytes 98312 | tf_op jit(solution)/shard_map/ppermute | solution.py:22
  139.1 8.0 %collective-permute-start.15 = (f32[2,1,4096]{2,0,1:T(2,128)S(1)}, f32[2,1,4096]{2,0,1:T(2,128)S(1)}, u32[]{:S(2)}, u32[]{:S(2)}) collective-permute-start(f32[2,1,4096]{2,0,1:T(2,128)S(1)} %get-tuple-element.17), channel_id=1, source_target_pairs={{0,1},{1,2},{2,3},{3,4},{4,5},{5,6},{6,7},{7,8},{8,9},{9,10},{10,1... | collective-permute-start | bytes 98312 | tf_op jit(solution)/shard_map/ppermute | solution.py:19
  147.1 19.6 %copy-start.1 = (s32[16]{0:T(128)S(1)}, s32[16]{0:T(128)}, u32[]{:S(2)}) copy-start(s32[16]{0:T(128)} %param.5) | copy-start | bytes 196
  153.4 25.9 %collective-permute-start.16 = (f32[2,32,4096]{2,0,1:T(2,128)S(1)}, f32[2,32,4096]{2,0,1:T(2,128)S(1)}, u32[]{:S(2)}, u32[]{:S(2)}) collective-permute-start(f32[2,32,4096]{2,0,1:T(2,128)S(1)} %fusion.32), channel_id=1, source_target_pairs={{64,0},{128,64},{192,128},{256,192},{320,256},{384,320},{448,384},... | collective-permute-start | bytes 3145736 | tf_op jit(solution)/shard_map/ppermute | solution.py:30
  166.7 164.8 %collective-permute-start.17 = (f32[2,32,4096]{2,0,1:T(2,128)S(1)}, f32[2,32,4096]{2,0,1:T(2,128)S(1)}, u32[]{:S(2)}, u32[]{:S(2)}) collective-permute-start(f32[2,32,4096]{2,0,1:T(2,128)S(1)} %fusion.32), channel_id=1, source_target_pairs={{0,64},{64,128},{128,192},{192,256},{256,320},{320,384},{384,448},... | collective-permute-start | bytes 3145736 | tf_op jit(solution)/shard_map/ppermute | solution.py:30
where the time goes:
time: 341 us; the launch traced here: 340 us
  blocking collectives  148 us (43%)
  starting transfers between devices  68.8 us (20%)
  other arithmetic  52.7 us (15%)
  waiting for transfers between devices  45.6 us (13%)
  local copies, waits for them, and re-layouts  16.1 us (5%)
  matrix products  7.23 us (2%)
    psum x1, blocking collectives, body(): summed = lax.psum(partial_sq, 'slab')  111 us
    add x8, other arithmetic, flow(): middle + DT * (lap + middle - middle * middle * middle + tilt_part[None])  50.6 us
    unnamed x1, blocking collectives  37.6 us
    ppermute x8, waiting for transfers between devices, padded_2(): lax.ppermute(lax.slice_in_dim(block, block.shape[dim] - width, None, axis...  36.1 us
    ppermute x8, starting transfers between devices, padded_2(): lax.ppermute(lax.slice_in_dim(block, 0, width, axis=dim), axis, backward)  28.1 us
    ppermute x8, starting transfers between devices, padded_2(): lax.ppermute(lax.slice_in_dim(block, block.shape[dim] - width, None, axis...  25.7 us
    ppermute x2, starting transfers between devices, shifted(): return lax.ppermute(block, axis, route)  15 us
    slice x16, local copies, waits for them, and re-layouts, flow(): jnp.roll(middle, -1, 2)  10.4 us
  transfers between devices with their start and end apart: 18, of which 9 were waited for; matrix products, arithmetic and copies ran while one was open for 2% of the time, Pallas kernels for 0%

commit v1 on v0

v1 whole, which is shorter than its diff:
```python
import functools

import jax
import jax.numpy as jnp
from jax import lax
from jax.experimental import pallas as pl
from jax.experimental.pallas import tpu as pltpu
from jax.sharding import PartitionSpec as P

SUBSTEPS = 8
DT = 0.1
EPS = 1e-06
LANES = 128
ROWS = 8
CHUNK = 8
VMEM_LIMIT = 48 * 1024 * 1024


def ring(axis, distance):
    count = lax.axis_size(axis)
    return [(i, (i + distance) % count) for i in range(count)]


def line(axis, distance):
    devices = range(lax.axis_size(axis))
    return [(i, i + distance) for i in devices if i + distance in devices]


def substep(source, target, tilt, row, blocks):
    lane = lax.broadcasted_iota(jnp.int32, (ROWS, LANES), 1)
    is_first = lane == 0
    is_last = lane == LANES - 1
    columns = blocks

    def chunk(index, carry):
        base = index * CHUNK
        places = [
            lax.rem(base + (j - 1 + columns), columns) if j in (0, CHUNK + 1) else base + (j - 1)
            for j in range(CHUNK + 2)
        ]
        forces = [tilt[places[j], pl.ds(row, ROWS), :] for j in range(1, CHUNK + 1)]
        for image in range(2):
            middle = [source[image, place, pl.ds(row, ROWS), :] for place in places]
            right_moved = [pltpu.roll(m, 1, 1) for m in middle[:-1]]
            left_moved = [pltpu.roll(m, LANES - 1, 1) for m in middle[1:]]
            for j in range(1, CHUNK + 1):
                u = middle[j]
                left = jnp.where(is_first, right_moved[j - 1], right_moved[j])
                right = jnp.where(is_last, left_moved[j], left_moved[j - 1])
                above = source[image, places[j], pl.ds(row - 1, ROWS), :]
                below = source[image, places[j], pl.ds(row + 1, ROWS), :]
                near = (above + below) + (left + right)
                target[image, places[j], pl.ds(row, ROWS), :] = (
                    u * (0.7 - DT * (u * u)) + (DT * near + forces[j - 1])
                )
        return carry

    lax.fori_loop(0, columns // CHUNK, chunk, 0)


def flow_kernel(string, tilt, low, high, first, second, even, odd, force):
    depth = string.shape[1]
    columns = string.shape[2] // LANES
    extended = depth + 2 * ROWS

    def load(c, carry):
        place = pl.ds(pl.multiple_of(c * LANES, LANES), LANES)
        for image in range(2):
            even[image, c, pl.ds(0, ROWS), :] = low[image, :, place]
            even[image, c, pl.ds(ROWS, depth), :] = string[image, :, place]
            even[image, c, pl.ds(ROWS + depth, ROWS), :] = high[image, :, place]
        force[c, pl.ds(0, ROWS), :] = DT * low[2, :, place]
        force[c, pl.ds(ROWS, depth), :] = DT * tilt[:, place]
        force[c, pl.ds(ROWS + depth, ROWS), :] = DT * high[2, :, place]
        return carry

    lax.fori_loop(0, columns, load, 0)
    buffers = (even, odd)
    for step in range(1, SUBSTEPS + 1):
        source, target = buffers[(step - 1) % 2], buffers[step % 2]
        last = extended - step - ROWS
        starts = sorted(set(list(range(step, last, ROWS)) + [last]))
        for row in starts:
            substep(source, target, force, row, columns)
    done = buffers[SUBSTEPS % 2]

    def store(c, carry):
        first[c] = done[0, c, pl.ds(ROWS, depth), :]
        second[c] = done[1, c, pl.ds(ROWS, depth), :]
        return carry

    lax.fori_loop(0, columns, store, 0)


def square_kernel(first, second, lower, out):
    columns = first.shape[0]
    shape = first.shape[1:]

    def one(c, sums):
        before = first[c] - lower[c]
        after = second[c] - first[c]
        return sums[0] + before * before, sums[1] + after * after

    zero = jnp.zeros(shape, jnp.float32)
    before, after = lax.fori_loop(0, columns, one, (zero, zero), unroll=4)
    before = jnp.sum(before, axis=(0, 1), keepdims=True)
    after = jnp.sum(after, axis=(0, 1), keepdims=True)
    lane = lax.broadcasted_iota(jnp.int32, (1, LANES), 1)
    row = jnp.where(lane == 0, before, jnp.where(lane == 1, after, 0.0))
    out[...] = jnp.broadcast_to(row[None], out.shape)


def total_kernel(parts, out):
    out[...] = jnp.broadcast_to(jnp.sum(parts[...], axis=0, keepdims=True), out.shape)


def mix_kernel(cells, images, rank, sources, squares, low_2, low_1, own_0, own_1, high_1, out):
    columns = own_0.shape[0]
    rows = squares.shape[0]
    squares = squares[...].reshape(rows, LANES)
    lane = lax.broadcasted_iota(jnp.int32, (rows, LANES), 1)
    index = 2 * lax.broadcasted_iota(jnp.int32, (rows, LANES), 0) - 1 + lane
    used = (lane < 2) & (index >= 0) & (index < images - 1)
    seg = jnp.where(used, jnp.sqrt(squares / cells + EPS), 0.0)
    total = jnp.sum(seg, axis=(0, 1), keepdims=True)
    first = 2 * rank[0]
    shares = []
    for t in range(2):
        target = first + t
        source = sources[target]
        arc = jnp.sum(jnp.where(index < source, seg, 0.0), axis=(0, 1), keepdims=True)
        length = jnp.sum(jnp.where(index == source, seg, 0.0), axis=(0, 1), keepdims=True)
        ratio = target.astype(jnp.float32) / (images - 1)
        weight = (ratio * total - arc) / length
        place = source - (first - 2)
        shares.append(
            [
                jnp.where(place == m, 1.0 - weight, 0.0) + jnp.where(place + 1 == m, weight, 0.0)
                for m in range(5)
            ]
        )

    def one(c, carry):
        fields = [ref[c] for ref in (low_2, low_1, own_0, own_1, high_1)]
        place = pl.ds(pl.multiple_of(c * LANES, LANES), LANES)
        for t in range(2):
            result = shares[t][0] * fields[0]
            for m in range(1, 5):
                result = result + shares[t][m] * fields[m]
            out[t, :, place] = result
        return carry

    lax.fori_loop(0, columns, one, 0)


def call(kernel, shapes, count, scratch=(), smem=0):
    vmem = pl.BlockSpec(memory_space=pltpu.VMEM)
    return pl.pallas_call(
        kernel,
        out_shape=shapes,
        in_specs=[pl.BlockSpec(memory_space=pltpu.SMEM)] * smem + [vmem] * count,
        out_specs=jax.tree.map(lambda _: vmem, shapes),
        scratch_shapes=list(scratch),
        compiler_params=pltpu.CompilerParams(vmem_limit_bytes=VMEM_LIMIT),
    )


def body(string, tilt, source_pair):
    count, depth, width = string.shape
    columns = width // LANES
    slabs = lax.axis_size("slab")
    ranks = lax.axis_size("image")
    up = jnp.concatenate([string[:, depth - ROWS :], tilt[None, depth - ROWS :]], axis=0)
    down = jnp.concatenate([string[:, :ROWS], tilt[None, :ROWS]], axis=0)
    low = lax.ppermute(up, "slab", ring("slab", 1))
    high = lax.ppermute(down, "slab", ring("slab", -1))
    field = jax.ShapeDtypeStruct((columns, depth, LANES), jnp.float32)
    extended = depth + 2 * ROWS
    first, second = call(
        flow_kernel,
        (field, field),
        4,
        [
            pltpu.VMEM((2, columns, extended, LANES), jnp.float32),
            pltpu.VMEM((2, columns, extended, LANES), jnp.float32),
            pltpu.VMEM((columns, extended, LANES), jnp.float32),
        ],
    )(string, tilt, low, high)
    low_1 = lax.ppermute(second, "image", line("image", 1))
    high_1 = lax.ppermute(first, "image", line("image", -1))
    low_2 = lax.ppermute(first, "image", line("image", 1))
    parts = call(square_kernel, jax.ShapeDtypeStruct((slabs, 1, LANES), jnp.float32), 3)(
        first, second, low_1
    )
    parts = lax.all_to_all(parts, "slab", 0, 0)
    sums = call(total_kernel, jax.ShapeDtypeStruct((ranks, 1, LANES), jnp.float32), 1)(parts)
    sums = lax.all_to_all(sums, "image", 0, 0)
    rank = lax.axis_index("image").reshape(1)
    cells = depth * slabs * width
    return call(
        functools.partial(mix_kernel, cells, count * ranks),
        jax.ShapeDtypeStruct(string.shape, jnp.float32),
        6,
        smem=2,
    )(rank, source_pair, sums, low_2, low_1, first, second, high_1)


def solution(mesh):
    placed = (P("image", "slab", None), P("slab", None), P())
    return jax.shard_map(
        body, mesh=mesh, in_specs=placed, out_specs=P("image", "slab", None), check_vma=False
    )
```

time: 341 us -> 90.3 us (0.26)
  blocking collectives: 148 us -> 19 us
  other arithmetic: 52.7 us -> 0.06 us
  starting transfers between devices: 68.8 us -> 33.7 us
  waiting for transfers between devices: 45.6 us -> 12.8 us
  Pallas kernels: 0 us -> 22.3 us
  local copies, waits for them, and re-layouts: 16.1 us -> 2.07 us
  matrix products: 7.23 us -> 0 us
    psum x1 -> x0, blocking collectives: 111 us -> none  [body(): summed = lax.psum(partial_sq, 'slab')]
    add x9 -> x0, other arithmetic: 50.6 us -> none  [the longest x8 50.6 us: flow(): middle + DT * (lap + middle - middle * middle * middle + tilt_part[None])]
    ppermute x18 -> x5, starting transfers between devices: 68.8 us -> 26.6 us  [the longest x1 12.3 us: body(): high = lax.ppermute(down, 'slab', ring('slab', -1))]
    unnamed x1 -> x0, blocking collectives: 37.6 us -> none
    ppermute x18 -> x5, waiting for transfers between devices: 45.6 us -> 8.29 us  [the longest x1 6.86 us: body(): low = lax.ppermute(up, 'slab', ring('slab', 1))]
    pallas_call x0 -> x4, Pallas kernels: none -> 22.3 us  [the longest x1 19.3 us: body(): call(flow_kernel, (field, field), 4, [pltpu.VMEM((2, columns, extended, L...]
    all_to_all x0 -> x1, blocking collectives: none -> 19 us  [body(): parts = lax.all_to_all(parts, 'slab', 0, 0)]
    slice x25 -> x1, local copies, waits for them, and re-layouts: 11 us -> 1.07 us  [body(): down = jnp.concatenate([string[:, :ROWS], tilt[None, :ROWS]], axis=0)]
  transfers between devices with their start and end apart: 18 -> 6, of which waited for: 9 -> 4; matrix products, arithmetic and copies ran while one was open for 2% -> 0% of each run, Pallas kernels for 0% -> 1%
where the time goes in v1:
time: 90.3 us; the launch traced here: 90 us
  starting transfers between devices  33.7 us (37%)
  Pallas kernels  22.3 us (25%)
  blocking collectives  19 us (21%)
  waiting for transfers between devices  12.8 us (14%)
  local copies, waits for them, and re-layouts  2.07 us (2%)
    pallas_call x1, Pallas kernels, body(): call(flow_kernel, (field, field), 4, [pltpu.VMEM((2, columns, extended, L...  19.3 us
    all_to_all x1, blocking collectives, body(): parts = lax.all_to_all(parts, 'slab', 0, 0)  19 us
    ppermute x1, starting transfers between devices, body(): high = lax.ppermute(down, 'slab', ring('slab', -1))  12.3 us
    all_to_all x1, starting transfers between devices, body(): sums = lax.all_to_all(sums, 'image', 0, 0)  7.11 us
    ppermute x1, waiting for transfers between devices, body(): low = lax.ppermute(up, 'slab', ring('slab', 1))  6.86 us
    ppermute x1, starting transfers between devices, body(): low_1 = lax.ppermute(second, 'image', line('image', 1))  4.55 us
    all_to_all x1, waiting for transfers between devices, body(): sums = lax.all_to_all(sums, 'image', 0, 0)  4.48 us
    ppermute x1, starting transfers between devices, body(): low = lax.ppermute(up, 'slab', ring('slab', 1))  4.17 us
  transfers between devices with their start and end apart: 6, of which 4 were waited for; matrix products, arithmetic and copies ran while one was open for 0% of the time, Pallas kernels for 1%

profile of v1, /device:TPU:1, one launch (start us, length us, event | category | flops | bytes accessed | tf_op | source)
XLA Modules:
  0.0 90.0 jit_solution(15464656426287686667)
XLA Ops:
  0.0 1.0 %slice_bitcast_fusion = (f32[1,8,4096]{2,1,0:T(8,128)S(1)}, f32[1,8,4096]{2,1,0:T(8,128)S(1)}) fusion(f32[32,4096]{1,0:T(8,128)} %tilt.1), kind=kLoop, calls=%fused_computation.2 | loop fusion | bytes 524288 | tf_op jit(solution)/shard_map/broadcast_in_dim | solution.py:174
  1.0 1.1 %fusion = (f32[2,8,4096]{2,1,0:T(8,128)S(1)}, f32[2,8,4096]{2,1,0:T(8,128)S(1)}) fusion(f32[2,32,4096]{2,1,0:T(8,128)} %string.1), kind=kLoop, calls=%fused_computation.4 | loop fusion | bytes 1048576 | tf_op jit(solution)/shard_map/slice | solution.py:174
  2.1 0.0 copy-start
  2.1 0.0 copy-start.1
  2.1 4.2 %collective-permute-start = (f32[3,8,4096]{2,1,0:T(8,128)S(1)}, f32[3,8,4096]{2,1,0:T(8,128)S(1)}, u32[]{:S(2)}, u32[]{:S(2)}) collective-permute-start(f32[3,8,4096]{2,1,0:T(8,128)S(1)} %pad_maximum_fusion), channel_id=1, source_target_pairs={{0,1},{1,2},{2,3},{3,4},{4,5},{5,6},{6,7},{7,8},{8,9},{9,10},{10,1... | collective-permute-start | bytes 1179656 | tf_op jit(solution)/shard_map/ppermute | solution.py:175
  6.3 12.3 %collective-permute-start.1 = (f32[3,8,4096]{2,1,0:T(8,128)S(1)}, f32[3,8,4096]{2,1,0:T(8,128)S(1)}, u32[]{:S(2)}, u32[]{:S(2)}) collective-permute-start(f32[3,8,4096]{2,1,0:T(8,128)S(1)} %pad_maximum_fusion.1), channel_id=1, source_target_pairs={{0,63},{1,0},{2,1},{3,2},{4,3},{5,4},{6,5},{7,6},{8,7},{9,8},{10,9... | collective-permute-start | bytes 1179656 | tf_op jit(solution)/shard_map/ppermute | solution.py:176
  18.6 6.9 %collective-permute-done.low = f32[3,8,4096]{2,1,0:T(8,128)S(1)} collective-permute-done((f32[3,8,4096]{2,1,0:T(8,128)S(1)}, f32[3,8,4096]{2,1,0:T(8,128)S(1)}, u32[]{:S(2)}, u32[]{:S(2)}) %collective-permute-start) | collective-permute-done | bytes 393248 | tf_op jit(solution)/shard_map/ppermute | solution.py:175
  25.5 0.9 collective-permute-done.1.high
  26.4 0.0 copy-done
  26.4 0.0 copy-done.1
  26.4 19.3 %shard_map.37 = (f32[32,32,128]{2,1,0:T(8,128)S(1)}, f32[32,32,128]{2,1,0:T(8,128)S(1)}) custom-call(f32[2,32,4096]{2,1,0:T(8,128)S(1)} %copy-done, f32[32,4096]{1,0:T(8,128)S(1)} %copy-done.1, f32[3,8,4096]{2,1,0:T(8,128)S(1)} %collective-permute-done.low, f32[3,8,4096]{2,1,0:T(8,128)S(1)} %collective-permute-done.1.high), custom_call_target="tpu_custom_call" | custom-call | tf_op jit(solution)/shard_map/pallas_call | solution.py:179
  45.7 4.6 %collective-permute-start.2 = (f32[32,32,128]{2,1,0:T(8,128)S(1)}, f32[32,32,128]{2,1,0:T(8,128)S(1)}, u32[]{:S(2)}, u32[]{:S(2)}) collective-permute-start(f32[32,32,128]{2,1,0:T(8,128)S(1)} %get-tuple-element.8.second.own_1), channel_id=1, source_target_pairs={{0,64},{64,128},{128,192},{192,256},{256,320},{320,384},{384,448},... | collective-permute-start | bytes 1572872 | tf_op jit(solution)/shard_map/ppermute | solution.py:189
  50.2 1.9 %collective-permute-start.4 = (f32[32,32,128]{2,1,0:T(8,128)S(1)}, f32[32,32,128]{2,1,0:T(8,128)S(1)}, u32[]{:S(2)}, u32[]{:S(2)}) collective-permute-start(f32[32,32,128]{2,1,0:T(8,128)S(1)} %get-tuple-element.7.first.own_0), channel_id=1, source_target_pairs={{64,0},{128,64},{192,128},{256,192},{320,256},{384,320},{448,384},... | collective-permute-start | bytes 1572872 | tf_op jit(solution)/shard_map/ppermute | solution.py:190
  52.2 3.6 %collective-permute-start.3 = (f32[32,32,128]{2,1,0:T(8,128)S(1)}, f32[32,32,128]{2,1,0:T(8,128)S(1)}, u32[]{:S(2)}, u32[]{:S(2)}) collective-permute-start(f32[32,32,128]{2,1,0:T(8,128)S(1)} %get-tuple-element.7.first.own_0), channel_id=1, source_target_pairs={{0,64},{64,128},{128,192},{192,256},{256,320},{320,384},{384,448},... | collective-permute-start | bytes 1572872 | tf_op jit(solution)/shard_map/ppermute | solution.py:191
  55.8 0.5 collective-permute-done.2.lower.low_1
  56.4 0.3 shard_map.38
  56.6 19.0 %all_to_all.10.parts = f32[64,1,128]{2,1,0:T(1,128)S(1)} all-to-all(f32[64,1,128]{2,1,0:T(1,128)S(1)} %shard_map.38), channel_id=1, replica_groups=mesh['image'=8,'slab'=64] {'slab'}, dimensions={0} | all-to-all | bytes 65536 | tf_op jit(solution)/shard_map/all_to_all | solution.py:195
  75.6 0.7 shard_map.39
  76.3 7.1 %all-to-all-start.1 = ((f32[8,1,128]{2,1,0:T(1,128)}), f32[8,1,128]{2,1,0:T(1,128)S(1)}, u32[]{:S(2)}, u32[]{:S(2)}) async-start(f32[8,1,128]{2,1,0:T(1,128)} %shard_map.39), calls=%async_computation.1 | async-start | bytes 8192 | tf_op jit(solution)/shard_map/all_to_all | solution.py:197
  83.4 0.0 copy-start.2
  83.4 0.0 collective-permute-done.4.high_1
  83.4 0.0 collective-permute-done.3.low_2
  83.4 4.5 %all-to-all-done.1.squares = f32[8,1,128]{2,1,0:T(1,128)S(1)} async-done(((f32[8,1,128]{2,1,0:T(1,128)}), f32[8,1,128]{2,1,0:T(1,128)S(1)}, u32[]{:S(2)}, u32[]{:S(2)}) %all-to-all-start.1) | async-done | bytes 4128 | tf_op jit(solution)/shard_map/all_to_all | solution.py:197
  87.9 0.0 copy-done.2
  87.9 2.1 %shard_map.40 = f32[2,32,4096]{2,1,0:T(8,128)} custom-call(s32[1]{0:T(128)} %bitcast.rank, s32[16]{0:T(128)S(1)} %copy-done.2, f32[8,1,128]{2,1,0:T(1,128)S(1)} %all-to-all-done.1.squares, f32[32,32,128]{2,1,0:T(8,128)S(1)} %collective-permute-done.3.low_2, f32[32,32,128]{2,1,0:T(8,128)S(1)} %collective-permute-done.2.lower.low_1, ...), custom_call_target="tpu_custom_call" | custom-call | tf_op jit(solution)/shard_map/pallas_call | solution.py:200
  (2 shorter events, 0.1 us)
Async XLA Ops:
  2.1 24.3 %copy-start = (f32[2,32,4096]{2,1,0:T(8,128)S(1)}, f32[2,32,4096]{2,1,0:T(8,128)}, u32[]{:S(2)}) copy-start(f32[2,32,4096]{2,1,0:T(8,128)} %string.1) | copy-start | bytes 3145732
  2.1 24.3 %copy-start.1 = (f32[32,4096]{1,0:T(8,128)S(1)}, f32[32,4096]{1,0:T(8,128)}, u32[]{:S(2)}) copy-start(f32[32,4096]{1,0:T(8,128)} %tilt.1) | copy-start | bytes 1572868
  2.1 23.4 %collective-permute-start = (f32[3,8,4096]{2,1,0:T(8,128)S(1)}, f32[3,8,4096]{2,1,0:T(8,128)S(1)}, u32[]{:S(2)}, u32[]{:S(2)}) collective-permute-start(f32[3,8,4096]{2,1,0:T(8,128)S(1)} %pad_maximum_fusion), channel_id=1, source_target_pairs={{0,1},{1,2},{2,3},{3,4},{4,5},{5,6},{6,7},{7,8},{8,9},{9,10},{10,1... | collective-permute-start | bytes 1179656 | tf_op jit(solution)/shard_map/ppermute | solution.py:175
  6.3 20.1 %collective-permute-start.1 = (f32[3,8,4096]{2,1,0:T(8,128)S(1)}, f32[3,8,4096]{2,1,0:T(8,128)S(1)}, u32[]{:S(2)}, u32[]{:S(2)}) collective-permute-start(f32[3,8,4096]{2,1,0:T(8,128)S(1)} %pad_maximum_fusion.1), channel_id=1, source_target_pairs={{0,63},{1,0},{2,1},{3,2},{4,3},{5,4},{6,5},{7,6},{8,7},{9,8},{10,9... | collective-permute-start | bytes 1179656 | tf_op jit(solution)/shard_map/ppermute | solution.py:176
  45.7 10.7 %collective-permute-start.2 = (f32[32,32,128]{2,1,0:T(8,128)S(1)}, f32[32,32,128]{2,1,0:T(8,128)S(1)}, u32[]{:S(2)}, u32[]{:S(2)}) collective-permute-start(f32[32,32,128]{2,1,0:T(8,128)S(1)} %get-tuple-element.8.second.own_1), channel_id=1, source_target_pairs={{0,64},{64,128},{128,192},{192,256},{256,320},{320,384},{384,448},... | collective-permute-start | bytes 1572872 | tf_op jit(solution)/shard_map/ppermute | solution.py:189
  50.2 33.1 %collective-permute-start.4 = (f32[32,32,128]{2,1,0:T(8,128)S(1)}, f32[32,32,128]{2,1,0:T(8,128)S(1)}, u32[]{:S(2)}, u32[]{:S(2)}) collective-permute-start(f32[32,32,128]{2,1,0:T(8,128)S(1)} %get-tuple-element.7.first.own_0), channel_id=1, source_target_pairs={{64,0},{128,64},{192,128},{256,192},{320,256},{384,320},{448,384},... | collective-permute-start | bytes 1572872 | tf_op jit(solution)/shard_map/ppermute | solution.py:190
  52.2 31.2 %collective-permute-start.3 = (f32[32,32,128]{2,1,0:T(8,128)S(1)}, f32[32,32,128]{2,1,0:T(8,128)S(1)}, u32[]{:S(2)}, u32[]{:S(2)}) collective-permute-start(f32[32,32,128]{2,1,0:T(8,128)S(1)} %get-tuple-element.7.first.own_0), channel_id=1, source_target_pairs={{0,64},{64,128},{128,192},{192,256},{256,320},{320,384},{384,448},... | collective-permute-start | bytes 1572872 | tf_op jit(solution)/shard_map/ppermute | solution.py:191
  76.3 11.6 %all-to-all-start.1 = ((f32[8,1,128]{2,1,0:T(1,128)}), f32[8,1,128]{2,1,0:T(1,128)S(1)}, u32[]{:S(2)}, u32[]{:S(2)}) async-start(f32[8,1,128]{2,1,0:T(1,128)} %shard_map.39), calls=%async_computation.1 | async-start | bytes 8192 | tf_op jit(solution)/shard_map/all_to_all | solution.py:197
  83.4 4.5 %copy-start.2 = (s32[16]{0:T(128)S(1)}, s32[16]{0:T(128)}, u32[]{:S(2)}) copy-start(s32[16]{0:T(128)} %sources.1) | copy-start | bytes 196

commit v2 on v0

v2 whole, which is shorter than its diff:
```python
import functools

import jax
import jax.numpy as jnp
from jax import lax
from jax.experimental import pallas as pl
from jax.experimental.pallas import tpu as pltpu
from jax.sharding import PartitionSpec as P

SUBSTEPS = 8
DT = 0.1
EPS = 1e-06
LANES = 128
ROWS = 8
VMEM_LIMIT = 48 * 1024 * 1024
HALO_LIMIT = 54136 * 1024


def ring(axis, distance):
    count = lax.axis_size(axis)
    return [(i, (i + distance) % count) for i in range(count)]


def line(axis, distance):
    devices = range(lax.axis_size(axis))
    return [(i, i + distance) for i in devices if i + distance in devices]


def substep(source, target, force, row, out_row, force_row, columns):
    lane = lax.broadcasted_iota(jnp.int32, (ROWS, LANES), 1)
    is_first = lane == 0
    is_last = lane == LANES - 1
    middle = [source[c % columns, pl.ds(row, ROWS), :] for c in range(-1, columns + 1)]
    right_moved = [pltpu.roll(m, 1, 1) for m in middle[:-1]]
    left_moved = [pltpu.roll(m, LANES - 1, 1) for m in middle[1:]]
    for c in range(columns):
        u = middle[c + 1]
        left = jnp.where(is_first, right_moved[c], right_moved[c + 1])
        right = jnp.where(is_last, left_moved[c + 1], left_moved[c])
        above = source[c, pl.ds(row - 1, ROWS), :]
        below = source[c, pl.ds(row + 1, ROWS), :]
        near = (above + below) + (left + right)
        target[c, pl.ds(out_row, ROWS), :] = u * (0.7 - DT * (u * u)) + (
            DT * near + force[c, pl.ds(force_row, ROWS), :]
        )


def halo_kernel(string, tilt, up, down, sems):
    depth = string.shape[1]
    copies = [
        pltpu.make_async_copy(string.at[:, pl.ds(depth - ROWS, ROWS)], up.at[pl.ds(0, 2)], sems.at[0]),
        pltpu.make_async_copy(tilt.at[pl.ds(depth - ROWS, ROWS)], up.at[2], sems.at[1]),
        pltpu.make_async_copy(string.at[:, pl.ds(0, ROWS)], down.at[pl.ds(0, 2)], sems.at[2]),
        pltpu.make_async_copy(tilt.at[pl.ds(0, ROWS)], down.at[2], sems.at[3]),
    ]
    for copy in copies:
        copy.start()
    for copy in copies:
        copy.wait()


def plan_weights(images, rank, sources, plan):
    shape = plan.shape[2:]
    lane = lax.broadcasted_iota(jnp.int32, shape, 1)
    index = 2 * lax.broadcasted_iota(jnp.int32, shape, 0) + lane
    used = (lane < 2) & (index < images - 1)
    first = 2 * rank[0]
    for t in range(2):
        target = first + t
        source = sources[target]
        place = source - (first - 2)
        plan[t, 0] = jnp.where(used & (index < source), 1.0, 0.0)
        plan[t, 1] = jnp.where(used & (index == source), 1.0, 0.0)
        plan[t, 2] = jnp.full(shape, target.astype(jnp.float32) / (images - 1))
        for m in range(5):
            plan[t, 3 + m] = jnp.full(shape, jnp.where(place == m, 1.0, 0.0))
            plan[t, 8 + m] = jnp.full(shape, jnp.where(place + 1 == m, 1.0, 0.0))


def inner_kernel(images, rank, sources, string, tilt, plan, full, mid_first, history, edge_force, even, odd, force):
    plan_weights(images, rank, sources, plan)
    depth = string.shape[1]
    columns = string.shape[2] // LANES
    for c in range(columns):
        place = pl.ds(c * LANES, LANES)
        for image in range(2):
            even[image, c] = string[image, :, place]
        scaled = DT * tilt[:, place]
        force[c] = scaled
        edge_force[c, pl.ds(0, ROWS), :] = scaled[:ROWS]
        edge_force[c, pl.ds(ROWS, ROWS), :] = scaled[depth - ROWS :]
    buffers = (even, odd)
    for step in range(1, SUBSTEPS + 1):
        source, target = buffers[(step - 1) % 2], buffers[step % 2]
        last = depth - step - ROWS
        for image in range(2):
            for c in range(columns):
                history[0, image, c, pl.ds(2 * step - 2, 2), :] = source[image, c, pl.ds(step - 1, 2), :]
                history[1, image, c, pl.ds(2 * step - 2, 2), :] = source[
                    image, c, pl.ds(depth - 1 - step, 2), :
                ]
            for row in sorted(set(list(range(step, last, ROWS)) + [last])):
                if step < SUBSTEPS:
                    substep(source.at[image], target.at[image], force, row, row, row, columns)
                else:
                    substep(source.at[image], full.at[image], force, row, row, row, columns)
    mid_first[...] = full[0, :, pl.ds(ROWS, depth - 2 * ROWS), :]


def edge_kernel(low, high, history, edge_force, inner, full, edge_first, top_even, top_odd, bottom_even, bottom_odd, force):
    columns, depth = full.shape[1:3]
    for c in range(columns):
        place = pl.ds(c * LANES, LANES)
        for image in range(2):
            top_even[image, c, pl.ds(0, ROWS), :] = low[image, :, place]
            bottom_even[image, c, pl.ds(ROWS, ROWS), :] = high[image, :, place]
        force[0, c, pl.ds(0, ROWS), :] = DT * low[2, :, place]
        force[0, c, pl.ds(ROWS, ROWS), :] = edge_force[c, pl.ds(0, ROWS), :]
        force[1, c, pl.ds(0, ROWS), :] = edge_force[c, pl.ds(ROWS, ROWS), :]
        force[1, c, pl.ds(ROWS, ROWS), :] = DT * high[2, :, place]
    tops, bottoms = (top_even, top_odd), (bottom_even, bottom_odd)
    for step in range(1, SUBSTEPS + 1):
        now, later = (step - 1) % 2, step % 2
        for image in range(2):
            top, bottom = tops[now].at[image], bottoms[now].at[image]
            for c in range(columns):
                top[c, pl.ds(ROWS, 2), :] = history[0, image, c, pl.ds(2 * step - 2, 2), :]
                bottom[c, pl.ds(ROWS - 2, 2), :] = history[1, image, c, pl.ds(2 * step - 2, 2), :]
            top_out, bottom_out = tops[later].at[image], bottoms[later].at[image]
            bottom_row = ROWS
            if step == SUBSTEPS:
                top_out = bottom_out = full.at[image]
                bottom_row = depth - ROWS
            substep(top, top_out, force.at[0], 1, 0, step, columns)
            substep(bottom, bottom_out, force.at[1], ROWS - 1, bottom_row, ROWS - step, columns)
    edge_first[:, pl.ds(0, ROWS), :] = full[0, :, pl.ds(0, ROWS), :]
    edge_first[:, pl.ds(ROWS, ROWS), :] = full[0, :, pl.ds(depth - ROWS, ROWS), :]


def differences(upper, lower, columns, sums):
    def one(c, total):
        difference = upper(c) - lower(c)
        return total + difference * difference

    return lax.fori_loop(0, columns, one, sums, unroll=8)


def local_kernel(full, mid_high, sums):
    columns, depth = full.shape[1:3]
    zero = jnp.zeros((depth, LANES), jnp.float32)
    sums[0] = differences(lambda c: full[1, c], lambda c: full[0, c], columns, zero)
    middle = pl.ds(ROWS, depth - 2 * ROWS)
    sums[1] = jnp.zeros((depth, LANES), jnp.float32)
    sums[1, middle, :] = differences(lambda c: mid_high[c], lambda c: full[1, c, middle], columns, zero[: depth - 2 * ROWS])


def square_kernel(sums, full, edge_high, out):
    columns, depth = full.shape[1:3]
    beyond = jnp.sum(sums[1].reshape(-1, ROWS, LANES), axis=0)
    for row, out_row in ((0, 0), (ROWS, depth - ROWS)):
        beyond = differences(
            lambda c: edge_high[c, pl.ds(row, ROWS)], lambda c: full[1, c, pl.ds(out_row, ROWS)], columns, beyond
        )
    after = jnp.sum(sums[0], axis=(0, 1), keepdims=True)
    beyond = jnp.sum(beyond, axis=(0, 1), keepdims=True)
    lane = lax.broadcasted_iota(jnp.int32, (1, LANES), 1)
    row = jnp.where(lane == 0, after, jnp.where(lane == 1, beyond, 0.0))
    out[...] = jnp.broadcast_to(row[None], out.shape)


def total_kernel(parts, full_low, out):
    out[...] = jnp.broadcast_to(jnp.sum(parts[...], axis=0, keepdims=True), out.shape)


def mix_kernel(cells, images, squares, plan, full, full_low, mid_high, edge_high, out, mixed, sems):
    columns, depth = full.shape[1:3]
    rows = squares.shape[0]
    seg = jnp.sqrt(squares[...].reshape(rows, LANES) / cells + EPS)
    lane = lax.broadcasted_iota(jnp.int32, (rows, LANES), 1)
    index = 2 * lax.broadcasted_iota(jnp.int32, (rows, LANES), 0) + lane
    seg = jnp.where((lane < 2) & (index < images - 1), seg, 0.0)

    def whole(values):
        return jnp.sum(values, axis=(0, 1), keepdims=True)

    total = whole(seg)
    shares = []
    for t in range(2):
        ratio = plan[t, 2]
        weight = (ratio * total - whole(plan[t, 0] * seg)) / whole(plan[t, 1] * seg)
        shares.append([(1.0 - weight) * plan[t, 3 + m] + weight * plan[t, 8 + m] for m in range(5)])
    group = columns // 4
    copies = []
    for g in range(4):
        for c in range(g * group, (g + 1) * group):
            place = pl.ds(c * LANES, LANES)
            for high, row, out_row in (
                (edge_high, 0, 0),
                (mid_high, 0, ROWS),
                (mid_high, ROWS, 2 * ROWS),
                (edge_high, ROWS, depth - ROWS),
            ):
                at = pl.ds(out_row, ROWS)
                fields = [full_low[0, c, at], full_low[1, c, at], full[0, c, at], full[1, c, at]]
                fields.append(high[c, pl.ds(row, ROWS)])
                for t in range(2):
                    result = shares[t][0] * fields[0]
                    for m in range(1, 5):
                        result = result + shares[t][m] * fields[m]
                    mixed[t, at, place] = result
        span = pl.ds(g * group * LANES, group * LANES)
        copy = pltpu.make_async_copy(mixed.at[:, :, span], out.at[:, :, span], sems.at[g])
        copy.start()
        copies.append(copy)
    for copy in copies:
        copy.wait()


VMEM = pl.BlockSpec(memory_space=pltpu.VMEM)
SMEM = pl.BlockSpec(memory_space=pltpu.SMEM)
HBM = pl.BlockSpec(memory_space=pltpu.HBM)
ANY = pl.BlockSpec(memory_space=pl.ANY)


def call(name, kernel, shapes, ins, scratch=(), outs=VMEM, cost=0, limit=VMEM_LIMIT, aliases=None):
    return pl.pallas_call(
        kernel,
        out_shape=shapes,
        in_specs=ins,
        out_specs=jax.tree.map(lambda _: outs, shapes),
        scratch_shapes=list(scratch),
        name=name,
        input_output_aliases=aliases or {},
        cost_estimate=pl.CostEstimate(flops=cost, bytes_accessed=1 << 20, transcendentals=0),
        compiler_params=pltpu.CompilerParams(vmem_limit_bytes=limit),
    )


def body(string, tilt, source_pair):
    count, depth, width = string.shape
    columns = width // LANES
    slabs = lax.axis_size("slab")
    ranks = lax.axis_size("image")
    images = count * ranks
    half = 2 * ROWS

    def array(*shape):
        return jax.ShapeDtypeStruct(shape, jnp.float32)

    def room(*shape):
        return pltpu.VMEM(shape, jnp.float32)

    halo = array(3, ROWS, width)
    up, down = call(
        "halo", halo_kernel, (halo, halo), [HBM] * 2, [pltpu.SemaphoreType.DMA((4,))], limit=HALO_LIMIT
    )(string, tilt)
    low = lax.ppermute(up, "slab", ring("slab", 1))
    high = lax.ppermute(down, "slab", ring("slab", -1))
    whole = array(2, columns, depth, LANES)
    single = array(columns, half, LANES)
    rank = lax.axis_index("image").reshape(1)
    plan, full, mid_first, history, edge_force = call(
        "inner",
        functools.partial(inner_kernel, images),
        (array(2, 13, ranks, LANES), whole, single, array(2, 2, columns, half, LANES), single),
        [SMEM] * 2 + [VMEM] * 2,
        [room(2, columns, depth, LANES), room(2, columns, depth, LANES), room(columns, depth, LANES)],
        cost=1 << 32,
    )(rank, source_pair, string, tilt)
    mid_high = lax.ppermute(mid_first, "image", line("image", -1))
    full, edge_first = call(
        "edge",
        edge_kernel,
        (whole, single),
        [VMEM] * 5,
        [room(2, columns, half, LANES)] * 4 + [room(2, columns, half, LANES)],
        cost=1 << 31,
        aliases={4: 0},
    )(low, high, history, edge_force, full)
    edge_high = lax.ppermute(edge_first, "image", line("image", -1))
    full_low = lax.ppermute(full, "image", line("image", 1))
    sums = call("local", local_kernel, array(2, depth, LANES), [VMEM] * 2, cost=1 << 28)(full, mid_high)
    parts = call("square", square_kernel, array(slabs, 1, LANES), [VMEM] * 3, cost=1 << 33)(sums, full, edge_high)
    parts = lax.all_to_all(parts, "slab", 0, 0)
    squares = call("total", total_kernel, array(ranks, 1, LANES), [VMEM, ANY], cost=1 << 33)(parts, full_low)
    squares = lax.all_to_all(squares, "image", 0, 0)
    cells = depth * slabs * width
    return call(
        "mix",
        functools.partial(mix_kernel, cells, images),
        array(*string.shape),
        [VMEM] * 6,
        [room(*string.shape), pltpu.SemaphoreType.DMA((4,))],
        outs=ANY,
    )(squares, plan, full, full_low, mid_high, edge_high)


def solution(mesh):
    placed = (P("image", "slab", None), P("slab", None), P())
    return jax.shard_map(
        body, mesh=mesh, in_specs=placed, out_specs=P("image", "slab", None), check_vma=False
    )
```

time: 341 us -> 66.5 us (0.20)
  blocking collectives: 148 us -> 27.3 us
  other arithmetic: 52.7 us -> 0 us
  starting transfers between devices: 68.8 us -> 24.8 us
  waiting for transfers between devices: 45.6 us -> 1.97 us
  local copies, waits for them, and re-layouts: 16.1 us -> 0.64 us
  Pallas kernels: 0 us -> 11.4 us
  matrix products: 7.23 us -> 0 us
    psum x1 -> x0, blocking collectives: 111 us -> none  [body(): summed = lax.psum(partial_sq, 'slab')]
    add x9 -> x0, other arithmetic: 50.6 us -> none  [the longest x8 50.6 us: flow(): middle + DT * (lap + middle - middle * middle * middle + tilt_part[None])]
    ppermute x18 -> x5, starting transfers between devices: 68.8 us -> 24.8 us  [the longest x1 12.3 us: body(): high = lax.ppermute(down, 'slab', ring('slab', -1))]
    ppermute x18 -> x5, waiting for transfers between devices: 45.6 us -> 1.97 us  [the longest x1 1.96 us: body(): edge_high = lax.ppermute(edge_first, 'image', line('image', -1))]
    unnamed x1 -> x0, blocking collectives: 37.6 us -> none
    all_to_all x0 -> x2, blocking collectives: none -> 27.3 us  [the longest x1 18.2 us: body(): parts = lax.all_to_all(parts, 'slab', 0, 0)]
    pallas_call x0 -> x7, Pallas kernels: none -> 11.4 us  [the longest x1 5.87 us: body(): call('inner', functools.partial(inner_kernel, images), (array(2, 13, rank...]
    slice x25 -> x0, local copies, waits for them, and re-layouts: 11 us -> none  [the longest x16 10.4 us: flow(): jnp.roll(middle, -1, 2)]
  transfers between devices with their start and end apart: 18 -> 5, of which waited for: 9 -> 1; matrix products, arithmetic and copies ran while one was open for 2% -> 0% of each run, Pallas kernels for 0% -> 13%
where the time goes in v2:
time: 66.5 us; the launch traced here: 66.2 us
  blocking collectives  27.3 us (41%)
  starting transfers between devices  24.8 us (37%)
  Pallas kernels  11.4 us (17%)
  waiting for transfers between devices  1.97 us (3%)
    all_to_all x1, blocking collectives, body(): parts = lax.all_to_all(parts, 'slab', 0, 0)  18.2 us
    ppermute x1, starting transfers between devices, body(): high = lax.ppermute(down, 'slab', ring('slab', -1))  12.3 us
    all_to_all x1, blocking collectives, body(): squares = lax.all_to_all(squares, 'image', 0, 0)  9.08 us
    pallas_call x1, Pallas kernels, body(): call('inner', functools.partial(inner_kernel, images), (array(2, 13, rank...  5.87 us
    ppermute x1, starting transfers between devices, body(): low = lax.ppermute(up, 'slab', ring('slab', 1))  4.03 us
    ppermute x1, starting transfers between devices, body(): full_low = lax.ppermute(full, 'image', line('image', 1))  3.64 us
    ppermute x1, starting transfers between devices, body(): mid_high = lax.ppermute(mid_first, 'image', line('image', -1))  2.87 us
    pallas_call x1, Pallas kernels, body(): call('edge', edge_kernel, (whole, single), [VMEM] * 5, [room(2, columns,...  2.57 us
  transfers between devices with their start and end apart: 5, of which 1 were waited for; matrix products, arithmetic and copies ran while one was open for 0% of the time, Pallas kernels for 13%

profile of v2, /device:TPU:1, one launch (start us, length us, event | category | flops | bytes accessed | tf_op | source)
XLA Modules:
  0.0 66.2 jit_solution(7193916016309599866)
XLA Ops:
  0.0 0.0 copy-start.1
  0.0 0.0 copy-start
  0.0 1.3 %halo.1 = (f32[3,8,4096]{2,1,0:T(8,128)S(1)}, f32[3,8,4096]{2,1,0:T(8,128)S(1)}) custom-call(f32[2,32,4096]{2,1,0:T(8,128)} %string.3, f32[32,4096]{1,0:T(8,128)} %tilt.3), custom_call_target="tpu_custom_call" | custom-call | bytes 1048576 | tf_op jit(solution)/shard_map/halo/pallas_call | solution.py:254
  1.3 4.0 %collective-permute-start = (f32[3,8,4096]{2,1,0:T(8,128)S(1)}, f32[3,8,4096]{2,1,0:T(8,128)S(1)}, u32[]{:S(2)}, u32[]{:S(2)}) collective-permute-start(f32[3,8,4096]{2,1,0:T(8,128)S(1)} %get-tuple-element.14), channel_id=1, source_target_pairs={{0,1},{1,2},{2,3},{3,4},{4,5},{5,6},{6,7},{7,8},{8,9},{9,10},{10,1... | collective-permute-start | bytes 1179656 | tf_op jit(solution)/shard_map/ppermute | solution.py:257
  5.3 12.3 %collective-permute-start.1 = (f32[3,8,4096]{2,1,0:T(8,128)S(1)}, f32[3,8,4096]{2,1,0:T(8,128)S(1)}, u32[]{:S(2)}, u32[]{:S(2)}) collective-permute-start(f32[3,8,4096]{2,1,0:T(8,128)S(1)} %get-tuple-element.15), channel_id=1, source_target_pairs={{0,63},{1,0},{2,1},{3,2},{4,3},{5,4},{6,5},{7,6},{8,7},{9,8},{10,9... | collective-permute-start | bytes 1179656 | tf_op jit(solution)/shard_map/ppermute | solution.py:258
  17.6 0.0 copy-start.2
  17.6 0.0 copy-done.1
  17.7 0.0 copy-done
  17.7 0.6 copy-done.2
  18.3 5.9 %inner.1 = (f32[2,13,8,128]{3,2,1,0:T(8,128)S(1)}, f32[2,32,32,128]{3,2,1,0:T(8,128)S(1)}, f32[32,16,128]{2,1,0:T(8,128)S(1)}, f32[2,2,32,16,128]{4,3,2,1,0:T(8,128)S(1)}, f32[32,16,128]{2,1,0:T(8,128)S(1)}) custom-call(s32[1]{0:T(128)} %bitcast.rank, s32[16]{0:T(128)S(1)} %copy-done.2, f32[2,32,4096]{2,1,0:T(8,128)S(1)} %copy-done, f32[32,4096]{1,0:T(8,128)S(1)} %copy-done.1), custom_call_target="tpu_custom_call" | custom-call | flops 4294967296 | bytes 1048576 | tf_op jit(solution)/shard_map/inner/pallas_call | solution.py:262
  24.2 2.9 %collective-permute-start.2 = (f32[32,16,128]{2,1,0:T(8,128)S(1)}, f32[32,16,128]{2,1,0:T(8,128)S(1)}, u32[]{:S(2)}, u32[]{:S(2)}) collective-permute-start(f32[32,16,128]{2,1,0:T(8,128)S(1)} %get-tuple-element.20), channel_id=1, source_target_pairs={{64,0},{128,64},{192,128},{256,192},{320,256},{384,320},{448,384},... | collective-permute-start | bytes 786440 | tf_op jit(solution)/shard_map/ppermute | solution.py:270
  27.0 0.0 collective-permute-done.low
  27.1 0.0 collective-permute-done.1.high
  27.1 2.6 %edge.1 = (f32[2,32,32,128]{3,2,1,0:T(8,128)S(1)}, f32[32,16,128]{2,1,0:T(8,128)S(1)}) custom-call(f32[3,8,4096]{2,1,0:T(8,128)S(1)} %collective-permute-done.low, f32[3,8,4096]{2,1,0:T(8,128)S(1)} %collective-permute-done.1.high, f32[2,2,32,16,128]{4,3,2,1,0:T(8,128)S(1)} %get-tuple-element.16.history, ...), custom_call_target="tpu_custom_call", output_to_operand_aliasing={{0}: (4, {})} | custom-call | flops 2147483648 | bytes 1048576 | tf_op jit(solution)/shard_map/edge/pallas_call | solution.py:271
  29.6 1.9 %collective-permute-start.3 = (f32[32,16,128]{2,1,0:T(8,128)S(1)}, f32[32,16,128]{2,1,0:T(8,128)S(1)}, u32[]{:S(2)}, u32[]{:S(2)}) collective-permute-start(f32[32,16,128]{2,1,0:T(8,128)S(1)} %get-tuple-element.21), channel_id=1, source_target_pairs={{64,0},{128,64},{192,128},{256,192},{320,256},{384,320},{448,384},... | collective-permute-start | bytes 786440 | tf_op jit(solution)/shard_map/ppermute | solution.py:280
  31.6 3.6 %collective-permute-start.4 = (f32[2,32,32,128]{3,2,1,0:T(8,128)S(1)}, f32[2,32,32,128]{3,2,1,0:T(8,128)S(1)}, u32[]{:S(2)}, u32[]{:S(2)}) collective-permute-start(f32[2,32,32,128]{3,2,1,0:T(8,128)S(1)} %get-tuple-element.19.full), channel_id=1, source_target_pairs={{0,64},{64,128},{128,192},{192,256},{256,320},{320,384},{384,448},... | collective-permute-start | bytes 3145736 | tf_op jit(solution)/shard_map/ppermute | solution.py:281
  35.2 0.0 collective-permute-done.2.mid_high
  35.2 0.1 local.1.sums
  35.4 2.0 %collective-permute-done.3.edge_high = f32[32,16,128]{2,1,0:T(8,128)S(1)} collective-permute-done((f32[32,16,128]{2,1,0:T(8,128)S(1)}, f32[32,16,128]{2,1,0:T(8,128)S(1)}, u32[]{:S(2)}, u32[]{:S(2)}) %collective-permute-start.3) | collective-permute-done | bytes 262176 | tf_op jit(solution)/shard_map/ppermute | solution.py:280
  37.3 0.2 square.1
  37.6 18.2 %all_to_all.10.parts = f32[64,1,128]{2,1,0:T(1,128)S(1)} all-to-all(f32[64,1,128]{2,1,0:T(1,128)S(1)} %square.1), channel_id=1, replica_groups=mesh['image'=8,'slab'=64] {'slab'}, dimensions={0} | all-to-all | bytes 65536 | tf_op jit(solution)/shard_map/all_to_all | solution.py:284
  55.8 0.0 collective-permute-done.4.full_low
  55.8 0.1 total.1
  55.9 9.1 %all_to_all.11.squares = f32[8,1,128]{2,1,0:T(1,128)S(1)} all-to-all(f32[8,1,128]{2,1,0:T(1,128)S(1)} %total.1), channel_id=1, replica_groups=mesh['image'=8,'slab'=64] {'image'}, dimensions={0} | all-to-all | bytes 8192 | tf_op jit(solution)/shard_map/all_to_all | solution.py:286
  65.0 1.2 %mix.1 = f32[2,32,4096]{2,1,0:T(8,128)} custom-call(f32[8,1,128]{2,1,0:T(1,128)S(1)} %all_to_all.11.squares, f32[2,13,8,128]{3,2,1,0:T(8,128)S(1)} %get-tuple-element.22.plan, f32[2,32,32,128]{3,2,1,0:T(8,128)S(1)} %get-tuple-element.19.full, f32[2,32,32,128]{3,2,1,0:T(8,128)S(1)} %collective-permute-done.4.full_low, ...), custom_call_target="tpu_custom_call" | custom-call | bytes 1048576 | tf_op jit(solution)/shard_map/mix/pallas_call | solution.py:288
Async XLA Ops:
  0.0 17.6 %copy-start.1 = (f32[32,4096]{1,0:T(8,128)S(1)}, f32[32,4096]{1,0:T(8,128)}, u32[]{:S(2)}) copy-start(f32[32,4096]{1,0:T(8,128)} %tilt.3) | copy-start | bytes 1572868
  0.0 17.7 %copy-start = (f32[2,32,4096]{2,1,0:T(8,128)S(1)}, f32[2,32,4096]{2,1,0:T(8,128)}, u32[]{:S(2)}) copy-start(f32[2,32,4096]{2,1,0:T(8,128)} %string.3) | copy-start | bytes 3145732
  1.3 25.8 %collective-permute-start = (f32[3,8,4096]{2,1,0:T(8,128)S(1)}, f32[3,8,4096]{2,1,0:T(8,128)S(1)}, u32[]{:S(2)}, u32[]{:S(2)}) collective-permute-start(f32[3,8,4096]{2,1,0:T(8,128)S(1)} %get-tuple-element.14), channel_id=1, source_target_pairs={{0,1},{1,2},{2,3},{3,4},{4,5},{5,6},{6,7},{7,8},{8,9},{9,10},{10,1... | collective-permute-start | bytes 1179656 | tf_op jit(solution)/shard_map/ppermute | solution.py:257
  5.3 21.7 %collective-permute-start.1 = (f32[3,8,4096]{2,1,0:T(8,128)S(1)}, f32[3,8,4096]{2,1,0:T(8,128)S(1)}, u32[]{:S(2)}, u32[]{:S(2)}) collective-permute-start(f32[3,8,4096]{2,1,0:T(8,128)S(1)} %get-tuple-element.15), channel_id=1, source_target_pairs={{0,63},{1,0},{2,1},{3,2},{4,3},{5,4},{6,5},{7,6},{8,7},{9,8},{10,9... | collective-permute-start | bytes 1179656 | tf_op jit(solution)/shard_map/ppermute | solution.py:258
  17.6 0.7 copy-start.2
  24.2 11.1 %collective-permute-start.2 = (f32[32,16,128]{2,1,0:T(8,128)S(1)}, f32[32,16,128]{2,1,0:T(8,128)S(1)}, u32[]{:S(2)}, u32[]{:S(2)}) collective-permute-start(f32[32,16,128]{2,1,0:T(8,128)S(1)} %get-tuple-element.20), channel_id=1, source_target_pairs={{64,0},{128,64},{192,128},{256,192},{320,256},{384,320},{448,384},... | collective-permute-start | bytes 786440 | tf_op jit(solution)/shard_map/ppermute | solution.py:270
  29.6 7.7 %collective-permute-start.3 = (f32[32,16,128]{2,1,0:T(8,128)S(1)}, f32[32,16,128]{2,1,0:T(8,128)S(1)}, u32[]{:S(2)}, u32[]{:S(2)}) collective-permute-start(f32[32,16,128]{2,1,0:T(8,128)S(1)} %get-tuple-element.21), channel_id=1, source_target_pairs={{64,0},{128,64},{192,128},{256,192},{320,256},{384,320},{448,384},... | collective-permute-start | bytes 786440 | tf_op jit(solution)/shard_map/ppermute | solution.py:280
  31.6 24.2 %collective-permute-start.4 = (f32[2,32,32,128]{3,2,1,0:T(8,128)S(1)}, f32[2,32,32,128]{3,2,1,0:T(8,128)S(1)}, u32[]{:S(2)}, u32[]{:S(2)}) collective-permute-start(f32[2,32,32,128]{3,2,1,0:T(8,128)S(1)} %get-tuple-element.19.full), channel_id=1, source_target_pairs={{0,64},{64,128},{128,192},{192,256},{256,320},{320,384},{384,448},... | collective-permute-start | bytes 3145736 | tf_op jit(solution)/shard_map/ppermute | solution.py:281

commit v3 on v2

v3 whole, which is shorter than its diff:
```python
import functools

import jax
import jax.numpy as jnp
from jax import lax
from jax.experimental import pallas as pl
from jax.experimental.pallas import tpu as pltpu
from jax.sharding import PartitionSpec as P

SUBSTEPS = 8
DT = 0.1
EPS = 1e-06
LANES = 128
ROWS = 8
VMEM_LIMIT = 48 * 1024 * 1024
HALO_LIMIT = 54136 * 1024


def partners(axis, first):
    count = lax.axis_size(axis)
    step = 1 if first else -1
    evens = range(0, count, 2)
    return [(i, (i + step) % count) for i in evens] + [((i + step) % count, i) for i in evens]


def line(axis, distance):
    devices = range(lax.axis_size(axis))
    return [(i, i + distance) for i in devices if i + distance in devices]


def is_odd(axis):
    return lax.rem(lax.axis_index(axis), 2)


def odd_mask():
    return jnp.full((ROWS, LANES), is_odd("slab"), jnp.int32) == 1


def substep(source, target, force, row, out_row, force_row, columns, keep=None, keep_row=0):
    lane = lax.broadcasted_iota(jnp.int32, (ROWS, LANES), 1)
    is_first = lane == 0
    is_last = lane == LANES - 1
    middle = [source[c % columns, pl.ds(row, ROWS), :] for c in range(-1, columns + 1)]
    right_moved = [pltpu.roll(m, 1, 1) for m in middle[:-1]]
    left_moved = [pltpu.roll(m, LANES - 1, 1) for m in middle[1:]]
    for c in range(columns):
        u = middle[c + 1]
        left = jnp.where(is_first, right_moved[c], right_moved[c + 1])
        right = jnp.where(is_last, left_moved[c + 1], left_moved[c])
        above = source[c, pl.ds(row - 1, ROWS), :]
        below = source[c, pl.ds(row + 1, ROWS), :]
        near = (above + below) + (left + right)
        result = u * (0.7 - DT * (u * u)) + (DT * near + force[c, pl.ds(force_row, ROWS), :])
        target[c, pl.ds(out_row, ROWS), :] = result
        if keep is not None:
            keep[c, pl.ds(keep_row, ROWS), :] = result


def halo_kernel(string, tilt, first, second, sems):
    odd = is_odd("slab")
    last = string.shape[1] - ROWS
    copies = []
    for n, (out, row) in enumerate(((first, (1 - odd) * last), (second, odd * last))):
        rows = pl.ds(pl.multiple_of(row, ROWS), ROWS)
        copies.append(pltpu.make_async_copy(string.at[:, rows], out.at[pl.ds(0, 2)], sems.at[2 * n]))
        copies.append(pltpu.make_async_copy(tilt.at[rows], out.at[2], sems.at[2 * n + 1]))
    for copy in copies:
        copy.start()
    for copy in copies:
        copy.wait()


def inner_kernel(string, tilt, full, history, edge_force, even, odd, force):
    depth = string.shape[1]
    columns = string.shape[2] // LANES
    bottom = 2 * SUBSTEPS - 2
    for c in range(columns):
        place = pl.ds(c * LANES, LANES)
        for image in range(2):
            rows = string[image, :, place]
            even[image, c] = rows
            history[0, image, c, pl.ds(0, ROWS), :] = rows[:ROWS]
            history[1, image, c, pl.ds(bottom, ROWS), :] = rows[depth - ROWS :]
        scaled = DT * tilt[:, place]
        force[c] = scaled
        edge_force[0, c] = scaled[:ROWS]
        edge_force[1, c] = scaled[depth - ROWS :]
    buffers = (even, odd)
    for step in range(1, SUBSTEPS + 1):
        source, target = buffers[(step - 1) % 2], buffers[step % 2]
        if step == SUBSTEPS:
            target = full
        last = depth - step - ROWS
        for image in range(2):
            for row in sorted(set(list(range(step, last, ROWS)) + [last])):
                keep, keep_row = None, 0
                if step < SUBSTEPS and row == step:
                    keep, keep_row = history.at[0, image], 2 * step
                if step < SUBSTEPS and row == last:
                    keep, keep_row = history.at[1, image], bottom - 2 * step
                substep(source.at[image], target.at[image], force, row, row, row, columns, keep, keep_row)


def edge_rows(side, halo, history, edge_force, full, even, odd, force):
    columns, depth = full.shape[1:3]
    mine, theirs = ((ROWS, 0), (0, ROWS))[side]
    for c in range(columns):
        place = pl.ds(c * LANES, LANES)
        for image in range(2):
            even[image, c, pl.ds(theirs, ROWS), :] = halo[image, :, place]
        force[c, pl.ds(theirs, ROWS), :] = DT * halo[2, :, place]
        force[c, pl.ds(mine, ROWS), :] = edge_force[side, c]
    buffers = (even, odd)
    for step in range(1, SUBSTEPS + 1):
        source, target = buffers[(step - 1) % 2], buffers[step % 2]
        out_row = theirs
        if step == SUBSTEPS:
            target, out_row = full, side * (depth - ROWS)
        kept = 2 * (step - 1) if side == 0 else 2 * SUBSTEPS + 4 - 2 * (step - 1)
        row, force_row = (1, step) if side == 0 else (ROWS - 1, ROWS - step)
        for image in range(2):
            for c in range(columns):
                source[image, c, pl.ds(ROWS - 2 * side, 2), :] = history[side, image, c, pl.ds(kept, 2), :]
            substep(source.at[image], target.at[image], force, row, out_row, force_row, columns)


def edge_kernel(is_second, halo, history, edge_force, inner, full, sent, even, odd, force):
    depth = full.shape[2]
    inside = depth - 2 * ROWS
    for side in range(2):

        @pl.when(is_odd("slab") == (side if is_second else 1 - side))
        def one():
            edge_rows(side, halo, history, edge_force, full, even, odd, force)
            rows = full[0, :, pl.ds(side * (depth - ROWS), ROWS), :]
            sent[:, pl.ds(0 if is_second else inside, ROWS), :] = rows

    if not is_second:
        sent[:, pl.ds(0, inside), :] = full[0, :, pl.ds(ROWS, inside), :]


def differences(upper, lower, columns, sums):
    def one(c, total):
        difference = upper(c) - lower(c)
        return total + difference * difference

    return lax.fori_loop(0, columns, one, sums, unroll=8)


def local_kernel(images, sources, full, early_high, sums, plan):
    columns, depth = full.shape[1:3]
    odd = odd_mask()
    upper, lower = pl.ds(0, ROWS), pl.ds(depth - ROWS, ROWS)
    inside = depth - 2 * ROWS
    zero = jnp.zeros((depth, LANES), jnp.float32)
    sums[0] = differences(lambda c: full[1, c], lambda c: full[0, c], columns, zero)
    sums[1] = zero
    sums[1, pl.ds(0, inside), :] = differences(
        lambda c: early_high[c, pl.ds(0, inside)], lambda c: full[1, c, pl.ds(ROWS, inside)], columns, zero[:inside]
    )
    sums[1, pl.ds(inside, ROWS), :] = differences(
        lambda c: early_high[c, pl.ds(inside, ROWS)],
        lambda c: jnp.where(odd, full[1, c, upper], full[1, c, lower]),
        columns,
        zero[:ROWS],
    )
    shape = plan.shape[2:]
    lane = lax.broadcasted_iota(jnp.int32, shape, 1)
    index = 2 * lax.broadcasted_iota(jnp.int32, shape, 0) + lane
    used = (lane < 2) & (index < images - 1)
    first = 2 * lax.axis_index("image")
    for t in range(2):
        target = first + t
        source = sources[target]
        place = source - (first - 2)
        plan[t, 0] = jnp.where(used & (index < source), 1.0, 0.0)
        plan[t, 1] = jnp.where(used & (index == source), 1.0, 0.0)
        plan[t, 2] = jnp.full(shape, target.astype(jnp.float32) / (images - 1))
        for m in range(5):
            plan[t, 3 + m] = jnp.full(shape, jnp.where(place == m, 1.0, 0.0))
            plan[t, 8 + m] = jnp.full(shape, jnp.where(place + 1 == m, 1.0, 0.0))


def square_kernel(sums, full, late_high, out):
    columns, depth = full.shape[1:3]
    odd = odd_mask()
    upper, lower = pl.ds(0, ROWS), pl.ds(depth - ROWS, ROWS)
    beyond = differences(
        lambda c: late_high[c],
        lambda c: jnp.where(odd, full[1, c, lower], full[1, c, upper]),
        columns,
        jnp.sum(sums[1].reshape(-1, ROWS, LANES), axis=0),
    )
    after = jnp.sum(sums[0], axis=(0, 1), keepdims=True)
    beyond = jnp.sum(beyond, axis=(0, 1), keepdims=True)
    lane = lax.broadcasted_iota(jnp.int32, (1, LANES), 1)
    row = jnp.where(lane == 0, after, jnp.where(lane == 1, beyond, 0.0))
    out[...] = jnp.broadcast_to(row[None], out.shape)


def total_kernel(parts, full_low, out):
    out[...] = jnp.broadcast_to(jnp.sum(parts[...], axis=0, keepdims=True), out.shape)


def mix_kernel(cells, images, squares, plan, full, full_low, early_high, late_high, out, mixed, sems):
    columns, depth = full.shape[1:3]
    rows = squares.shape[0]
    seg = jnp.sqrt(squares[...].reshape(rows, LANES) / cells + EPS)
    lane = lax.broadcasted_iota(jnp.int32, (rows, LANES), 1)
    index = 2 * lax.broadcasted_iota(jnp.int32, (rows, LANES), 0) + lane
    seg = jnp.where((lane < 2) & (index < images - 1), seg, 0.0)

    def whole(values):
        return jnp.sum(values, axis=(0, 1), keepdims=True)

    total = whole(seg)
    shares = []
    for t in range(2):
        weight = (plan[t, 2] * total - whole(plan[t, 0] * seg)) / whole(plan[t, 1] * seg)
        shares.append([(1.0 - weight) * plan[t, 3 + m] + weight * plan[t, 8 + m] for m in range(5)])
    odd = odd_mask()
    group = columns // 4
    copies = []
    for g in range(4):
        for c in range(g * group, (g + 1) * group):
            place = pl.ds(c * LANES, LANES)
            early, late = early_high[c, pl.ds(depth - 2 * ROWS, ROWS)], late_high[c]
            for high, row in (
                (jnp.where(odd, early, late), 0),
                (early_high[c, pl.ds(0, ROWS)], ROWS),
                (early_high[c, pl.ds(ROWS, ROWS)], 2 * ROWS),
                (jnp.where(odd, late, early), depth - ROWS),
            ):
                at = pl.ds(row, ROWS)
                fields = [full_low[0, c, at], full_low[1, c, at], full[0, c, at], full[1, c, at], high]
                for t in range(2):
                    result = shares[t][0] * fields[0]
                    for m in range(1, 5):
                        result = result + shares[t][m] * fields[m]
                    mixed[t, at, place] = result
        span = pl.ds(g * group * LANES, group * LANES)
        copy = pltpu.make_async_copy(mixed.at[:, :, span], out.at[:, :, span], sems.at[g])
        copy.start()
        copies.append(copy)
    for copy in copies:
        copy.wait()


VMEM = pl.BlockSpec(memory_space=pltpu.VMEM)
SMEM = pl.BlockSpec(memory_space=pltpu.SMEM)
HBM = pl.BlockSpec(memory_space=pltpu.HBM)
ANY = pl.BlockSpec(memory_space=pl.ANY)


def call(name, kernel, shapes, ins, scratch=(), outs=VMEM, cost=0, limit=VMEM_LIMIT, aliases=None):
    return pl.pallas_call(
        kernel,
        out_shape=shapes,
        in_specs=ins,
        out_specs=jax.tree.map(lambda _: outs, shapes),
        scratch_shapes=list(scratch),
        name=name,
        input_output_aliases=aliases or {},
        cost_estimate=pl.CostEstimate(flops=cost, bytes_accessed=1 << 20, transcendentals=0),
        compiler_params=pltpu.CompilerParams(vmem_limit_bytes=limit),
    )


def body(string, tilt, source_pair):
    count, depth, width = string.shape
    columns = width // LANES
    slabs = lax.axis_size("slab")
    ranks = lax.axis_size("image")
    images = count * ranks
    half = 2 * ROWS

    def array(*shape):
        return jax.ShapeDtypeStruct(shape, jnp.float32)

    def room(*shape):
        return pltpu.VMEM(shape, jnp.float32)

    halo = array(3, ROWS, width)
    first, second = call(
        "halo", halo_kernel, (halo, halo), [HBM] * 2, [pltpu.SemaphoreType.DMA((4,))], limit=HALO_LIMIT
    )(string, tilt)
    first = lax.ppermute(first, "slab", partners("slab", True))
    second = lax.ppermute(second, "slab", partners("slab", False))
    whole = array(2, columns, depth, LANES)
    full, history, edge_force = call(
        "inner",
        inner_kernel,
        (whole, array(2, 2, columns, 3 * ROWS, LANES), array(2, columns, ROWS, LANES)),
        [VMEM] * 2,
        [room(2, columns, depth, LANES), room(2, columns, depth, LANES), room(columns, depth, LANES)],
        cost=1 << 31,
    )(string, tilt)
    scratch = [room(2, columns, half, LANES), room(2, columns, half, LANES), room(columns, half, LANES)]

    def edge(name, is_second, received, full):
        rows = ROWS if is_second else depth - ROWS
        return call(
            name,
            functools.partial(edge_kernel, is_second),
            (whole, array(columns, rows, LANES)),
            [VMEM] * 4,
            scratch,
            cost=1 << 30 if is_second else 1 << 32,
            aliases={3: 0},
        )(received, history, edge_force, full)

    full, early = edge("edge_first", False, first, full)
    early_high = lax.ppermute(early, "image", line("image", -1))
    full, late = edge("edge_second", True, second, full)
    late_high = lax.ppermute(late, "image", line("image", -1))
    full_low = lax.ppermute(full, "image", line("image", 1))
    sums, plan = call(
        "local",
        functools.partial(local_kernel, images),
        (array(2, depth, LANES), array(2, 13, ranks, LANES)),
        [SMEM] + [VMEM] * 2,
        cost=1 << 28,
    )(source_pair, full, early_high)
    parts = call("square", square_kernel, array(slabs, 1, LANES), [VMEM] * 3, cost=3 << 32)(sums, full, late_high)
    parts = lax.all_to_all(parts, "slab", 0, 0)
    squares = call("total", total_kernel, array(ranks, 1, LANES), [VMEM, ANY], cost=1 << 33)(parts, full_low)
    squares = lax.all_to_all(squares, "image", 0, 0)
    cells = depth * slabs * width
    return call(
        "mix",
        functools.partial(mix_kernel, cells, images),
        array(*string.shape),
        [VMEM] * 6,
        [room(*string.shape), pltpu.SemaphoreType.DMA((4,))],
        outs=ANY,
    )(squares, plan, full, full_low, early_high, late_high)


def solution(mesh):
    placed = (P("image", "slab", None), P("slab", None), P())
    return jax.shard_map(
        body, mesh=mesh, in_specs=placed, out_specs=P("image", "slab", None), check_vma=False
    )
```

time: 66.5 us -> 65.1 us (0.979)
  waiting for transfers between devices: 1.97 us -> 0.12 us
  starting transfers between devices: 24.8 us -> 26.1 us
    ppermute x4, waiting for transfers between devices: 1.97 us -> 0.11 us  [the longest x1 0.1 us: body(): late_high = lax.ppermute(late, 'image', line('image', -1))]
    ppermute x4, starting transfers between devices: 21.1 us -> 22.5 us  [the longest x1 13.3 us: body(): second = lax.ppermute(second, 'slab', partners('slab', False))]
    all_to_all x1, blocking collectives: 18.2 us -> 17.4 us  [body(): parts = lax.all_to_all(parts, 'slab', 0, 0)]
    pallas_call x4 -> x5, Pallas kernels: 8.81 us -> 9.13 us  [the longest x1 5.27 us: body(): call('inner', inner_kernel, (whole, array(2, 2, columns, 3 * ROWS, LANES)...]
  transfers between devices with their start and end apart: 5 -> 5, of which waited for: 1 -> 1; matrix products, arithmetic and copies ran while one was open for 0% -> 0% of each run, Pallas kernels for 13% -> 14%
where the time goes in v3:
time: 65.1 us; the launch traced here: 64.8 us
  blocking collectives  26.8 us (41%)
  starting transfers between devices  26.1 us (40%)
  Pallas kernels  11.7 us (18%)
    all_to_all x1, blocking collectives, body(): parts = lax.all_to_all(parts, 'slab', 0, 0)  17.4 us
    ppermute x1, starting transfers between devices, body(): second = lax.ppermute(second, 'slab', partners('slab', False))  13.3 us
    all_to_all x1, blocking collectives, body(): squares = lax.all_to_all(squares, 'image', 0, 0)  9.32 us
    pallas_call x1, Pallas kernels, body(): call('inner', inner_kernel, (whole, array(2, 2, columns, 3 * ROWS, LANES)...  5.27 us
    ppermute x1, starting transfers between devices, body(): first = lax.ppermute(first, 'slab', partners('slab', True))  4.03 us
    ppermute x1, starting transfers between devices, body(): full_low = lax.ppermute(full, 'image', line('image', 1))  3.58 us
    ppermute x1, starting transfers between devices, body(): early_high = lax.ppermute(early, 'image', line('image', -1))  3.15 us
    pallas_call x2, Pallas kernels, edge(): call(name, functools.partial(edge_kernel, is_second), (whole, array(colum...  2.91 us
  transfers between devices with their start and end apart: 5, of which 1 were waited for; matrix products, arithmetic and copies ran while one was open for 0% of the time, Pallas kernels for 14%

profile of v3, /device:TPU:1, one launch (start us, length us, event | category | flops | bytes accessed | tf_op | source)
XLA Modules:
  0.0 64.8 jit_solution(9347854461535701364)
XLA Ops:
  0.0 0.0 copy-start.1
  0.0 0.0 copy-start
  0.0 1.3 %halo.1 = (f32[3,8,4096]{2,1,0:T(8,128)S(1)}, f32[3,8,4096]{2,1,0:T(8,128)S(1)}) custom-call(f32[2,32,4096]{2,1,0:T(8,128)} %string.3, f32[32,4096]{1,0:T(8,128)} %tilt.3), custom_call_target="tpu_custom_call" | custom-call | bytes 1048576 | tf_op jit(solution)/shard_map/halo/pallas_call | solution.py:284
  1.3 4.0 %collective-permute-start.1 = (f32[3,8,4096]{2,1,0:T(8,128)S(1)}, f32[3,8,4096]{2,1,0:T(8,128)S(1)}, u32[]{:S(2)}, u32[]{:S(2)}) collective-permute-start(f32[3,8,4096]{2,1,0:T(8,128)S(1)} %get-tuple-element.19), channel_id=1, source_target_pairs={{0,1},{2,3},{4,5},{6,7},{8,9},{10,11},{12,13},{14,15},{16,17},{18,... | collective-permute-start | bytes 1179656 | tf_op jit(solution)/shard_map/ppermute | solution.py:287
  5.3 13.3 %collective-permute-start = (f32[3,8,4096]{2,1,0:T(8,128)S(1)}, f32[3,8,4096]{2,1,0:T(8,128)S(1)}, u32[]{:S(2)}, u32[]{:S(2)}) collective-permute-start(f32[3,8,4096]{2,1,0:T(8,128)S(1)} %get-tuple-element.16), channel_id=1, source_target_pairs={{0,63},{2,1},{4,3},{6,5},{8,7},{10,9},{12,11},{14,13},{16,15},{18,... | collective-permute-start | bytes 1179656 | tf_op jit(solution)/shard_map/ppermute | solution.py:288
  18.7 0.0 copy-done.1
  18.7 0.0 copy-done
  18.7 5.3 %inner.1 = (f32[2,32,32,128]{3,2,1,0:T(8,128)S(1)}, f32[2,2,32,24,128]{4,3,2,1,0:T(8,128)S(1)}, f32[2,32,8,128]{3,2,1,0:T(8,128)S(1)}) custom-call(f32[2,32,4096]{2,1,0:T(8,128)S(1)} %copy-done, f32[32,4096]{1,0:T(8,128)S(1)} %copy-done.1), custom_call_target="tpu_custom_call" | custom-call | flops 2147483648 | bytes 1048576 | tf_op jit(solution)/shard_map/inner/pallas_call | solution.py:290
  24.0 0.0 collective-permute-done.1.halo
  24.0 1.5 %edge_first.1 = (f32[2,32,32,128]{3,2,1,0:T(8,128)S(1)}, f32[32,24,128]{2,1,0:T(8,128)S(1)}) custom-call(f32[3,8,4096]{2,1,0:T(8,128)S(1)} %collective-permute-done.1.halo, f32[2,2,32,24,128]{4,3,2,1,0:T(8,128)S(1)} %get-tuple-element.17.history, f32[2,32,8,128]{3,2,1,0:T(8,128)S(1)} %get-tuple-element.18.edge_force, ...), custom_call_target="tpu_custom_call", output_to_operand_aliasing={{0}: (3, {})} | custom-call | flops 4294967296 | bytes 1048576 | tf_op jit(solution)/shard_map/edge_first/pallas_call | solution.py:302
  25.5 3.2 %collective-permute-start.2 = (f32[32,24,128]{2,1,0:T(8,128)S(1)}, f32[32,24,128]{2,1,0:T(8,128)S(1)}, u32[]{:S(2)}, u32[]{:S(2)}) collective-permute-start(f32[32,24,128]{2,1,0:T(8,128)S(1)} %get-tuple-element.23), channel_id=1, source_target_pairs={{64,0},{128,64},{192,128},{256,192},{320,256},{384,320},{448,384},... | collective-permute-start | bytes 1179656 | tf_op jit(solution)/shard_map/ppermute | solution.py:313
  28.6 0.0 collective-permute-done.halo
  28.6 0.0 copy-start.2
  28.7 1.4 %edge_second.1 = (f32[2,32,32,128]{3,2,1,0:T(8,128)S(1)}, f32[32,8,128]{2,1,0:T(8,128)S(1)}) custom-call(f32[3,8,4096]{2,1,0:T(8,128)S(1)} %collective-permute-done.halo, f32[2,2,32,24,128]{4,3,2,1,0:T(8,128)S(1)} %get-tuple-element.17.history, f32[2,32,8,128]{3,2,1,0:T(8,128)S(1)} %get-tuple-element.18.edge_force, ...), custom_call_target="tpu_custom_call", output_to_operand_aliasing={{0}: (3, {})} | custom-call | flops 1073741824 | bytes 1048576 | tf_op jit(solution)/shard_map/edge_second/pallas_call | solution.py:302
  30.1 2.0 %collective-permute-start.3 = (f32[32,8,128]{2,1,0:T(8,128)S(1)}, f32[32,8,128]{2,1,0:T(8,128)S(1)}, u32[]{:S(2)}, u32[]{:S(2)}) collective-permute-start(f32[32,8,128]{2,1,0:T(8,128)S(1)} %get-tuple-element.25), channel_id=1, source_target_pairs={{64,0},{128,64},{192,128},{256,192},{320,256},{384,320},{448,384},... | collective-permute-start | bytes 393224 | tf_op jit(solution)/shard_map/ppermute | solution.py:315
  32.1 3.6 %collective-permute-start.4 = (f32[2,32,32,128]{3,2,1,0:T(8,128)S(1)}, f32[2,32,32,128]{3,2,1,0:T(8,128)S(1)}, u32[]{:S(2)}, u32[]{:S(2)}) collective-permute-start(f32[2,32,32,128]{3,2,1,0:T(8,128)S(1)} %get-tuple-element.22.full), channel_id=1, source_target_pairs={{0,64},{64,128},{128,192},{192,256},{256,320},{320,384},{384,448},... | collective-permute-start | bytes 3145736 | tf_op jit(solution)/shard_map/ppermute | solution.py:316
  35.7 0.0 collective-permute-done.2.early_high
  35.7 0.0 copy-done.2
  35.7 0.8 %local.1 = (f32[2,32,128]{2,1,0:T(8,128)S(1)}, f32[2,13,8,128]{3,2,1,0:T(8,128)S(1)}) custom-call(s32[16]{0:T(128)S(1)} %copy-done.2, f32[2,32,32,128]{3,2,1,0:T(8,128)S(1)} %get-tuple-element.22.full, f32[32,24,128]{2,1,0:T(8,128)S(1)} %collective-permute-done.2.early_high), custom_call_target="tpu_custom_call" | custom-call | flops 268435456 | bytes 1048576 | tf_op jit(solution)/shard_map/local/pallas_call | solution.py:317
  36.5 0.1 collective-permute-done.3.late_high
  36.6 0.2 square.1
  36.8 17.4 %all_to_all.10.parts = f32[64,1,128]{2,1,0:T(1,128)S(1)} all-to-all(f32[64,1,128]{2,1,0:T(1,128)S(1)} %square.1), channel_id=1, replica_groups=mesh['image'=8,'slab'=64] {'slab'}, dimensions={0} | all-to-all | bytes 65536 | tf_op jit(solution)/shard_map/all_to_all | solution.py:325
  54.2 0.0 collective-permute-done.4.full_low
  54.2 0.1 total.1
  54.3 9.3 %all_to_all.11.squares = f32[8,1,128]{2,1,0:T(1,128)S(1)} all-to-all(f32[8,1,128]{2,1,0:T(1,128)S(1)} %total.1), channel_id=1, replica_groups=mesh['image'=8,'slab'=64] {'image'}, dimensions={0} | all-to-all | bytes 8192 | tf_op jit(solution)/shard_map/all_to_all | solution.py:327
  63.6 1.2 %mix.1 = f32[2,32,4096]{2,1,0:T(8,128)} custom-call(f32[8,1,128]{2,1,0:T(1,128)S(1)} %all_to_all.11.squares, f32[2,13,8,128]{3,2,1,0:T(8,128)S(1)} %get-tuple-element.26.plan, f32[2,32,32,128]{3,2,1,0:T(8,128)S(1)} %get-tuple-element.22.full, f32[2,32,32,128]{3,2,1,0:T(8,128)S(1)} %collective-permute-done.4.full_low, ...), custom_call_target="tpu_custom_call" | custom-call | bytes 1048576 | tf_op jit(solution)/shard_map/mix/pallas_call | solution.py:329
Async XLA Ops:
  0.0 18.7 %copy-start.1 = (f32[32,4096]{1,0:T(8,128)S(1)}, f32[32,4096]{1,0:T(8,128)}, u32[]{:S(2)}) copy-start(f32[32,4096]{1,0:T(8,128)} %tilt.3) | copy-start | bytes 1572868
  0.0 18.7 %copy-start = (f32[2,32,4096]{2,1,0:T(8,128)S(1)}, f32[2,32,4096]{2,1,0:T(8,128)}, u32[]{:S(2)}) copy-start(f32[2,32,4096]{2,1,0:T(8,128)} %string.3) | copy-start | bytes 3145732
  1.3 22.7 %collective-permute-start.1 = (f32[3,8,4096]{2,1,0:T(8,128)S(1)}, f32[3,8,4096]{2,1,0:T(8,128)S(1)}, u32[]{:S(2)}, u32[]{:S(2)}) collective-permute-start(f32[3,8,4096]{2,1,0:T(8,128)S(1)} %get-tuple-element.19), channel_id=1, source_target_pairs={{0,1},{2,3},{4,5},{6,7},{8,9},{10,11},{12,13},{14,15},{16,17},{18,... | collective-permute-start | bytes 1179656 | tf_op jit(solution)/shard_map/ppermute | solution.py:287
  5.3 23.3 %collective-permute-start = (f32[3,8,4096]{2,1,0:T(8,128)S(1)}, f32[3,8,4096]{2,1,0:T(8,128)S(1)}, u32[]{:S(2)}, u32[]{:S(2)}) collective-permute-start(f32[3,8,4096]{2,1,0:T(8,128)S(1)} %get-tuple-element.16), channel_id=1, source_target_pairs={{0,63},{2,1},{4,3},{6,5},{8,7},{10,9},{12,11},{14,13},{16,15},{18,... | collective-permute-start | bytes 1179656 | tf_op jit(solution)/shard_map/ppermute | solution.py:288
  25.5 10.2 %collective-permute-start.2 = (f32[32,24,128]{2,1,0:T(8,128)S(1)}, f32[32,24,128]{2,1,0:T(8,128)S(1)}, u32[]{:S(2)}, u32[]{:S(2)}) collective-permute-start(f32[32,24,128]{2,1,0:T(8,128)S(1)} %get-tuple-element.23), channel_id=1, source_target_pairs={{64,0},{128,64},{192,128},{256,192},{320,256},{384,320},{448,384},... | collective-permute-start | bytes 1179656 | tf_op jit(solution)/shard_map/ppermute | solution.py:313
  28.6 7.1 %copy-start.2 = (s32[16]{0:T(128)S(1)}, s32[16]{0:T(128)}, u32[]{:S(2)}) copy-start(s32[16]{0:T(128)} %sources.1) | copy-start | bytes 196
  30.1 6.5 %collective-permute-start.3 = (f32[32,8,128]{2,1,0:T(8,128)S(1)}, f32[32,8,128]{2,1,0:T(8,128)S(1)}, u32[]{:S(2)}, u32[]{:S(2)}) collective-permute-start(f32[32,8,128]{2,1,0:T(8,128)S(1)} %get-tuple-element.25), channel_id=1, source_target_pairs={{64,0},{128,64},{192,128},{256,192},{320,256},{384,320},{448,384},... | collective-permute-start | bytes 393224 | tf_op jit(solution)/shard_map/ppermute | solution.py:315
  32.1 22.1 %collective-permute-start.4 = (f32[2,32,32,128]{3,2,1,0:T(8,128)S(1)}, f32[2,32,32,128]{3,2,1,0:T(8,128)S(1)}, u32[]{:S(2)}, u32[]{:S(2)}) collective-permute-start(f32[2,32,32,128]{3,2,1,0:T(8,128)S(1)} %get-tuple-element.22.full), channel_id=1, source_target_pairs={{0,64},{64,128},{128,192},{192,256},{256,320},{320,384},{384,448},... | collective-permute-start | bytes 3145736 | tf_op jit(solution)/shard_map/ppermute | solution.py:316

commit v4 on v3

--- a/solution.py
+++ b/solution.py
@@ -30,10 +30,6 @@
 
 def is_odd(axis):
     return lax.rem(lax.axis_index(axis), 2)
-
-
-def odd_mask():
-    return jnp.full((ROWS, LANES), is_odd("slab"), jnp.int32) == 1
 
 
 def substep(source, target, force, row, out_row, force_row, columns, keep=None, keep_row=0):
@@ -70,7 +66,7 @@
         copy.wait()
 
 
-def inner_kernel(string, tilt, full, history, edge_force, even, odd, force):
+def inner_kernel(string, tilt, full, middle, history, edge_force, even, odd, force):
     depth = string.shape[1]
     columns = string.shape[2] // LANES
     bottom = 2 * SUBSTEPS - 2
@@ -99,6 +95,7 @@
                 if step < SUBSTEPS and row == last:
                     keep, keep_row = history.at[1, image], bottom - 2 * step
                 substep(source.at[image], target.at[image], force, row, row, row, columns, keep, keep_row)
+    middle[...] = full[0, :, pl.ds(ROWS, depth - 2 * ROWS), :]
 
 
 def edge_rows(side, halo, history, edge_force, full, even, odd, force):
@@ -124,19 +121,19 @@
             substep(source.at[image], target.at[image], force, row, out_row, force_row, columns)
 
 
-def edge_kernel(is_second, halo, history, edge_force, inner, full, sent, even, odd, force):
+def edge_kernel(is_second, halo, history, edge_force, inner, full, *rest):
+    even, odd, force = rest[-3:]
     depth = full.shape[2]
-    inside = depth - 2 * ROWS
     for side in range(2):
 
         @pl.when(is_odd("slab") == (side if is_second else 1 - side))
         def one():
             edge_rows(side, halo, history, edge_force, full, even, odd, force)
-            rows = full[0, :, pl.ds(side * (depth - ROWS), ROWS), :]
-            sent[:, pl.ds(0 if is_second else inside, ROWS), :] = rows
-
-    if not is_second:
-        sent[:, pl.ds(0, inside), :] = full[0, :, pl.ds(ROWS, inside), :]
+
+    if is_second:
+        edges = rest[0]
+        edges[:, pl.ds(0, ROWS), :] = full[0, :, pl.ds(0, ROWS), :]
+        edges[:, pl.ds(ROWS, ROWS), :] = full[0, :, pl.ds(depth - ROWS, ROWS), :]
 
 
 def differences(upper, lower, columns, sums):
@@ -147,22 +144,13 @@
     return lax.fori_loop(0, columns, one, sums, unroll=8)
 
 
-def local_kernel(images, sources, full, early_high, sums, plan):
+def local_kernel(images, sources, full, middle_high, sums, plan):
     columns, depth = full.shape[1:3]
-    odd = odd_mask()
-    upper, lower = pl.ds(0, ROWS), pl.ds(depth - ROWS, ROWS)
     inside = depth - 2 * ROWS
     zero = jnp.zeros((depth, LANES), jnp.float32)
-    sums[0] = differences(lambda c: full[1, c], lambda c: full[0, c], columns, zero)
-    sums[1] = zero
-    sums[1, pl.ds(0, inside), :] = differences(
-        lambda c: early_high[c, pl.ds(0, inside)], lambda c: full[1, c, pl.ds(ROWS, inside)], columns, zero[:inside]
-    )
-    sums[1, pl.ds(inside, ROWS), :] = differences(
-        lambda c: early_high[c, pl.ds(inside, ROWS)],
-        lambda c: jnp.where(odd, full[1, c, upper], full[1, c, lower]),
-        columns,
-        zero[:ROWS],
+    sums[pl.ds(0, depth), :] = differences(lambda c: full[1, c], lambda c: full[0, c], columns, zero)
+    sums[pl.ds(depth, inside), :] = differences(
+        lambda c: middle_high[c], lambda c: full[1, c, pl.ds(ROWS, inside)], columns, zero[:inside]
     )
     shape = plan.shape[2:]
     lane = lax.broadcasted_iota(jnp.int32, shape, 1)
@@ -181,17 +169,14 @@
             plan[t, 8 + m] = jnp.full(shape, jnp.where(place + 1 == m, 1.0, 0.0))
 
 
-def square_kernel(sums, full, late_high, out):
+def square_kernel(sums, full, edges_high, out):
     columns, depth = full.shape[1:3]
-    odd = odd_mask()
-    upper, lower = pl.ds(0, ROWS), pl.ds(depth - ROWS, ROWS)
-    beyond = differences(
-        lambda c: late_high[c],
-        lambda c: jnp.where(odd, full[1, c, lower], full[1, c, upper]),
-        columns,
-        jnp.sum(sums[1].reshape(-1, ROWS, LANES), axis=0),
-    )
-    after = jnp.sum(sums[0], axis=(0, 1), keepdims=True)
+    beyond = sums[pl.ds(depth, ROWS), :] + sums[pl.ds(depth + ROWS, ROWS), :]
+    for row, at in ((0, 0), (ROWS, depth - ROWS)):
+        beyond = differences(
+            lambda c: edges_high[c, pl.ds(row, ROWS)], lambda c: full[1, c, pl.ds(at, ROWS)], columns, beyond
+        )
+    after = jnp.sum(sums[pl.ds(0, depth), :], axis=(0, 1), keepdims=True)
     beyond = jnp.sum(beyond, axis=(0, 1), keepdims=True)
     lane = lax.broadcasted_iota(jnp.int32, (1, LANES), 1)
     row = jnp.where(lane == 0, after, jnp.where(lane == 1, beyond, 0.0))
@@ -202,7 +187,7 @@
     out[...] = jnp.broadcast_to(jnp.sum(parts[...], axis=0, keepdims=True), out.shape)
 
 
-def mix_kernel(cells, images, squares, plan, full, full_low, early_high, late_high, out, mixed, sems):
+def mix_kernel(cells, images, squares, plan, full, full_low, middle_high, edges_high, out, mixed, sems):
     columns, depth = full.shape[1:3]
     rows = squares.shape[0]
     seg = jnp.sqrt(squares[...].reshape(rows, LANES) / cells + EPS)
@@ -218,20 +203,19 @@
     for t in range(2):
         weight = (plan[t, 2] * total - whole(plan[t, 0] * seg)) / whole(plan[t, 1] * seg)
         shares.append([(1.0 - weight) * plan[t, 3 + m] + weight * plan[t, 8 + m] for m in range(5)])
-    odd = odd_mask()
     group = columns // 4
     copies = []
     for g in range(4):
         for c in range(g * group, (g + 1) * group):
             place = pl.ds(c * LANES, LANES)
-            early, late = early_high[c, pl.ds(depth - 2 * ROWS, ROWS)], late_high[c]
-            for high, row in (
-                (jnp.where(odd, early, late), 0),
-                (early_high[c, pl.ds(0, ROWS)], ROWS),
-                (early_high[c, pl.ds(ROWS, ROWS)], 2 * ROWS),
-                (jnp.where(odd, late, early), depth - ROWS),
+            for high, row, at in (
+                (edges_high, 0, 0),
+                (middle_high, 0, ROWS),
+                (middle_high, ROWS, 2 * ROWS),
+                (edges_high, ROWS, depth - ROWS),
             ):
-                at = pl.ds(row, ROWS)
+                high = high[c, pl.ds(row, ROWS)]
+                at = pl.ds(at, ROWS)
                 fields = [full_low[0, c, at], full_low[1, c, at], full[0, c, at], full[1, c, at], high]
                 for t in range(2):
                     result = shares[t][0] * fields[0]
@@ -287,41 +271,40 @@
     first = lax.ppermute(first, "slab", partners("slab", True))
     second = lax.ppermute(second, "slab", partners("slab", False))
     whole = array(2, columns, depth, LANES)
-    full, history, edge_force = call(
+    single = array(columns, half, LANES)
+    full, middle, history, edge_force = call(
         "inner",
         inner_kernel,
-        (whole, array(2, 2, columns, 3 * ROWS, LANES), array(2, columns, ROWS, LANES)),
+        (whole, single, array(2, 2, columns, 3 * ROWS, LANES), array(2, columns, ROWS, LANES)),
         [VMEM] * 2,
         [room(2, columns, depth, LANES), room(2, columns, depth, LANES), room(columns, depth, LANES)],
         cost=1 << 31,
     )(string, tilt)
-    scratch = [room(2, columns, half, LANES), room(2, columns, half, LANES), room(columns, half, LANES)]
+    middle_high = lax.ppermute(middle, "image", line("image", -1))
 
     def edge(name, is_second, received, full):
-        rows = ROWS if is_second else depth - ROWS
         return call(
             name,
             functools.partial(edge_kernel, is_second),
-            (whole, array(columns, rows, LANES)),
+            (whole, single) if is_second else (whole,),
             [VMEM] * 4,
-            scratch,
+            [room(2, columns, half, LANES), room(2, columns, half, LANES), room(columns, half, LANES)],
             cost=1 << 30 if is_second else 1 << 32,
             aliases={3: 0},
         )(received, history, edge_force, full)
 
-    full, early = edge("edge_first", False, first, full)
-    early_high = lax.ppermute(early, "image", line("image", -1))
-    full, late = edge("edge_second", True, second, full)
-    late_high = lax.ppermute(late, "image", line("image", -1))
+    (full,) = edge("edge_first", False, first, full)
+    full, edges = edge("edge_second", True, second, full)
+    edges_high = lax.ppermute(edges, "image", line("image", -1))
     full_low = lax.ppermute(full, "image", line("image", 1))
     sums, plan = call(
         "local",
         functools.partial(local_kernel, images),
-        (array(2, depth, LANES), array(2, 13, ranks, LANES)),
+        (array(depth + half, LANES), array(2, 13, ranks, LANES)),
         [SMEM] + [VMEM] * 2,
         cost=1 << 28,
-    )(source_pair, full, early_high)
-    parts = call("square", square_kernel, array(slabs, 1, LANES), [VMEM] * 3, cost=3 << 32)(sums, full, late_high)
+    )(source_pair, full, middle_high)
+    parts = call("square", square_kernel, array(slabs, 1, LANES), [VMEM] * 3, cost=3 << 32)(sums, full, edges_high)
     parts = lax.all_to_all(parts, "slab", 0, 0)
     squares = call("total", total_kernel, array(ranks, 1, LANES), [VMEM, ANY], cost=1 << 33)(parts, full_low)
     squares = lax.all_to_all(squares, "image", 0, 0)
@@ -333,7 +316,7 @@
         [VMEM] * 6,
         [room(*string.shape), pltpu.SemaphoreType.DMA((4,))],
         outs=ANY,
-    )(squares, plan, full, full_low, early_high, late_high)
+    )(squares, plan, full, full_low, middle_high, edges_high)
 
 
 def solution(mesh):

time: 65.1 us -> 65.7 us (level)
  waiting for transfers between devices: 0.12 us -> 1.4 us
  blocking collectives: 26.8 us -> 26 us
    ppermute x2, waiting for transfers between devices: 0.11 us -> 1.39 us  [the longest x1 1.39 us: body(): edges_high = lax.ppermute(edges, 'image', line('image', -1))]
where the time goes in v4:
time: 65.7 us; the launch traced here: 65.4 us
  starting transfers between devices  26.1 us (40%)
  blocking collectives  26 us (40%)
  Pallas kernels  11.7 us (18%)
  waiting for transfers between devices  1.4 us (2%)
    all_to_all x1, blocking collectives, body(): parts = lax.all_to_all(parts, 'slab', 0, 0)  17.2 us
    ppermute x1, starting transfers between devices, body(): second = lax.ppermute(second, 'slab', partners('slab', False))  13.3 us
    all_to_all x1, blocking collectives, body(): squares = lax.all_to_all(squares, 'image', 0, 0)  8.84 us
    pallas_call x1, Pallas kernels, body(): call('inner', inner_kernel, (whole, single, array(2, 2, columns, 3 * ROWS...  5.27 us
    ppermute x1, starting transfers between devices, body(): first = lax.ppermute(first, 'slab', partners('slab', True))  4.03 us
    ppermute x1, starting transfers between devices, body(): full_low = lax.ppermute(full, 'image', line('image', 1))  3.56 us
    ppermute x1, starting transfers between devices, body(): middle_high = lax.ppermute(middle, 'image', line('image', -1))  3.15 us
    pallas_call x2, Pallas kernels, edge(): call(name, functools.partial(edge_kernel, is_second), (whole, single) if...  2.92 us
  transfers between devices with their start and end apart: 5, of which 1 were waited for; matrix products, arithmetic and copies ran while one was open for 0% of the time, Pallas kernels for 14%

profile of v4, /device:TPU:1, one launch (start us, length us, event | category | flops | bytes accessed | tf_op | source)
XLA Modules:
  0.0 65.4 jit_solution(11882817765714284783)
XLA Ops:
  0.0 0.0 copy-start.1
  0.0 0.0 copy-start
  0.0 1.3 %halo.1 = (f32[3,8,4096]{2,1,0:T(8,128)S(1)}, f32[3,8,4096]{2,1,0:T(8,128)S(1)}) custom-call(f32[2,32,4096]{2,1,0:T(8,128)} %string.3, f32[32,4096]{1,0:T(8,128)} %tilt.3), custom_call_target="tpu_custom_call" | custom-call | bytes 1048576 | tf_op jit(solution)/shard_map/halo/pallas_call | solution.py:268
  1.3 4.0 %collective-permute-start.1 = (f32[3,8,4096]{2,1,0:T(8,128)S(1)}, f32[3,8,4096]{2,1,0:T(8,128)S(1)}, u32[]{:S(2)}, u32[]{:S(2)}) collective-permute-start(f32[3,8,4096]{2,1,0:T(8,128)S(1)} %get-tuple-element.18), channel_id=1, source_target_pairs={{0,1},{2,3},{4,5},{6,7},{8,9},{10,11},{12,13},{14,15},{16,17},{18,... | collective-permute-start | bytes 1179656 | tf_op jit(solution)/shard_map/ppermute | solution.py:271
  5.3 13.3 %collective-permute-start = (f32[3,8,4096]{2,1,0:T(8,128)S(1)}, f32[3,8,4096]{2,1,0:T(8,128)S(1)}, u32[]{:S(2)}, u32[]{:S(2)}) collective-permute-start(f32[3,8,4096]{2,1,0:T(8,128)S(1)} %get-tuple-element.15), channel_id=1, source_target_pairs={{0,63},{2,1},{4,3},{6,5},{8,7},{10,9},{12,11},{14,13},{16,15},{18,... | collective-permute-start | bytes 1179656 | tf_op jit(solution)/shard_map/ppermute | solution.py:272
  18.7 0.0 copy-done.1
  18.7 0.0 copy-done
  18.7 5.3 %inner.1 = (f32[2,32,32,128]{3,2,1,0:T(8,128)S(1)}, f32[32,16,128]{2,1,0:T(8,128)S(1)}, f32[2,2,32,24,128]{4,3,2,1,0:T(8,128)S(1)}, f32[2,32,8,128]{3,2,1,0:T(8,128)S(1)}) custom-call(f32[2,32,4096]{2,1,0:T(8,128)S(1)} %copy-done, f32[32,4096]{1,0:T(8,128)S(1)} %copy-done.1), custom_call_target="tpu_custom_call" | custom-call | flops 2147483648 | bytes 1048576 | tf_op jit(solution)/shard_map/inner/pallas_call | solution.py:275
  24.0 3.2 %collective-permute-start.2 = (f32[32,16,128]{2,1,0:T(8,128)S(1)}, f32[32,16,128]{2,1,0:T(8,128)S(1)}, u32[]{:S(2)}, u32[]{:S(2)}) collective-permute-start(f32[32,16,128]{2,1,0:T(8,128)S(1)} %get-tuple-element.21), channel_id=1, source_target_pairs={{64,0},{128,64},{192,128},{256,192},{320,256},{384,320},{448,384},... | collective-permute-start | bytes 786440 | tf_op jit(solution)/shard_map/ppermute | solution.py:283
  27.1 0.0 collective-permute-done.1.halo
  27.2 1.5 %edge_first.1.inner = f32[2,32,32,128]{3,2,1,0:T(8,128)S(1)} custom-call(f32[3,8,4096]{2,1,0:T(8,128)S(1)} %collective-permute-done.1.halo, f32[2,2,32,24,128]{4,3,2,1,0:T(8,128)S(1)} %get-tuple-element.16.history, f32[2,32,8,128]{3,2,1,0:T(8,128)S(1)} %get-tuple-element.17.edge_force, ...), custom_call_target="tpu_custom_call", output_to_operand_aliasing={{}: (3, {})} | custom-call | flops 4294967296 | bytes 1048576 | tf_op jit(solution)/shard_map/edge_first/pallas_call | solution.py:286
  28.6 0.0 copy-start.2
  28.6 0.0 collective-permute-done.halo
  28.6 1.5 %edge_second.1 = (f32[2,32,32,128]{3,2,1,0:T(8,128)S(1)}, f32[32,16,128]{2,1,0:T(8,128)S(1)}) custom-call(f32[3,8,4096]{2,1,0:T(8,128)S(1)} %collective-permute-done.halo, f32[2,2,32,24,128]{4,3,2,1,0:T(8,128)S(1)} %get-tuple-element.16.history, f32[2,32,8,128]{3,2,1,0:T(8,128)S(1)} %get-tuple-element.17.edge_force, ...), custom_call_target="tpu_custom_call", output_to_operand_aliasing={{0}: (3, {})} | custom-call | flops 1073741824 | bytes 1048576 | tf_op jit(solution)/shard_map/edge_second/pallas_call | solution.py:286
  30.1 2.0 %collective-permute-start.3 = (f32[32,16,128]{2,1,0:T(8,128)S(1)}, f32[32,16,128]{2,1,0:T(8,128)S(1)}, u32[]{:S(2)}, u32[]{:S(2)}) collective-permute-start(f32[32,16,128]{2,1,0:T(8,128)S(1)} %get-tuple-element.23), channel_id=1, source_target_pairs={{64,0},{128,64},{192,128},{256,192},{320,256},{384,320},{448,384},... | collective-permute-start | bytes 786440 | tf_op jit(solution)/shard_map/ppermute | solution.py:298
  32.1 3.6 %collective-permute-start.4 = (f32[2,32,32,128]{3,2,1,0:T(8,128)S(1)}, f32[2,32,32,128]{3,2,1,0:T(8,128)S(1)}, u32[]{:S(2)}, u32[]{:S(2)}) collective-permute-start(f32[2,32,32,128]{3,2,1,0:T(8,128)S(1)} %get-tuple-element.20.full), channel_id=1, source_target_pairs={{0,64},{64,128},{128,192},{192,256},{256,320},{320,384},{384,448},... | collective-permute-start | bytes 3145736 | tf_op jit(solution)/shard_map/ppermute | solution.py:299
  35.7 0.0 collective-permute-done.2.middle_high
  35.7 0.0 copy-done.2
  35.7 0.7 %local.1 = (f32[48,128]{1,0:T(8,128)S(1)}, f32[2,13,8,128]{3,2,1,0:T(8,128)S(1)}) custom-call(s32[16]{0:T(128)S(1)} %copy-done.2, f32[2,32,32,128]{3,2,1,0:T(8,128)S(1)} %get-tuple-element.20.full, f32[32,16,128]{2,1,0:T(8,128)S(1)} %collective-permute-done.2.middle_high), custom_call_target="tpu_custom_call" | custom-call | flops 268435456 | bytes 1048576 | tf_op jit(solution)/shard_map/local/pallas_call | solution.py:300
  36.4 1.4 %collective-permute-done.3.edges_high = f32[32,16,128]{2,1,0:T(8,128)S(1)} collective-permute-done((f32[32,16,128]{2,1,0:T(8,128)S(1)}, f32[32,16,128]{2,1,0:T(8,128)S(1)}, u32[]{:S(2)}, u32[]{:S(2)}) %collective-permute-start.3) | collective-permute-done | bytes 262176 | tf_op jit(solution)/shard_map/ppermute | solution.py:298
  37.8 0.2 square.1
  38.0 17.2 %all_to_all.10.parts = f32[64,1,128]{2,1,0:T(1,128)S(1)} all-to-all(f32[64,1,128]{2,1,0:T(1,128)S(1)} %square.1), channel_id=1, replica_groups=mesh['image'=8,'slab'=64] {'slab'}, dimensions={0} | all-to-all | bytes 65536 | tf_op jit(solution)/shard_map/all_to_all | solution.py:308
  55.2 0.0 collective-permute-done.4.full_low
  55.2 0.1 total.1
  55.3 8.8 %all_to_all.11.squares = f32[8,1,128]{2,1,0:T(1,128)S(1)} all-to-all(f32[8,1,128]{2,1,0:T(1,128)S(1)} %total.1), channel_id=1, replica_groups=mesh['image'=8,'slab'=64] {'image'}, dimensions={0} | all-to-all | bytes 8192 | tf_op jit(solution)/shard_map/all_to_all | solution.py:310
  64.1 1.2 %mix.1 = f32[2,32,4096]{2,1,0:T(8,128)} custom-call(f32[8,1,128]{2,1,0:T(1,128)S(1)} %all_to_all.11.squares, f32[2,13,8,128]{3,2,1,0:T(8,128)S(1)} %get-tuple-element.24.plan, f32[2,32,32,128]{3,2,1,0:T(8,128)S(1)} %get-tuple-element.20.full, f32[2,32,32,128]{3,2,1,0:T(8,128)S(1)} %collective-permute-done.4.full_low, ...), custom_call_target="tpu_custom_call" | custom-call | bytes 1048576 | tf_op jit(solution)/shard_map/mix/pallas_call | solution.py:312
Async XLA Ops:
  0.0 18.7 %copy-start.1 = (f32[32,4096]{1,0:T(8,128)S(1)}, f32[32,4096]{1,0:T(8,128)}, u32[]{:S(2)}) copy-start(f32[32,4096]{1,0:T(8,128)} %tilt.3) | copy-start | bytes 1572868
  0.0 18.7 %copy-start = (f32[2,32,4096]{2,1,0:T(8,128)S(1)}, f32[2,32,4096]{2,1,0:T(8,128)}, u32[]{:S(2)}) copy-start(f32[2,32,4096]{2,1,0:T(8,128)} %string.3) | copy-start | bytes 3145732
  1.3 25.9 %collective-permute-start.1 = (f32[3,8,4096]{2,1,0:T(8,128)S(1)}, f32[3,8,4096]{2,1,0:T(8,128)S(1)}, u32[]{:S(2)}, u32[]{:S(2)}) collective-permute-start(f32[3,8,4096]{2,1,0:T(8,128)S(1)} %get-tuple-element.18), channel_id=1, source_target_pairs={{0,1},{2,3},{4,5},{6,7},{8,9},{10,11},{12,13},{14,15},{16,17},{18,... | collective-permute-start | bytes 1179656 | tf_op jit(solution)/shard_map/ppermute | solution.py:271
  5.3 23.3 %collective-permute-start = (f32[3,8,4096]{2,1,0:T(8,128)S(1)}, f32[3,8,4096]{2,1,0:T(8,128)S(1)}, u32[]{:S(2)}, u32[]{:S(2)}) collective-permute-start(f32[3,8,4096]{2,1,0:T(8,128)S(1)} %get-tuple-element.15), channel_id=1, source_target_pairs={{0,63},{2,1},{4,3},{6,5},{8,7},{10,9},{12,11},{14,13},{16,15},{18,... | collective-permute-start | bytes 1179656 | tf_op jit(solution)/shard_map/ppermute | solution.py:272
  24.0 11.7 %collective-permute-start.2 = (f32[32,16,128]{2,1,0:T(8,128)S(1)}, f32[32,16,128]{2,1,0:T(8,128)S(1)}, u32[]{:S(2)}, u32[]{:S(2)}) collective-permute-start(f32[32,16,128]{2,1,0:T(8,128)S(1)} %get-tuple-element.21), channel_id=1, source_target_pairs={{64,0},{128,64},{192,128},{256,192},{320,256},{384,320},{448,384},... | collective-permute-start | bytes 786440 | tf_op jit(solution)/shard_map/ppermute | solution.py:283
  28.6 7.1 %copy-start.2 = (s32[16]{0:T(128)S(1)}, s32[16]{0:T(128)}, u32[]{:S(2)}) copy-start(s32[16]{0:T(128)} %sources.1) | copy-start | bytes 196
  30.1 7.7 %collective-permute-start.3 = (f32[32,16,128]{2,1,0:T(8,128)S(1)}, f32[32,16,128]{2,1,0:T(8,128)S(1)}, u32[]{:S(2)}, u32[]{:S(2)}) collective-permute-start(f32[32,16,128]{2,1,0:T(8,128)S(1)} %get-tuple-element.23), channel_id=1, source_target_pairs={{64,0},{128,64},{192,128},{256,192},{320,256},{384,320},{448,384},... | collective-permute-start | bytes 786440 | tf_op jit(solution)/shard_map/ppermute | solution.py:298
  32.1 23.1 %collective-permute-start.4 = (f32[2,32,32,128]{3,2,1,0:T(8,128)S(1)}, f32[2,32,32,128]{3,2,1,0:T(8,128)S(1)}, u32[]{:S(2)}, u32[]{:S(2)}) collective-permute-start(f32[2,32,32,128]{3,2,1,0:T(8,128)S(1)} %get-tuple-element.20.full), channel_id=1, source_target_pairs={{0,64},{64,128},{128,192},{192,256},{256,320},{320,384},{384,448},... | collective-permute-start | bytes 3145736 | tf_op jit(solution)/shard_map/ppermute | solution.py:299

commit v5 on v4

--- a/solution.py
+++ b/solution.py
@@ -18,7 +18,7 @@
 
 def partners(axis, first):
     count = lax.axis_size(axis)
-    step = 1 if first else -1
+    step = -1 if first else 1
     evens = range(0, count, 2)
     return [(i, (i + step) % count) for i in evens] + [((i + step) % count, i) for i in evens]
 
@@ -56,7 +56,7 @@
     odd = is_odd("slab")
     last = string.shape[1] - ROWS
     copies = []
-    for n, (out, row) in enumerate(((first, (1 - odd) * last), (second, odd * last))):
+    for n, (out, row) in enumerate(((first, odd * last), (second, (1 - odd) * last))):
         rows = pl.ds(pl.multiple_of(row, ROWS), ROWS)
         copies.append(pltpu.make_async_copy(string.at[:, rows], out.at[pl.ds(0, 2)], sems.at[2 * n]))
         copies.append(pltpu.make_async_copy(tilt.at[rows], out.at[2], sems.at[2 * n + 1]))
@@ -126,7 +126,7 @@
     depth = full.shape[2]
     for side in range(2):
 
-        @pl.when(is_odd("slab") == (side if is_second else 1 - side))
+        @pl.when(is_odd("slab") == (1 - side if is_second else side))
         def one():
             edge_rows(side, halo, history, edge_force, full, even, odd, force)
 

time: 65.7 us -> 64.4 us (0.980)
  blocking collectives: 26 us -> 24.9 us
    ppermute x1, starting transfers between devices: 13.3 us -> 1.92 us  [body(): second = lax.ppermute(second, 'slab', partners('slab', False))]
    ppermute x1, starting transfers between devices: 4.03 us -> 14.4 us  [body(): first = lax.ppermute(first, 'slab', partners('slab', True))]
    ppermute x1, starting transfers between devices: 2 us -> 3.72 us  [body(): edges_high = lax.ppermute(edges, 'image', line('image', -1))]
    all_to_all x1, blocking collectives: 17.2 us -> 16.1 us  [body(): parts = lax.all_to_all(parts, 'slab', 0, 0)]
where the time goes in v5:
time: 64.4 us; the launch traced here: 64.1 us
  starting transfers between devices  25.9 us (40%)
  blocking collectives  24.9 us (39%)
  Pallas kernels  11.7 us (18%)
  waiting for transfers between devices  1.4 us (2%)
    all_to_all x1, blocking collectives, body(): parts = lax.all_to_all(parts, 'slab', 0, 0)  16.1 us
    ppermute x1, starting transfers between devices, body(): first = lax.ppermute(first, 'slab', partners('slab', True))  14.4 us
    all_to_all x1, blocking collectives, body(): squares = lax.all_to_all(squares, 'image', 0, 0)  8.84 us
    pallas_call x1, Pallas kernels, body(): call('inner', inner_kernel, (whole, single, array(2, 2, columns, 3 * ROWS...  5.26 us
    ppermute x1, starting transfers between devices, body(): edges_high = lax.ppermute(edges, 'image', line('image', -1))  3.72 us
    ppermute x1, starting transfers between devices, body(): full_low = lax.ppermute(full, 'image', line('image', 1))  3.02 us
    pallas_call x2, Pallas kernels, edge(): call(name, functools.partial(edge_kernel, is_second), (whole, single) if...  2.92 us
    ppermute x1, starting transfers between devices, body(): middle_high = lax.ppermute(middle, 'image', line('image', -1))  2.88 us
  transfers between devices with their start and end apart: 5, of which 1 were waited for; matrix products, arithmetic and copies ran while one was open for 0% of the time, Pallas kernels for 14%

profile of v5, /device:TPU:1, one launch (start us, length us, event | category | flops | bytes accessed | tf_op | source)
XLA Modules:
  0.0 64.1 jit_solution(6252261662575592202)
XLA Ops:
  0.0 0.0 copy-start.1
  0.0 0.0 copy-start
  0.0 1.3 %halo.1 = (f32[3,8,4096]{2,1,0:T(8,128)S(1)}, f32[3,8,4096]{2,1,0:T(8,128)S(1)}) custom-call(f32[2,32,4096]{2,1,0:T(8,128)} %string.3, f32[32,4096]{1,0:T(8,128)} %tilt.3), custom_call_target="tpu_custom_call" | custom-call | bytes 1048576 | tf_op jit(solution)/shard_map/halo/pallas_call | solution.py:268
  1.3 14.4 %collective-permute-start.1 = (f32[3,8,4096]{2,1,0:T(8,128)S(1)}, f32[3,8,4096]{2,1,0:T(8,128)S(1)}, u32[]{:S(2)}, u32[]{:S(2)}) collective-permute-start(f32[3,8,4096]{2,1,0:T(8,128)S(1)} %get-tuple-element.18), channel_id=1, source_target_pairs={{0,63},{2,1},{4,3},{6,5},{8,7},{10,9},{12,11},{14,13},{16,15},{18,... | collective-permute-start | bytes 1179656 | tf_op jit(solution)/shard_map/ppermute | solution.py:271
  15.7 1.9 %collective-permute-start = (f32[3,8,4096]{2,1,0:T(8,128)S(1)}, f32[3,8,4096]{2,1,0:T(8,128)S(1)}, u32[]{:S(2)}, u32[]{:S(2)}) collective-permute-start(f32[3,8,4096]{2,1,0:T(8,128)S(1)} %get-tuple-element.15), channel_id=1, source_target_pairs={{0,1},{2,3},{4,5},{6,7},{8,9},{10,11},{12,13},{14,15},{16,17},{18,... | collective-permute-start | bytes 1179656 | tf_op jit(solution)/shard_map/ppermute | solution.py:272
  17.6 0.0 copy-done.1
  17.6 0.0 copy-done
  17.6 5.3 %inner.1 = (f32[2,32,32,128]{3,2,1,0:T(8,128)S(1)}, f32[32,16,128]{2,1,0:T(8,128)S(1)}, f32[2,2,32,24,128]{4,3,2,1,0:T(8,128)S(1)}, f32[2,32,8,128]{3,2,1,0:T(8,128)S(1)}) custom-call(f32[2,32,4096]{2,1,0:T(8,128)S(1)} %copy-done, f32[32,4096]{1,0:T(8,128)S(1)} %copy-done.1), custom_call_target="tpu_custom_call" | custom-call | flops 2147483648 | bytes 1048576 | tf_op jit(solution)/shard_map/inner/pallas_call | solution.py:275
  22.9 2.9 %collective-permute-start.2 = (f32[32,16,128]{2,1,0:T(8,128)S(1)}, f32[32,16,128]{2,1,0:T(8,128)S(1)}, u32[]{:S(2)}, u32[]{:S(2)}) collective-permute-start(f32[32,16,128]{2,1,0:T(8,128)S(1)} %get-tuple-element.21), channel_id=1, source_target_pairs={{64,0},{128,64},{192,128},{256,192},{320,256},{384,320},{448,384},... | collective-permute-start | bytes 786440 | tf_op jit(solution)/shard_map/ppermute | solution.py:283
  25.8 0.0 collective-permute-done.1.halo
  25.8 1.4 %edge_first.1.inner = f32[2,32,32,128]{3,2,1,0:T(8,128)S(1)} custom-call(f32[3,8,4096]{2,1,0:T(8,128)S(1)} %collective-permute-done.1.halo, f32[2,2,32,24,128]{4,3,2,1,0:T(8,128)S(1)} %get-tuple-element.16.history, f32[2,32,8,128]{3,2,1,0:T(8,128)S(1)} %get-tuple-element.17.edge_force, ...), custom_call_target="tpu_custom_call", output_to_operand_aliasing={{}: (3, {})} | custom-call | flops 4294967296 | bytes 1048576 | tf_op jit(solution)/shard_map/edge_first/pallas_call | solution.py:286
  27.3 0.0 copy-start.2
  27.3 0.0 collective-permute-done.halo
  27.3 1.5 %edge_second.1 = (f32[2,32,32,128]{3,2,1,0:T(8,128)S(1)}, f32[32,16,128]{2,1,0:T(8,128)S(1)}) custom-call(f32[3,8,4096]{2,1,0:T(8,128)S(1)} %collective-permute-done.halo, f32[2,2,32,24,128]{4,3,2,1,0:T(8,128)S(1)} %get-tuple-element.16.history, f32[2,32,8,128]{3,2,1,0:T(8,128)S(1)} %get-tuple-element.17.edge_force, ...), custom_call_target="tpu_custom_call", output_to_operand_aliasing={{0}: (3, {})} | custom-call | flops 1073741824 | bytes 1048576 | tf_op jit(solution)/shard_map/edge_second/pallas_call | solution.py:286
  28.8 3.7 %collective-permute-start.3 = (f32[32,16,128]{2,1,0:T(8,128)S(1)}, f32[32,16,128]{2,1,0:T(8,128)S(1)}, u32[]{:S(2)}, u32[]{:S(2)}) collective-permute-start(f32[32,16,128]{2,1,0:T(8,128)S(1)} %get-tuple-element.23), channel_id=1, source_target_pairs={{64,0},{128,64},{192,128},{256,192},{320,256},{384,320},{448,384},... | collective-permute-start | bytes 786440 | tf_op jit(solution)/shard_map/ppermute | solution.py:298
  32.5 3.0 %collective-permute-start.4 = (f32[2,32,32,128]{3,2,1,0:T(8,128)S(1)}, f32[2,32,32,128]{3,2,1,0:T(8,128)S(1)}, u32[]{:S(2)}, u32[]{:S(2)}) collective-permute-start(f32[2,32,32,128]{3,2,1,0:T(8,128)S(1)} %get-tuple-element.20.full), channel_id=1, source_target_pairs={{0,64},{64,128},{128,192},{192,256},{256,320},{320,384},{384,448},... | collective-permute-start | bytes 3145736 | tf_op jit(solution)/shard_map/ppermute | solution.py:299
  35.5 0.0 collective-permute-done.2.middle_high
  35.5 0.0 copy-done.2
  35.5 0.7 %local.1 = (f32[48,128]{1,0:T(8,128)S(1)}, f32[2,13,8,128]{3,2,1,0:T(8,128)S(1)}) custom-call(s32[16]{0:T(128)S(1)} %copy-done.2, f32[2,32,32,128]{3,2,1,0:T(8,128)S(1)} %get-tuple-element.20.full, f32[32,16,128]{2,1,0:T(8,128)S(1)} %collective-permute-done.2.middle_high), custom_call_target="tpu_custom_call" | custom-call | flops 268435456 | bytes 1048576 | tf_op jit(solution)/shard_map/local/pallas_call | solution.py:300
  36.3 1.4 %collective-permute-done.3.edges_high = f32[32,16,128]{2,1,0:T(8,128)S(1)} collective-permute-done((f32[32,16,128]{2,1,0:T(8,128)S(1)}, f32[32,16,128]{2,1,0:T(8,128)S(1)}, u32[]{:S(2)}, u32[]{:S(2)}) %collective-permute-start.3) | collective-permute-done | bytes 262176 | tf_op jit(solution)/shard_map/ppermute | solution.py:298
  37.6 0.2 square.1
  37.9 16.1 %all_to_all.10.parts = f32[64,1,128]{2,1,0:T(1,128)S(1)} all-to-all(f32[64,1,128]{2,1,0:T(1,128)S(1)} %square.1), channel_id=1, replica_groups=mesh['image'=8,'slab'=64] {'slab'}, dimensions={0} | all-to-all | bytes 65536 | tf_op jit(solution)/shard_map/all_to_all | solution.py:308
  53.9 0.0 collective-permute-done.4.full_low
  53.9 0.1 total.1
  54.0 8.8 %all_to_all.11.squares = f32[8,1,128]{2,1,0:T(1,128)S(1)} all-to-all(f32[8,1,128]{2,1,0:T(1,128)S(1)} %total.1), channel_id=1, replica_groups=mesh['image'=8,'slab'=64] {'image'}, dimensions={0} | all-to-all | bytes 8192 | tf_op jit(solution)/shard_map/all_to_all | solution.py:310
  62.9 1.2 %mix.1 = f32[2,32,4096]{2,1,0:T(8,128)} custom-call(f32[8,1,128]{2,1,0:T(1,128)S(1)} %all_to_all.11.squares, f32[2,13,8,128]{3,2,1,0:T(8,128)S(1)} %get-tuple-element.24.plan, f32[2,32,32,128]{3,2,1,0:T(8,128)S(1)} %get-tuple-element.20.full, f32[2,32,32,128]{3,2,1,0:T(8,128)S(1)} %collective-permute-done.4.full_low, ...), custom_call_target="tpu_custom_call" | custom-call | bytes 1048576 | tf_op jit(solution)/shard_map/mix/pallas_call | solution.py:312
Async XLA Ops:
  0.0 17.6 %copy-start.1 = (f32[32,4096]{1,0:T(8,128)S(1)}, f32[32,4096]{1,0:T(8,128)}, u32[]{:S(2)}) copy-start(f32[32,4096]{1,0:T(8,128)} %tilt.3) | copy-start | bytes 1572868
  0.0 17.6 %copy-start = (f32[2,32,4096]{2,1,0:T(8,128)S(1)}, f32[2,32,4096]{2,1,0:T(8,128)}, u32[]{:S(2)}) copy-start(f32[2,32,4096]{2,1,0:T(8,128)} %string.3) | copy-start | bytes 3145732
  1.3 24.5 %collective-permute-start.1 = (f32[3,8,4096]{2,1,0:T(8,128)S(1)}, f32[3,8,4096]{2,1,0:T(8,128)S(1)}, u32[]{:S(2)}, u32[]{:S(2)}) collective-permute-start(f32[3,8,4096]{2,1,0:T(8,128)S(1)} %get-tuple-element.18), channel_id=1, source_target_pairs={{0,63},{2,1},{4,3},{6,5},{8,7},{10,9},{12,11},{14,13},{16,15},{18,... | collective-permute-start | bytes 1179656 | tf_op jit(solution)/shard_map/ppermute | solution.py:271
  15.7 11.6 %collective-permute-start = (f32[3,8,4096]{2,1,0:T(8,128)S(1)}, f32[3,8,4096]{2,1,0:T(8,128)S(1)}, u32[]{:S(2)}, u32[]{:S(2)}) collective-permute-start(f32[3,8,4096]{2,1,0:T(8,128)S(1)} %get-tuple-element.15), channel_id=1, source_target_pairs={{0,1},{2,3},{4,5},{6,7},{8,9},{10,11},{12,13},{14,15},{16,17},{18,... | collective-permute-start | bytes 1179656 | tf_op jit(solution)/shard_map/ppermute | solution.py:272
  22.9 12.6 %collective-permute-start.2 = (f32[32,16,128]{2,1,0:T(8,128)S(1)}, f32[32,16,128]{2,1,0:T(8,128)S(1)}, u32[]{:S(2)}, u32[]{:S(2)}) collective-permute-start(f32[32,16,128]{2,1,0:T(8,128)S(1)} %get-tuple-element.21), channel_id=1, source_target_pairs={{64,0},{128,64},{192,128},{256,192},{320,256},{384,320},{448,384},... | collective-permute-start | bytes 786440 | tf_op jit(solution)/shard_map/ppermute | solution.py:283
  27.3 8.3 %copy-start.2 = (s32[16]{0:T(128)S(1)}, s32[16]{0:T(128)}, u32[]{:S(2)}) copy-start(s32[16]{0:T(128)} %sources.1) | copy-start | bytes 196
  28.8 8.9 %collective-permute-start.3 = (f32[32,16,128]{2,1,0:T(8,128)S(1)}, f32[32,16,128]{2,1,0:T(8,128)S(1)}, u32[]{:S(2)}, u32[]{:S(2)}) collective-permute-start(f32[32,16,128]{2,1,0:T(8,128)S(1)} %get-tuple-element.23), channel_id=1, source_target_pairs={{64,0},{128,64},{192,128},{256,192},{320,256},{384,320},{448,384},... | collective-permute-start | bytes 786440 | tf_op jit(solution)/shard_map/ppermute | solution.py:298
  32.5 21.4 %collective-permute-start.4 = (f32[2,32,32,128]{3,2,1,0:T(8,128)S(1)}, f32[2,32,32,128]{3,2,1,0:T(8,128)S(1)}, u32[]{:S(2)}, u32[]{:S(2)}) collective-permute-start(f32[2,32,32,128]{3,2,1,0:T(8,128)S(1)} %get-tuple-element.20.full), channel_id=1, source_target_pairs={{0,64},{64,128},{128,192},{192,256},{256,320},{320,384},{384,448},... | collective-permute-start | bytes 3145736 | tf_op jit(solution)/shard_map/ppermute | solution.py:299

commit v6 on v5

--- a/solution.py
+++ b/solution.py
@@ -16,11 +16,15 @@
 HALO_LIMIT = 54136 * 1024
 
 
-def partners(axis, first):
-    count = lax.axis_size(axis)
+def partners(first):
+    ranks, slabs = lax.axis_size("image"), lax.axis_size("slab")
     step = -1 if first else 1
-    evens = range(0, count, 2)
-    return [(i, (i + step) % count) for i in evens] + [((i + step) % count, i) for i in evens]
+    pairs = []
+    for i in range(ranks):
+        for s in range(i % 2, slabs, 2):
+            here, there = i * slabs + s, i * slabs + (s + step) % slabs
+            pairs += [(here, there), (there, here)]
+    return pairs
 
 
 def line(axis, distance):
@@ -28,8 +32,8 @@
     return [(i, i + distance) for i in devices if i + distance in devices]
 
 
-def is_odd(axis):
-    return lax.rem(lax.axis_index(axis), 2)
+def is_odd():
+    return lax.rem(lax.axis_index("image") + lax.axis_index("slab"), 2)
 
 
 def substep(source, target, force, row, out_row, force_row, columns, keep=None, keep_row=0):
@@ -53,7 +57,7 @@
 
 
 def halo_kernel(string, tilt, first, second, sems):
-    odd = is_odd("slab")
+    odd = is_odd()
     last = string.shape[1] - ROWS
     copies = []
     for n, (out, row) in enumerate(((first, odd * last), (second, (1 - odd) * last))):
@@ -126,7 +130,7 @@
     depth = full.shape[2]
     for side in range(2):
 
-        @pl.when(is_odd("slab") == (1 - side if is_second else side))
+        @pl.when(is_odd() == (1 - side if is_second else side))
         def one():
             edge_rows(side, halo, history, edge_force, full, even, odd, force)
 
@@ -268,8 +272,8 @@
     first, second = call(
         "halo", halo_kernel, (halo, halo), [HBM] * 2, [pltpu.SemaphoreType.DMA((4,))], limit=HALO_LIMIT
     )(string, tilt)
-    first = lax.ppermute(first, "slab", partners("slab", True))
-    second = lax.ppermute(second, "slab", partners("slab", False))
+    first = lax.ppermute(first, ("image", "slab"), partners(True))
+    second = lax.ppermute(second, ("image", "slab"), partners(False))
     whole = array(2, columns, depth, LANES)
     single = array(columns, half, LANES)
     full, middle, history, edge_force = call(

time: 64.4 us -> 64.3 us (level)
  blocking collectives: 24.9 us -> 25.9 us
  starting transfers between devices: 25.9 us -> 24.9 us
    ppermute x1, starting transfers between devices: 3.72 us -> 1.92 us  [body(): edges_high = lax.ppermute(edges, 'image', line('image', -1))]
    ppermute x2, starting transfers between devices: 16.3 us -> 17.4 us  [the longest x1 13.3 us: body(): second = lax.ppermute(second, ('image', 'slab'), partners(False))]
    all_to_all x1, blocking collectives: 16.1 us -> 17.1 us  [body(): parts = lax.all_to_all(parts, 'slab', 0, 0)]
    ppermute x1, starting transfers between devices: 2.88 us -> 1.92 us  [body(): middle_high = lax.ppermute(middle, 'image', line('image', -1))]
where the time goes in v6:
time: 64.3 us; the launch traced here: 64 us
  blocking collectives  25.9 us (40%)
  starting transfers between devices  24.9 us (39%)
  Pallas kernels  11.7 us (18%)
  waiting for transfers between devices  1.4 us (2%)
    all_to_all x1, blocking collectives, body(): parts = lax.all_to_all(parts, 'slab', 0, 0)  17.1 us
    ppermute x1, starting transfers between devices, body(): second = lax.ppermute(second, ('image', 'slab'), partners(False))  13.3 us
    all_to_all x1, blocking collectives, body(): squares = lax.all_to_all(squares, 'image', 0, 0)  8.84 us
    pallas_call x1, Pallas kernels, body(): call('inner', inner_kernel, (whole, single, array(2, 2, columns, 3 * ROWS...  5.27 us
    ppermute x1, starting transfers between devices, body(): first = lax.ppermute(first, ('image', 'slab'), partners(True))  4.03 us
    ppermute x1, starting transfers between devices, body(): full_low = lax.ppermute(full, 'image', line('image', 1))  3.64 us
    pallas_call x2, Pallas kernels, edge(): call(name, functools.partial(edge_kernel, is_second), (whole, single) if...  2.92 us
    ppermute x1, starting transfers between devices, body(): middle_high = lax.ppermute(middle, 'image', line('image', -1))  1.92 us
  transfers between devices with their start and end apart: 5, of which 1 were waited for; matrix products, arithmetic and copies ran while one was open for 0% of the time, Pallas kernels for 14%

profile of v6, /device:TPU:1, one launch (start us, length us, event | category | flops | bytes accessed | tf_op | source)
XLA Modules:
  0.0 64.0 jit_solution(2135682977032241597)
XLA Ops:
  0.0 0.0 copy-start.1
  0.0 0.0 copy-start
  0.0 1.3 %halo.1 = (f32[3,8,4096]{2,1,0:T(8,128)S(1)}, f32[3,8,4096]{2,1,0:T(8,128)S(1)}) custom-call(f32[2,32,4096]{2,1,0:T(8,128)} %string.3, f32[32,4096]{1,0:T(8,128)} %tilt.3), custom_call_target="tpu_custom_call" | custom-call | bytes 1048576 | tf_op jit(solution)/shard_map/halo/pallas_call | solution.py:272
  1.3 4.0 %collective-permute-start.1 = (f32[3,8,4096]{2,1,0:T(8,128)S(1)}, f32[3,8,4096]{2,1,0:T(8,128)S(1)}, u32[]{:S(2)}, u32[]{:S(2)}) collective-permute-start(f32[3,8,4096]{2,1,0:T(8,128)S(1)} %get-tuple-element.18), channel_id=1, source_target_pairs={{0,63},{63,0},{2,1},{1,2},{4,3},{3,4},{6,5},{5,6},{8,7},{7,8},{10,... | collective-permute-start | bytes 1179656 | tf_op jit(solution)/shard_map/ppermute | solution.py:275
  5.3 13.3 %collective-permute-start = (f32[3,8,4096]{2,1,0:T(8,128)S(1)}, f32[3,8,4096]{2,1,0:T(8,128)S(1)}, u32[]{:S(2)}, u32[]{:S(2)}) collective-permute-start(f32[3,8,4096]{2,1,0:T(8,128)S(1)} %get-tuple-element.15), channel_id=1, source_target_pairs={{0,1},{1,0},{2,3},{3,2},{4,5},{5,4},{6,7},{7,6},{8,9},{9,8},{10,11... | collective-permute-start | bytes 1179656 | tf_op jit(solution)/shard_map/ppermute | solution.py:276
  18.7 0.0 copy-done.1
  18.7 0.0 copy-done
  18.7 5.3 %inner.1 = (f32[2,32,32,128]{3,2,1,0:T(8,128)S(1)}, f32[32,16,128]{2,1,0:T(8,128)S(1)}, f32[2,2,32,24,128]{4,3,2,1,0:T(8,128)S(1)}, f32[2,32,8,128]{3,2,1,0:T(8,128)S(1)}) custom-call(f32[2,32,4096]{2,1,0:T(8,128)S(1)} %copy-done, f32[32,4096]{1,0:T(8,128)S(1)} %copy-done.1), custom_call_target="tpu_custom_call" | custom-call | flops 2147483648 | bytes 1048576 | tf_op jit(solution)/shard_map/inner/pallas_call | solution.py:279
  24.0 1.9 %collective-permute-start.2 = (f32[32,16,128]{2,1,0:T(8,128)S(1)}, f32[32,16,128]{2,1,0:T(8,128)S(1)}, u32[]{:S(2)}, u32[]{:S(2)}) collective-permute-start(f32[32,16,128]{2,1,0:T(8,128)S(1)} %get-tuple-element.21), channel_id=1, source_target_pairs={{64,0},{128,64},{192,128},{256,192},{320,256},{384,320},{448,384},... | collective-permute-start | bytes 786440 | tf_op jit(solution)/shard_map/ppermute | solution.py:287
  25.9 0.0 collective-permute-done.1.halo
  25.9 1.5 %edge_first.1.inner = f32[2,32,32,128]{3,2,1,0:T(8,128)S(1)} custom-call(f32[3,8,4096]{2,1,0:T(8,128)S(1)} %collective-permute-done.1.halo, f32[2,2,32,24,128]{4,3,2,1,0:T(8,128)S(1)} %get-tuple-element.16.history, f32[2,32,8,128]{3,2,1,0:T(8,128)S(1)} %get-tuple-element.17.edge_force, ...), custom_call_target="tpu_custom_call", output_to_operand_aliasing={{}: (3, {})} | custom-call | flops 4294967296 | bytes 1048576 | tf_op jit(solution)/shard_map/edge_first/pallas_call | solution.py:290
  27.4 0.0 copy-start.2
  27.4 0.0 collective-permute-done.halo
  27.4 1.5 %edge_second.1 = (f32[2,32,32,128]{3,2,1,0:T(8,128)S(1)}, f32[32,16,128]{2,1,0:T(8,128)S(1)}) custom-call(f32[3,8,4096]{2,1,0:T(8,128)S(1)} %collective-permute-done.halo, f32[2,2,32,24,128]{4,3,2,1,0:T(8,128)S(1)} %get-tuple-element.16.history, f32[2,32,8,128]{3,2,1,0:T(8,128)S(1)} %get-tuple-element.17.edge_force, ...), custom_call_target="tpu_custom_call", output_to_operand_aliasing={{0}: (3, {})} | custom-call | flops 1073741824 | bytes 1048576 | tf_op jit(solution)/shard_map/edge_second/pallas_call | solution.py:290
  28.9 1.9 %collective-permute-start.3 = (f32[32,16,128]{2,1,0:T(8,128)S(1)}, f32[32,16,128]{2,1,0:T(8,128)S(1)}, u32[]{:S(2)}, u32[]{:S(2)}) collective-permute-start(f32[32,16,128]{2,1,0:T(8,128)S(1)} %get-tuple-element.23), channel_id=1, source_target_pairs={{64,0},{128,64},{192,128},{256,192},{320,256},{384,320},{448,384},... | collective-permute-start | bytes 786440 | tf_op jit(solution)/shard_map/ppermute | solution.py:302
  30.8 3.6 %collective-permute-start.4 = (f32[2,32,32,128]{3,2,1,0:T(8,128)S(1)}, f32[2,32,32,128]{3,2,1,0:T(8,128)S(1)}, u32[]{:S(2)}, u32[]{:S(2)}) collective-permute-start(f32[2,32,32,128]{3,2,1,0:T(8,128)S(1)} %get-tuple-element.20.full), channel_id=1, source_target_pairs={{0,64},{64,128},{128,192},{192,256},{256,320},{320,384},{384,448},... | collective-permute-start | bytes 3145736 | tf_op jit(solution)/shard_map/ppermute | solution.py:303
  34.5 0.0 collective-permute-done.2.middle_high
  34.5 0.0 copy-done.2
  34.5 0.7 %local.1 = (f32[48,128]{1,0:T(8,128)S(1)}, f32[2,13,8,128]{3,2,1,0:T(8,128)S(1)}) custom-call(s32[16]{0:T(128)S(1)} %copy-done.2, f32[2,32,32,128]{3,2,1,0:T(8,128)S(1)} %get-tuple-element.20.full, f32[32,16,128]{2,1,0:T(8,128)S(1)} %collective-permute-done.2.middle_high), custom_call_target="tpu_custom_call" | custom-call | flops 268435456 | bytes 1048576 | tf_op jit(solution)/shard_map/local/pallas_call | solution.py:304
  35.2 1.4 %collective-permute-done.3.edges_high = f32[32,16,128]{2,1,0:T(8,128)S(1)} collective-permute-done((f32[32,16,128]{2,1,0:T(8,128)S(1)}, f32[32,16,128]{2,1,0:T(8,128)S(1)}, u32[]{:S(2)}, u32[]{:S(2)}) %collective-permute-start.3) | collective-permute-done | bytes 262176 | tf_op jit(solution)/shard_map/ppermute | solution.py:302
  36.6 0.2 square.1
  36.8 17.1 %all_to_all.10.parts = f32[64,1,128]{2,1,0:T(1,128)S(1)} all-to-all(f32[64,1,128]{2,1,0:T(1,128)S(1)} %square.1), channel_id=1, replica_groups=mesh['image'=8,'slab'=64] {'slab'}, dimensions={0} | all-to-all | bytes 65536 | tf_op jit(solution)/shard_map/all_to_all | solution.py:312
  53.9 0.0 collective-permute-done.4.full_low
  53.9 0.1 total.1
  54.0 8.8 %all_to_all.11.squares = f32[8,1,128]{2,1,0:T(1,128)S(1)} all-to-all(f32[8,1,128]{2,1,0:T(1,128)S(1)} %total.1), channel_id=1, replica_groups=mesh['image'=8,'slab'=64] {'image'}, dimensions={0} | all-to-all | bytes 8192 | tf_op jit(solution)/shard_map/all_to_all | solution.py:314
  62.8 1.2 %mix.1 = f32[2,32,4096]{2,1,0:T(8,128)} custom-call(f32[8,1,128]{2,1,0:T(1,128)S(1)} %all_to_all.11.squares, f32[2,13,8,128]{3,2,1,0:T(8,128)S(1)} %get-tuple-element.24.plan, f32[2,32,32,128]{3,2,1,0:T(8,128)S(1)} %get-tuple-element.20.full, f32[2,32,32,128]{3,2,1,0:T(8,128)S(1)} %collective-permute-done.4.full_low, ...), custom_call_target="tpu_custom_call" | custom-call | bytes 1048576 | tf_op jit(solution)/shard_map/mix/pallas_call | solution.py:316
Async XLA Ops:
  0.0 18.7 %copy-start.1 = (f32[32,4096]{1,0:T(8,128)S(1)}, f32[32,4096]{1,0:T(8,128)}, u32[]{:S(2)}) copy-start(f32[32,4096]{1,0:T(8,128)} %tilt.3) | copy-start | bytes 1572868
  0.0 18.7 %copy-start = (f32[2,32,4096]{2,1,0:T(8,128)S(1)}, f32[2,32,4096]{2,1,0:T(8,128)}, u32[]{:S(2)}) copy-start(f32[2,32,4096]{2,1,0:T(8,128)} %string.3) | copy-start | bytes 3145732
  1.3 24.6 %collective-permute-start.1 = (f32[3,8,4096]{2,1,0:T(8,128)S(1)}, f32[3,8,4096]{2,1,0:T(8,128)S(1)}, u32[]{:S(2)}, u32[]{:S(2)}) collective-permute-start(f32[3,8,4096]{2,1,0:T(8,128)S(1)} %get-tuple-element.18), channel_id=1, source_target_pairs={{0,63},{63,0},{2,1},{1,2},{4,3},{3,4},{6,5},{5,6},{8,7},{7,8},{10,... | collective-permute-start | bytes 1179656 | tf_op jit(solution)/shard_map/ppermute | solution.py:275
  5.3 22.1 %collective-permute-start = (f32[3,8,4096]{2,1,0:T(8,128)S(1)}, f32[3,8,4096]{2,1,0:T(8,128)S(1)}, u32[]{:S(2)}, u32[]{:S(2)}) collective-permute-start(f32[3,8,4096]{2,1,0:T(8,128)S(1)} %get-tuple-element.15), channel_id=1, source_target_pairs={{0,1},{1,0},{2,3},{3,2},{4,5},{5,4},{6,7},{7,6},{8,9},{9,8},{10,11... | collective-permute-start | bytes 1179656 | tf_op jit(solution)/shard_map/ppermute | solution.py:276
  24.0 10.5 %collective-permute-start.2 = (f32[32,16,128]{2,1,0:T(8,128)S(1)}, f32[32,16,128]{2,1,0:T(8,128)S(1)}, u32[]{:S(2)}, u32[]{:S(2)}) collective-permute-start(f32[32,16,128]{2,1,0:T(8,128)S(1)} %get-tuple-element.21), channel_id=1, source_target_pairs={{64,0},{128,64},{192,128},{256,192},{320,256},{384,320},{448,384},... | collective-permute-start | bytes 786440 | tf_op jit(solution)/shard_map/ppermute | solution.py:287
  27.4 7.1 %copy-start.2 = (s32[16]{0:T(128)S(1)}, s32[16]{0:T(128)}, u32[]{:S(2)}) copy-start(s32[16]{0:T(128)} %sources.1) | copy-start | bytes 196
  28.9 7.7 %collective-permute-start.3 = (f32[32,16,128]{2,1,0:T(8,128)S(1)}, f32[32,16,128]{2,1,0:T(8,128)S(1)}, u32[]{:S(2)}, u32[]{:S(2)}) collective-permute-start(f32[32,16,128]{2,1,0:T(8,128)S(1)} %get-tuple-element.23), channel_id=1, source_target_pairs={{64,0},{128,64},{192,128},{256,192},{320,256},{384,320},{448,384},... | collective-permute-start | bytes 786440 | tf_op jit(solution)/shard_map/ppermute | solution.py:302
  30.8 23.1 %collective-permute-start.4 = (f32[2,32,32,128]{3,2,1,0:T(8,128)S(1)}, f32[2,32,32,128]{3,2,1,0:T(8,128)S(1)}, u32[]{:S(2)}, u32[]{:S(2)}) collective-permute-start(f32[2,32,32,128]{3,2,1,0:T(8,128)S(1)} %get-tuple-element.20.full), channel_id=1, source_target_pairs={{0,64},{64,128},{128,192},{192,256},{256,320},{320,384},{384,448},... | collective-permute-start | bytes 3145736 | tf_op jit(solution)/shard_map/ppermute | solution.py:303

commit v7 on v5

--- a/solution.py
+++ b/solution.py
@@ -52,18 +52,29 @@
             keep[c, pl.ds(keep_row, ROWS), :] = result
 
 
-def halo_kernel(string, tilt, first, second, sems):
+def halo_kernel(string, tilt, first, second, rows, sems):
     odd = is_odd("slab")
     last = string.shape[1] - ROWS
+    columns = string.shape[2] // LANES
     copies = []
-    for n, (out, row) in enumerate(((first, odd * last), (second, (1 - odd) * last))):
-        rows = pl.ds(pl.multiple_of(row, ROWS), ROWS)
-        copies.append(pltpu.make_async_copy(string.at[:, rows], out.at[pl.ds(0, 2)], sems.at[2 * n]))
-        copies.append(pltpu.make_async_copy(tilt.at[rows], out.at[2], sems.at[2 * n + 1]))
+    for n, row in enumerate((odd * last, (1 - odd) * last)):
+        span = pl.ds(pl.multiple_of(row, ROWS), ROWS)
+        copies.append(pltpu.make_async_copy(string.at[:, span], rows.at[n, pl.ds(0, 2)], sems.at[2 * n]))
+        copies.append(pltpu.make_async_copy(tilt.at[span], rows.at[n, 2], sems.at[2 * n + 1]))
     for copy in copies:
         copy.start()
     for copy in copies:
         copy.wait()
+    bottom_first = jnp.full((ROWS, LANES), odd, jnp.int32) == 1
+    for n, out in enumerate((first, second)):
+        for c in range(columns):
+            place = pl.ds(c * LANES, LANES)
+            for image in range(2):
+                out[pl.ds((image * columns + c) * ROWS, ROWS), :] = rows[n, image, :, place]
+            whole = rows[n, 2, :, place]
+            moved = pltpu.roll(whole, ROWS - 1, 0)
+            near = jnp.where(bottom_first, moved, whole) if n == 0 else jnp.where(bottom_first, whole, moved)
+            out[pl.ds(2 * columns * ROWS + (ROWS - 1) * c, ROWS - 1), :] = near[: ROWS - 1]
 
 
 def inner_kernel(string, tilt, full, middle, history, edge_force, even, odd, force):
@@ -102,10 +113,10 @@
     columns, depth = full.shape[1:3]
     mine, theirs = ((ROWS, 0), (0, ROWS))[side]
     for c in range(columns):
-        place = pl.ds(c * LANES, LANES)
         for image in range(2):
-            even[image, c, pl.ds(theirs, ROWS), :] = halo[image, :, place]
-        force[c, pl.ds(theirs, ROWS), :] = DT * halo[2, :, place]
+            even[image, c, pl.ds(theirs, ROWS), :] = halo[pl.ds((image * columns + c) * ROWS, ROWS), :]
+        near = halo[pl.ds(2 * columns * ROWS + (ROWS - 1) * c, ROWS - 1), :]
+        force[c, pl.ds(theirs + 1 - side, ROWS - 1), :] = DT * near
         force[c, pl.ds(mine, ROWS), :] = edge_force[side, c]
     buffers = (even, odd)
     for step in range(1, SUBSTEPS + 1):
@@ -264,9 +275,14 @@
     def room(*shape):
         return pltpu.VMEM(shape, jnp.float32)
 
-    halo = array(3, ROWS, width)
+    halo = array(columns * (3 * ROWS - 1), LANES)
     first, second = call(
-        "halo", halo_kernel, (halo, halo), [HBM] * 2, [pltpu.SemaphoreType.DMA((4,))], limit=HALO_LIMIT
+        "halo",
+        halo_kernel,
+        (halo, halo),
+        [HBM] * 2,
+        [room(2, 3, ROWS, width), pltpu.SemaphoreType.DMA((4,))],
+        limit=HALO_LIMIT,
     )(string, tilt)
     first = lax.ppermute(first, "slab", partners("slab", True))
     second = lax.ppermute(second, "slab", partners("slab", False))

time: 64.4 us -> 64.1 us (level)
  no operation moved by 1% of the time
where the time goes in v7:
time: 64.1 us; the launch traced here: 63.8 us
  starting transfers between devices  25.6 us (40%)
  blocking collectives  24.9 us (39%)
  Pallas kernels  11.8 us (18%)
  waiting for transfers between devices  1.4 us (2%)
    all_to_all x1, blocking collectives, body(): parts = lax.all_to_all(parts, 'slab', 0, 0)  16.1 us
    ppermute x1, starting transfers between devices, body(): first = lax.ppermute(first, 'slab', partners('slab', True))  14.4 us
    all_to_all x1, blocking collectives, body(): squares = lax.all_to_all(squares, 'image', 0, 0)  8.84 us
    pallas_call x1, Pallas kernels, body(): call('inner', inner_kernel, (whole, single, array(2, 2, columns, 3 * ROWS...  5.27 us
    ppermute x1, starting transfers between devices, body(): edges_high = lax.ppermute(edges, 'image', line('image', -1))  3.39 us
    ppermute x1, starting transfers between devices, body(): full_low = lax.ppermute(full, 'image', line('image', 1))  3.02 us
    pallas_call x2, Pallas kernels, edge(): call(name, functools.partial(edge_kernel, is_second), (whole, single) if...  2.92 us
    ppermute x1, starting transfers between devices, body(): middle_high = lax.ppermute(middle, 'image', line('image', -1))  2.85 us
  transfers between devices with their start and end apart: 5, of which 1 were waited for; matrix products, arithmetic and copies ran while one was open for 0% of the time, Pallas kernels for 14%

profile of v7, /device:TPU:1, one launch (start us, length us, event | category | flops | bytes accessed | tf_op | source)
XLA Modules:
  0.0 63.8 jit_solution(9496055134050929388)
XLA Ops:
  0.0 0.0 copy-start.1
  0.0 0.0 copy-start
  0.0 1.3 %halo.1 = (f32[736,128]{1,0:T(8,128)S(1)}, f32[736,128]{1,0:T(8,128)S(1)}) custom-call(f32[2,32,4096]{2,1,0:T(8,128)} %string.3, f32[32,4096]{1,0:T(8,128)} %tilt.3), custom_call_target="tpu_custom_call" | custom-call | bytes 1048576 | tf_op jit(solution)/shard_map/halo/pallas_call | solution.py:279
  1.3 14.4 %collective-permute-start.1 = (f32[736,128]{1,0:T(8,128)S(1)}, f32[736,128]{1,0:T(8,128)S(1)}, u32[]{:S(2)}, u32[]{:S(2)}) collective-permute-start(f32[736,128]{1,0:T(8,128)S(1)} %get-tuple-element.18), channel_id=1, source_target_pairs={{0,63},{2,1},{4,3},{6,5},{8,7},{10,9},{12,11},{14,13},{16,15},{18,... | collective-permute-start | bytes 1130504 | tf_op jit(solution)/shard_map/ppermute | solution.py:287
  15.8 1.9 %collective-permute-start = (f32[736,128]{1,0:T(8,128)S(1)}, f32[736,128]{1,0:T(8,128)S(1)}, u32[]{:S(2)}, u32[]{:S(2)}) collective-permute-start(f32[736,128]{1,0:T(8,128)S(1)} %get-tuple-element.15), channel_id=1, source_target_pairs={{0,1},{2,3},{4,5},{6,7},{8,9},{10,11},{12,13},{14,15},{16,17},{18,... | collective-permute-start | bytes 1130504 | tf_op jit(solution)/shard_map/ppermute | solution.py:288
  17.7 0.0 copy-done.1
  17.7 0.0 copy-done
  17.7 5.3 %inner.1 = (f32[2,32,32,128]{3,2,1,0:T(8,128)S(1)}, f32[32,16,128]{2,1,0:T(8,128)S(1)}, f32[2,2,32,24,128]{4,3,2,1,0:T(8,128)S(1)}, f32[2,32,8,128]{3,2,1,0:T(8,128)S(1)}) custom-call(f32[2,32,4096]{2,1,0:T(8,128)S(1)} %copy-done, f32[32,4096]{1,0:T(8,128)S(1)} %copy-done.1), custom_call_target="tpu_custom_call" | custom-call | flops 2147483648 | bytes 1048576 | tf_op jit(solution)/shard_map/inner/pallas_call | solution.py:291
  23.0 2.9 %collective-permute-start.2 = (f32[32,16,128]{2,1,0:T(8,128)S(1)}, f32[32,16,128]{2,1,0:T(8,128)S(1)}, u32[]{:S(2)}, u32[]{:S(2)}) collective-permute-start(f32[32,16,128]{2,1,0:T(8,128)S(1)} %get-tuple-element.21), channel_id=1, source_target_pairs={{64,0},{128,64},{192,128},{256,192},{320,256},{384,320},{448,384},... | collective-permute-start | bytes 786440 | tf_op jit(solution)/shard_map/ppermute | solution.py:299
  25.8 0.0 collective-permute-done.1.halo
  25.9 1.4 %edge_first.1.inner = f32[2,32,32,128]{3,2,1,0:T(8,128)S(1)} custom-call(f32[736,128]{1,0:T(8,128)S(1)} %collective-permute-done.1.halo, f32[2,2,32,24,128]{4,3,2,1,0:T(8,128)S(1)} %get-tuple-element.16.history, f32[2,32,8,128]{3,2,1,0:T(8,128)S(1)} %get-tuple-element.17.edge_force, ...), custom_call_target="tpu_custom_call", output_to_operand_aliasing={{}: (3, {})} | custom-call | flops 4294967296 | bytes 1048576 | tf_op jit(solution)/shard_map/edge_first/pallas_call | solution.py:302
  27.3 0.0 copy-start.2
  27.3 0.0 collective-permute-done.halo
  27.3 1.5 %edge_second.1 = (f32[2,32,32,128]{3,2,1,0:T(8,128)S(1)}, f32[32,16,128]{2,1,0:T(8,128)S(1)}) custom-call(f32[736,128]{1,0:T(8,128)S(1)} %collective-permute-done.halo, f32[2,2,32,24,128]{4,3,2,1,0:T(8,128)S(1)} %get-tuple-element.16.history, f32[2,32,8,128]{3,2,1,0:T(8,128)S(1)} %get-tuple-element.17.edge_force, ...), custom_call_target="tpu_custom_call", output_to_operand_aliasing={{0}: (3, {})} | custom-call | flops 1073741824 | bytes 1048576 | tf_op jit(solution)/shard_map/edge_second/pallas_call | solution.py:302
  28.8 3.4 %collective-permute-start.3 = (f32[32,16,128]{2,1,0:T(8,128)S(1)}, f32[32,16,128]{2,1,0:T(8,128)S(1)}, u32[]{:S(2)}, u32[]{:S(2)}) collective-permute-start(f32[32,16,128]{2,1,0:T(8,128)S(1)} %get-tuple-element.23), channel_id=1, source_target_pairs={{64,0},{128,64},{192,128},{256,192},{320,256},{384,320},{448,384},... | collective-permute-start | bytes 786440 | tf_op jit(solution)/shard_map/ppermute | solution.py:314
  32.2 3.0 %collective-permute-start.4 = (f32[2,32,32,128]{3,2,1,0:T(8,128)S(1)}, f32[2,32,32,128]{3,2,1,0:T(8,128)S(1)}, u32[]{:S(2)}, u32[]{:S(2)}) collective-permute-start(f32[2,32,32,128]{3,2,1,0:T(8,128)S(1)} %get-tuple-element.20.full), channel_id=1, source_target_pairs={{0,64},{64,128},{128,192},{192,256},{256,320},{320,384},{384,448},... | collective-permute-start | bytes 3145736 | tf_op jit(solution)/shard_map/ppermute | solution.py:315
  35.2 0.0 collective-permute-done.2.middle_high
  35.2 0.0 copy-done.2
  35.2 0.7 %local.1 = (f32[48,128]{1,0:T(8,128)S(1)}, f32[2,13,8,128]{3,2,1,0:T(8,128)S(1)}) custom-call(s32[16]{0:T(128)S(1)} %copy-done.2, f32[2,32,32,128]{3,2,1,0:T(8,128)S(1)} %get-tuple-element.20.full, f32[32,16,128]{2,1,0:T(8,128)S(1)} %collective-permute-done.2.middle_high), custom_call_target="tpu_custom_call" | custom-call | flops 268435456 | bytes 1048576 | tf_op jit(solution)/shard_map/local/pallas_call | solution.py:316
  35.9 1.4 %collective-permute-done.3.edges_high = f32[32,16,128]{2,1,0:T(8,128)S(1)} collective-permute-done((f32[32,16,128]{2,1,0:T(8,128)S(1)}, f32[32,16,128]{2,1,0:T(8,128)S(1)}, u32[]{:S(2)}, u32[]{:S(2)}) %collective-permute-start.3) | collective-permute-done | bytes 262176 | tf_op jit(solution)/shard_map/ppermute | solution.py:314
  37.3 0.2 square.1
  37.6 16.1 %all_to_all.10.parts = f32[64,1,128]{2,1,0:T(1,128)S(1)} all-to-all(f32[64,1,128]{2,1,0:T(1,128)S(1)} %square.1), channel_id=1, replica_groups=mesh['image'=8,'slab'=64] {'slab'}, dimensions={0} | all-to-all | bytes 65536 | tf_op jit(solution)/shard_map/all_to_all | solution.py:324
  53.6 0.0 collective-permute-done.4.full_low
  53.6 0.1 total.1
  53.7 8.8 %all_to_all.11.squares = f32[8,1,128]{2,1,0:T(1,128)S(1)} all-to-all(f32[8,1,128]{2,1,0:T(1,128)S(1)} %total.1), channel_id=1, replica_groups=mesh['image'=8,'slab'=64] {'image'}, dimensions={0} | all-to-all | bytes 8192 | tf_op jit(solution)/shard_map/all_to_all | solution.py:326
  62.6 1.2 %mix.1 = f32[2,32,4096]{2,1,0:T(8,128)} custom-call(f32[8,1,128]{2,1,0:T(1,128)S(1)} %all_to_all.11.squares, f32[2,13,8,128]{3,2,1,0:T(8,128)S(1)} %get-tuple-element.24.plan, f32[2,32,32,128]{3,2,1,0:T(8,128)S(1)} %get-tuple-element.20.full, f32[2,32,32,128]{3,2,1,0:T(8,128)S(1)} %collective-permute-done.4.full_low, ...), custom_call_target="tpu_custom_call" | custom-call | bytes 1048576 | tf_op jit(solution)/shard_map/mix/pallas_call | solution.py:328
Async XLA Ops:
  0.0 17.7 %copy-start.1 = (f32[32,4096]{1,0:T(8,128)S(1)}, f32[32,4096]{1,0:T(8,128)}, u32[]{:S(2)}) copy-start(f32[32,4096]{1,0:T(8,128)} %tilt.3) | copy-start | bytes 1572868
  0.0 17.7 %copy-start = (f32[2,32,4096]{2,1,0:T(8,128)S(1)}, f32[2,32,4096]{2,1,0:T(8,128)}, u32[]{:S(2)}) copy-start(f32[2,32,4096]{2,1,0:T(8,128)} %string.3) | copy-start | bytes 3145732
  1.3 24.5 %collective-permute-start.1 = (f32[736,128]{1,0:T(8,128)S(1)}, f32[736,128]{1,0:T(8,128)S(1)}, u32[]{:S(2)}, u32[]{:S(2)}) collective-permute-start(f32[736,128]{1,0:T(8,128)S(1)} %get-tuple-element.18), channel_id=1, source_target_pairs={{0,63},{2,1},{4,3},{6,5},{8,7},{10,9},{12,11},{14,13},{16,15},{18,... | collective-permute-start | bytes 1130504 | tf_op jit(solution)/shard_map/ppermute | solution.py:287
  15.8 11.6 %collective-permute-start = (f32[736,128]{1,0:T(8,128)S(1)}, f32[736,128]{1,0:T(8,128)S(1)}, u32[]{:S(2)}, u32[]{:S(2)}) collective-permute-start(f32[736,128]{1,0:T(8,128)S(1)} %get-tuple-element.15), channel_id=1, source_target_pairs={{0,1},{2,3},{4,5},{6,7},{8,9},{10,11},{12,13},{14,15},{16,17},{18,... | collective-permute-start | bytes 1130504 | tf_op jit(solution)/shard_map/ppermute | solution.py:288
  23.0 12.2 %collective-permute-start.2 = (f32[32,16,128]{2,1,0:T(8,128)S(1)}, f32[32,16,128]{2,1,0:T(8,128)S(1)}, u32[]{:S(2)}, u32[]{:S(2)}) collective-permute-start(f32[32,16,128]{2,1,0:T(8,128)S(1)} %get-tuple-element.21), channel_id=1, source_target_pairs={{64,0},{128,64},{192,128},{256,192},{320,256},{384,320},{448,384},... | collective-permute-start | bytes 786440 | tf_op jit(solution)/shard_map/ppermute | solution.py:299
  27.3 7.9 %copy-start.2 = (s32[16]{0:T(128)S(1)}, s32[16]{0:T(128)}, u32[]{:S(2)}) copy-start(s32[16]{0:T(128)} %sources.1) | copy-start | bytes 196
  28.8 8.5 %collective-permute-start.3 = (f32[32,16,128]{2,1,0:T(8,128)S(1)}, f32[32,16,128]{2,1,0:T(8,128)S(1)}, u32[]{:S(2)}, u32[]{:S(2)}) collective-permute-start(f32[32,16,128]{2,1,0:T(8,128)S(1)} %get-tuple-element.23), channel_id=1, source_target_pairs={{64,0},{128,64},{192,128},{256,192},{320,256},{384,320},{448,384},... | collective-permute-start | bytes 786440 | tf_op jit(solution)/shard_map/ppermute | solution.py:314
  32.2 21.4 %collective-permute-start.4 = (f32[2,32,32,128]{3,2,1,0:T(8,128)S(1)}, f32[2,32,32,128]{3,2,1,0:T(8,128)S(1)}, u32[]{:S(2)}, u32[]{:S(2)}) collective-permute-start(f32[2,32,32,128]{3,2,1,0:T(8,128)S(1)} %get-tuple-element.20.full), channel_id=1, source_target_pairs={{0,64},{64,128},{128,192},{192,256},{256,320},{320,384},{384,448},... | collective-permute-start | bytes 3145736 | tf_op jit(solution)/shard_map/ppermute | solution.py:315

commit v8 on v7

--- a/solution.py
+++ b/solution.py
@@ -16,11 +16,15 @@
 HALO_LIMIT = 54136 * 1024
 
 
-def partners(axis, first):
-    count = lax.axis_size(axis)
+def partners(first):
+    ranks, slabs = lax.axis_size("image"), lax.axis_size("slab")
     step = -1 if first else 1
-    evens = range(0, count, 2)
-    return [(i, (i + step) % count) for i in evens] + [((i + step) % count, i) for i in evens]
+    pairs = []
+    for i in range(ranks):
+        for s in range(i % 2, slabs, 2):
+            here, there = i * slabs + s, i * slabs + (s + step) % slabs
+            pairs += [(here, there), (there, here)]
+    return pairs
 
 
 def line(axis, distance):
@@ -28,8 +32,8 @@
     return [(i, i + distance) for i in devices if i + distance in devices]
 
 
-def is_odd(axis):
-    return lax.rem(lax.axis_index(axis), 2)
+def is_odd():
+    return lax.rem(lax.axis_index("image") + lax.axis_index("slab"), 2)
 
 
 def substep(source, target, force, row, out_row, force_row, columns, keep=None, keep_row=0):
@@ -53,7 +57,7 @@
 
 
 def halo_kernel(string, tilt, first, second, rows, sems):
-    odd = is_odd("slab")
+    odd = is_odd()
     last = string.shape[1] - ROWS
     columns = string.shape[2] // LANES
     copies = []
@@ -137,7 +141,7 @@
     depth = full.shape[2]
     for side in range(2):
 
-        @pl.when(is_odd("slab") == (1 - side if is_second else side))
+        @pl.when(is_odd() == (1 - side if is_second else side))
         def one():
             edge_rows(side, halo, history, edge_force, full, even, odd, force)
 
@@ -284,8 +288,8 @@
         [room(2, 3, ROWS, width), pltpu.SemaphoreType.DMA((4,))],
         limit=HALO_LIMIT,
     )(string, tilt)
-    first = lax.ppermute(first, "slab", partners("slab", True))
-    second = lax.ppermute(second, "slab", partners("slab", False))
+    first = lax.ppermute(first, ("image", "slab"), partners(True))
+    second = lax.ppermute(second, ("image", "slab"), partners(False))
     whole = array(2, columns, depth, LANES)
     single = array(columns, half, LANES)
     full, middle, history, edge_force = call(

time: 64.1 us -> 64 us (level)
  blocking collectives: 24.9 us -> 25.6 us
  starting transfers between devices: 25.6 us -> 24.9 us
    ppermute x1, starting transfers between devices: 3.39 us -> 1.92 us  [body(): edges_high = lax.ppermute(edges, 'image', line('image', -1))]
    ppermute x2, starting transfers between devices: 16.3 us -> 17.4 us  [the longest x1 13.3 us: body(): second = lax.ppermute(second, ('image', 'slab'), partners(False))]
    ppermute x1, starting transfers between devices: 2.85 us -> 1.92 us  [body(): middle_high = lax.ppermute(middle, 'image', line('image', -1))]
    all_to_all x1, blocking collectives: 16.1 us -> 16.7 us  [body(): parts = lax.all_to_all(parts, 'slab', 0, 0)]
where the time goes in v8:
time: 64 us; the launch traced here: 63.7 us
  blocking collectives  25.6 us (40%)
  starting transfers between devices  24.9 us (39%)
  Pallas kernels  11.8 us (18%)
  waiting for transfers between devices  1.4 us (2%)
    all_to_all x1, blocking collectives, body(): parts = lax.all_to_all(parts, 'slab', 0, 0)  16.7 us
    ppermute x1, starting transfers between devices, body(): second = lax.ppermute(second, ('image', 'slab'), partners(False))  13.3 us
    all_to_all x1, blocking collectives, body(): squares = lax.all_to_all(squares, 'image', 0, 0)  8.84 us
    pallas_call x1, Pallas kernels, body(): call('inner', inner_kernel, (whole, single, array(2, 2, columns, 3 * ROWS...  5.27 us
    ppermute x1, starting transfers between devices, body(): first = lax.ppermute(first, ('image', 'slab'), partners(True))  4.03 us
    ppermute x1, starting transfers between devices, body(): full_low = lax.ppermute(full, 'image', line('image', 1))  3.64 us
    pallas_call x2, Pallas kernels, edge(): call(name, functools.partial(edge_kernel, is_second), (whole, single) if...  2.92 us
    ppermute x1, starting transfers between devices, body(): middle_high = lax.ppermute(middle, 'image', line('image', -1))  1.92 us
  transfers between devices with their start and end apart: 5, of which 1 were waited for; matrix products, arithmetic and copies ran while one was open for 0% of the time, Pallas kernels for 14%

profile of v8, /device:TPU:1, one launch (start us, length us, event | category | flops | bytes accessed | tf_op | source)
XLA Modules:
  0.0 63.7 jit_solution(13452871188736283363)
XLA Ops:
  0.0 0.0 copy-start.1
  0.0 0.0 copy-start
  0.0 1.3 %halo.1 = (f32[736,128]{1,0:T(8,128)S(1)}, f32[736,128]{1,0:T(8,128)S(1)}) custom-call(f32[2,32,4096]{2,1,0:T(8,128)} %string.3, f32[32,4096]{1,0:T(8,128)} %tilt.3), custom_call_target="tpu_custom_call" | custom-call | bytes 1048576 | tf_op jit(solution)/shard_map/halo/pallas_call | solution.py:283
  1.3 4.0 %collective-permute-start.1 = (f32[736,128]{1,0:T(8,128)S(1)}, f32[736,128]{1,0:T(8,128)S(1)}, u32[]{:S(2)}, u32[]{:S(2)}) collective-permute-start(f32[736,128]{1,0:T(8,128)S(1)} %get-tuple-element.18), channel_id=1, source_target_pairs={{0,63},{63,0},{2,1},{1,2},{4,3},{3,4},{6,5},{5,6},{8,7},{7,8},{10,... | collective-permute-start | bytes 1130504 | tf_op jit(solution)/shard_map/ppermute | solution.py:291
  5.4 13.3 %collective-permute-start = (f32[736,128]{1,0:T(8,128)S(1)}, f32[736,128]{1,0:T(8,128)S(1)}, u32[]{:S(2)}, u32[]{:S(2)}) collective-permute-start(f32[736,128]{1,0:T(8,128)S(1)} %get-tuple-element.15), channel_id=1, source_target_pairs={{0,1},{1,0},{2,3},{3,2},{4,5},{5,4},{6,7},{7,6},{8,9},{9,8},{10,11... | collective-permute-start | bytes 1130504 | tf_op jit(solution)/shard_map/ppermute | solution.py:292
  18.7 0.0 copy-done.1
  18.7 0.0 copy-done
  18.8 5.3 %inner.1 = (f32[2,32,32,128]{3,2,1,0:T(8,128)S(1)}, f32[32,16,128]{2,1,0:T(8,128)S(1)}, f32[2,2,32,24,128]{4,3,2,1,0:T(8,128)S(1)}, f32[2,32,8,128]{3,2,1,0:T(8,128)S(1)}) custom-call(f32[2,32,4096]{2,1,0:T(8,128)S(1)} %copy-done, f32[32,4096]{1,0:T(8,128)S(1)} %copy-done.1), custom_call_target="tpu_custom_call" | custom-call | flops 2147483648 | bytes 1048576 | tf_op jit(solution)/shard_map/inner/pallas_call | solution.py:295
  24.0 1.9 %collective-permute-start.2 = (f32[32,16,128]{2,1,0:T(8,128)S(1)}, f32[32,16,128]{2,1,0:T(8,128)S(1)}, u32[]{:S(2)}, u32[]{:S(2)}) collective-permute-start(f32[32,16,128]{2,1,0:T(8,128)S(1)} %get-tuple-element.21), channel_id=1, source_target_pairs={{64,0},{128,64},{192,128},{256,192},{320,256},{384,320},{448,384},... | collective-permute-start | bytes 786440 | tf_op jit(solution)/shard_map/ppermute | solution.py:303
  26.0 0.0 collective-permute-done.1.halo
  26.0 1.5 %edge_first.1.inner = f32[2,32,32,128]{3,2,1,0:T(8,128)S(1)} custom-call(f32[736,128]{1,0:T(8,128)S(1)} %collective-permute-done.1.halo, f32[2,2,32,24,128]{4,3,2,1,0:T(8,128)S(1)} %get-tuple-element.16.history, f32[2,32,8,128]{3,2,1,0:T(8,128)S(1)} %get-tuple-element.17.edge_force, ...), custom_call_target="tpu_custom_call", output_to_operand_aliasing={{}: (3, {})} | custom-call | flops 4294967296 | bytes 1048576 | tf_op jit(solution)/shard_map/edge_first/pallas_call | solution.py:306
  27.4 0.0 copy-start.2
  27.4 0.0 collective-permute-done.halo
  27.5 1.5 %edge_second.1 = (f32[2,32,32,128]{3,2,1,0:T(8,128)S(1)}, f32[32,16,128]{2,1,0:T(8,128)S(1)}) custom-call(f32[736,128]{1,0:T(8,128)S(1)} %collective-permute-done.halo, f32[2,2,32,24,128]{4,3,2,1,0:T(8,128)S(1)} %get-tuple-element.16.history, f32[2,32,8,128]{3,2,1,0:T(8,128)S(1)} %get-tuple-element.17.edge_force, ...), custom_call_target="tpu_custom_call", output_to_operand_aliasing={{0}: (3, {})} | custom-call | flops 1073741824 | bytes 1048576 | tf_op jit(solution)/shard_map/edge_second/pallas_call | solution.py:306
  28.9 1.9 %collective-permute-start.3 = (f32[32,16,128]{2,1,0:T(8,128)S(1)}, f32[32,16,128]{2,1,0:T(8,128)S(1)}, u32[]{:S(2)}, u32[]{:S(2)}) collective-permute-start(f32[32,16,128]{2,1,0:T(8,128)S(1)} %get-tuple-element.23), channel_id=1, source_target_pairs={{64,0},{128,64},{192,128},{256,192},{320,256},{384,320},{448,384},... | collective-permute-start | bytes 786440 | tf_op jit(solution)/shard_map/ppermute | solution.py:318
  30.9 3.6 %collective-permute-start.4 = (f32[2,32,32,128]{3,2,1,0:T(8,128)S(1)}, f32[2,32,32,128]{3,2,1,0:T(8,128)S(1)}, u32[]{:S(2)}, u32[]{:S(2)}) collective-permute-start(f32[2,32,32,128]{3,2,1,0:T(8,128)S(1)} %get-tuple-element.20.full), channel_id=1, source_target_pairs={{0,64},{64,128},{128,192},{192,256},{256,320},{320,384},{384,448},... | collective-permute-start | bytes 3145736 | tf_op jit(solution)/shard_map/ppermute | solution.py:319
  34.5 0.0 collective-permute-done.2.middle_high
  34.5 0.0 copy-done.2
  34.5 0.7 %local.1 = (f32[48,128]{1,0:T(8,128)S(1)}, f32[2,13,8,128]{3,2,1,0:T(8,128)S(1)}) custom-call(s32[16]{0:T(128)S(1)} %copy-done.2, f32[2,32,32,128]{3,2,1,0:T(8,128)S(1)} %get-tuple-element.20.full, f32[32,16,128]{2,1,0:T(8,128)S(1)} %collective-permute-done.2.middle_high), custom_call_target="tpu_custom_call" | custom-call | flops 268435456 | bytes 1048576 | tf_op jit(solution)/shard_map/local/pallas_call | solution.py:320
  35.2 1.4 %collective-permute-done.3.edges_high = f32[32,16,128]{2,1,0:T(8,128)S(1)} collective-permute-done((f32[32,16,128]{2,1,0:T(8,128)S(1)}, f32[32,16,128]{2,1,0:T(8,128)S(1)}, u32[]{:S(2)}, u32[]{:S(2)}) %collective-permute-start.3) | collective-permute-done | bytes 262176 | tf_op jit(solution)/shard_map/ppermute | solution.py:318
  36.6 0.2 square.1
  36.9 16.7 %all_to_all.10.parts = f32[64,1,128]{2,1,0:T(1,128)S(1)} all-to-all(f32[64,1,128]{2,1,0:T(1,128)S(1)} %square.1), channel_id=1, replica_groups=mesh['image'=8,'slab'=64] {'slab'}, dimensions={0} | all-to-all | bytes 65536 | tf_op jit(solution)/shard_map/all_to_all | solution.py:328
  53.6 0.0 collective-permute-done.4.full_low
  53.6 0.1 total.1
  53.7 8.8 %all_to_all.11.squares = f32[8,1,128]{2,1,0:T(1,128)S(1)} all-to-all(f32[8,1,128]{2,1,0:T(1,128)S(1)} %total.1), channel_id=1, replica_groups=mesh['image'=8,'slab'=64] {'image'}, dimensions={0} | all-to-all | bytes 8192 | tf_op jit(solution)/shard_map/all_to_all | solution.py:330
  62.5 1.2 %mix.1 = f32[2,32,4096]{2,1,0:T(8,128)} custom-call(f32[8,1,128]{2,1,0:T(1,128)S(1)} %all_to_all.11.squares, f32[2,13,8,128]{3,2,1,0:T(8,128)S(1)} %get-tuple-element.24.plan, f32[2,32,32,128]{3,2,1,0:T(8,128)S(1)} %get-tuple-element.20.full, f32[2,32,32,128]{3,2,1,0:T(8,128)S(1)} %collective-permute-done.4.full_low, ...), custom_call_target="tpu_custom_call" | custom-call | bytes 1048576 | tf_op jit(solution)/shard_map/mix/pallas_call | solution.py:332
Async XLA Ops:
  0.0 18.7 %copy-start.1 = (f32[32,4096]{1,0:T(8,128)S(1)}, f32[32,4096]{1,0:T(8,128)}, u32[]{:S(2)}) copy-start(f32[32,4096]{1,0:T(8,128)} %tilt.3) | copy-start | bytes 1572868
  0.0 18.7 %copy-start = (f32[2,32,4096]{2,1,0:T(8,128)S(1)}, f32[2,32,4096]{2,1,0:T(8,128)}, u32[]{:S(2)}) copy-start(f32[2,32,4096]{2,1,0:T(8,128)} %string.3) | copy-start | bytes 3145732
  1.3 24.6 %collective-permute-start.1 = (f32[736,128]{1,0:T(8,128)S(1)}, f32[736,128]{1,0:T(8,128)S(1)}, u32[]{:S(2)}, u32[]{:S(2)}) collective-permute-start(f32[736,128]{1,0:T(8,128)S(1)} %get-tuple-element.18), channel_id=1, source_target_pairs={{0,63},{63,0},{2,1},{1,2},{4,3},{3,4},{6,5},{5,6},{8,7},{7,8},{10,... | collective-permute-start | bytes 1130504 | tf_op jit(solution)/shard_map/ppermute | solution.py:291
  5.4 22.1 %collective-permute-start = (f32[736,128]{1,0:T(8,128)S(1)}, f32[736,128]{1,0:T(8,128)S(1)}, u32[]{:S(2)}, u32[]{:S(2)}) collective-permute-start(f32[736,128]{1,0:T(8,128)S(1)} %get-tuple-element.15), channel_id=1, source_target_pairs={{0,1},{1,0},{2,3},{3,2},{4,5},{5,4},{6,7},{7,6},{8,9},{9,8},{10,11... | collective-permute-start | bytes 1130504 | tf_op jit(solution)/shard_map/ppermute | solution.py:292
  24.0 10.5 %collective-permute-start.2 = (f32[32,16,128]{2,1,0:T(8,128)S(1)}, f32[32,16,128]{2,1,0:T(8,128)S(1)}, u32[]{:S(2)}, u32[]{:S(2)}) collective-permute-start(f32[32,16,128]{2,1,0:T(8,128)S(1)} %get-tuple-element.21), channel_id=1, source_target_pairs={{64,0},{128,64},{192,128},{256,192},{320,256},{384,320},{448,384},... | collective-permute-start | bytes 786440 | tf_op jit(solution)/shard_map/ppermute | solution.py:303
  27.4 7.1 %copy-start.2 = (s32[16]{0:T(128)S(1)}, s32[16]{0:T(128)}, u32[]{:S(2)}) copy-start(s32[16]{0:T(128)} %sources.1) | copy-start | bytes 196
  28.9 7.7 %collective-permute-start.3 = (f32[32,16,128]{2,1,0:T(8,128)S(1)}, f32[32,16,128]{2,1,0:T(8,128)S(1)}, u32[]{:S(2)}, u32[]{:S(2)}) collective-permute-start(f32[32,16,128]{2,1,0:T(8,128)S(1)} %get-tuple-element.23), channel_id=1, source_target_pairs={{64,0},{128,64},{192,128},{256,192},{320,256},{384,320},{448,384},... | collective-permute-start | bytes 786440 | tf_op jit(solution)/shard_map/ppermute | solution.py:318
  30.9 22.7 %collective-permute-start.4 = (f32[2,32,32,128]{3,2,1,0:T(8,128)S(1)}, f32[2,32,32,128]{3,2,1,0:T(8,128)S(1)}, u32[]{:S(2)}, u32[]{:S(2)}) collective-permute-start(f32[2,32,32,128]{3,2,1,0:T(8,128)S(1)} %get-tuple-element.20.full), channel_id=1, source_target_pairs={{0,64},{64,128},{128,192},{192,256},{256,320},{320,384},{384,448},... | collective-permute-start | bytes 3145736 | tf_op jit(solution)/shard_map/ppermute | solution.py:319

commit v9 on v8

--- a/solution.py
+++ b/solution.py
@@ -113,42 +113,38 @@
     middle[...] = full[0, :, pl.ds(ROWS, depth - 2 * ROWS), :]
 
 
-def edge_rows(side, halo, history, edge_force, full, even, odd, force):
+def edge_kernel(first, second, history, edge_force, inner, full, edges, even, odd, force):
     columns, depth = full.shape[1:3]
-    mine, theirs = ((ROWS, 0), (0, ROWS))[side]
-    for c in range(columns):
-        for image in range(2):
-            even[image, c, pl.ds(theirs, ROWS), :] = halo[pl.ds((image * columns + c) * ROWS, ROWS), :]
-        near = halo[pl.ds(2 * columns * ROWS + (ROWS - 1) * c, ROWS - 1), :]
-        force[c, pl.ds(theirs + 1 - side, ROWS - 1), :] = DT * near
-        force[c, pl.ds(mine, ROWS), :] = edge_force[side, c]
+    tall = jnp.full((ROWS, LANES), is_odd(), jnp.int32) == 1
+
+    def received(side, span, rows):
+        pair = (first[span, :], second[span, :])
+        return jnp.where(tall[:rows], pair[1 - side], pair[side])
+
+    for side in range(2):
+        mine, theirs = ((ROWS, 0), (0, ROWS))[side]
+        for c in range(columns):
+            for image in range(2):
+                span = pl.ds((image * columns + c) * ROWS, ROWS)
+                even[side, image, c, pl.ds(theirs, ROWS), :] = received(side, span, ROWS)
+            near = received(side, pl.ds(2 * columns * ROWS + (ROWS - 1) * c, ROWS - 1), ROWS - 1)
+            force[side, c, pl.ds(theirs + 1 - side, ROWS - 1), :] = DT * near
+            force[side, c, pl.ds(mine, ROWS), :] = edge_force[side, c]
     buffers = (even, odd)
     for step in range(1, SUBSTEPS + 1):
         source, target = buffers[(step - 1) % 2], buffers[step % 2]
-        out_row = theirs
-        if step == SUBSTEPS:
-            target, out_row = full, side * (depth - ROWS)
-        kept = 2 * (step - 1) if side == 0 else 2 * SUBSTEPS + 4 - 2 * (step - 1)
-        row, force_row = (1, step) if side == 0 else (ROWS - 1, ROWS - step)
         for image in range(2):
-            for c in range(columns):
-                source[image, c, pl.ds(ROWS - 2 * side, 2), :] = history[side, image, c, pl.ds(kept, 2), :]
-            substep(source.at[image], target.at[image], force, row, out_row, force_row, columns)
-
-
-def edge_kernel(is_second, halo, history, edge_force, inner, full, *rest):
-    even, odd, force = rest[-3:]
-    depth = full.shape[2]
-    for side in range(2):
-
-        @pl.when(is_odd() == (1 - side if is_second else side))
-        def one():
-            edge_rows(side, halo, history, edge_force, full, even, odd, force)
-
-    if is_second:
-        edges = rest[0]
-        edges[:, pl.ds(0, ROWS), :] = full[0, :, pl.ds(0, ROWS), :]
-        edges[:, pl.ds(ROWS, ROWS), :] = full[0, :, pl.ds(depth - ROWS, ROWS), :]
+            for side in range(2):
+                out, out_row = target.at[side, image], (0, ROWS)[side]
+                if step == SUBSTEPS:
+                    out, out_row = full.at[image], side * (depth - ROWS)
+                kept = 2 * (step - 1) if side == 0 else 2 * SUBSTEPS + 4 - 2 * (step - 1)
+                row, force_row = (1, step) if side == 0 else (ROWS - 1, ROWS - step)
+                for c in range(columns):
+                    source[side, image, c, pl.ds(ROWS - 2 * side, 2), :] = history[side, image, c, pl.ds(kept, 2), :]
+                substep(source.at[side, image], out, force.at[side], row, out_row, force_row, columns)
+    edges[:, pl.ds(0, ROWS), :] = full[0, :, pl.ds(0, ROWS), :]
+    edges[:, pl.ds(ROWS, ROWS), :] = full[0, :, pl.ds(depth - ROWS, ROWS), :]
 
 
 def differences(upper, lower, columns, sums):
@@ -302,19 +298,15 @@
     )(string, tilt)
     middle_high = lax.ppermute(middle, "image", line("image", -1))
 
-    def edge(name, is_second, received, full):
-        return call(
-            name,
-            functools.partial(edge_kernel, is_second),
-            (whole, single) if is_second else (whole,),
-            [VMEM] * 4,
-            [room(2, columns, half, LANES), room(2, columns, half, LANES), room(columns, half, LANES)],
-            cost=1 << 30 if is_second else 1 << 32,
-            aliases={3: 0},
-        )(received, history, edge_force, full)
-
-    (full,) = edge("edge_first", False, first, full)
-    full, edges = edge("edge_second", True, second, full)
+    full, edges = call(
+        "edge",
+        edge_kernel,
+        (whole, single),
+        [VMEM] * 5,
+        [room(2, 2, columns, half, LANES), room(2, 2, columns, half, LANES), room(2, columns, half, LANES)],
+        cost=1 << 31,
+        aliases={4: 0},
+    )(first, second, history, edge_force, full)
     edges_high = lax.ppermute(edges, "image", line("image", -1))
     full_low = lax.ppermute(full, "image", line("image", 1))
     sums, plan = call(

time: 64 us -> 65.1 us (1.017)
  blocking collectives: 25.6 us -> 26.9 us
    all_to_all x1, blocking collectives: 16.7 us -> 17.9 us  [body(): parts = lax.all_to_all(parts, 'slab', 0, 0)]
    pallas_call x2 -> x1, Pallas kernels: 2.92 us -> 2.61 us  [body(): call('edge', edge_kernel, (whole, single), [VMEM] * 5, [room(2, 2, column...]
where the time goes in v9:
time: 65.1 us; the launch traced here: 64.8 us
  blocking collectives  26.9 us (41%)
  starting transfers between devices  24.9 us (38%)
  Pallas kernels  11.4 us (18%)
  waiting for transfers between devices  1.4 us (2%)
    all_to_all x1, blocking collectives, body(): parts = lax.all_to_all(parts, 'slab', 0, 0)  17.9 us
    ppermute x1, starting transfers between devices, body(): second = lax.ppermute(second, ('image', 'slab'), partners(False))  13.3 us
    all_to_all x1, blocking collectives, body(): squares = lax.all_to_all(squares, 'image', 0, 0)  9.07 us
    pallas_call x1, Pallas kernels, body(): call('inner', inner_kernel, (whole, single, array(2, 2, columns, 3 * ROWS...  5.27 us
    ppermute x1, starting transfers between devices, body(): first = lax.ppermute(first, ('image', 'slab'), partners(True))  4.03 us
    ppermute x1, starting transfers between devices, body(): full_low = lax.ppermute(full, 'image', line('image', 1))  3.44 us
    pallas_call x1, Pallas kernels, body(): call('edge', edge_kernel, (whole, single), [VMEM] * 5, [room(2, 2, column...  2.61 us
    ppermute x1, starting transfers between devices, body(): edges_high = lax.ppermute(edges, 'image', line('image', -1))  2.12 us
  transfers between devices with their start and end apart: 5, of which 1 were waited for; matrix products, arithmetic and copies ran while one was open for 0% of the time, Pallas kernels for 14%

profile of v9, /device:TPU:1, one launch (start us, length us, event | category | flops | bytes accessed | tf_op | source)
XLA Modules:
  0.0 64.8 jit_solution(1476069117662385220)
XLA Ops:
  0.0 0.0 copy-start.1
  0.0 0.0 copy-start
  0.0 1.3 %halo.1 = (f32[736,128]{1,0:T(8,128)S(1)}, f32[736,128]{1,0:T(8,128)S(1)}) custom-call(f32[2,32,4096]{2,1,0:T(8,128)} %string.3, f32[32,4096]{1,0:T(8,128)} %tilt.3), custom_call_target="tpu_custom_call" | custom-call | bytes 1048576 | tf_op jit(solution)/shard_map/halo/pallas_call | solution.py:279
  1.3 4.0 %collective-permute-start = (f32[736,128]{1,0:T(8,128)S(1)}, f32[736,128]{1,0:T(8,128)S(1)}, u32[]{:S(2)}, u32[]{:S(2)}) collective-permute-start(f32[736,128]{1,0:T(8,128)S(1)} %get-tuple-element.15), channel_id=1, source_target_pairs={{0,63},{63,0},{2,1},{1,2},{4,3},{3,4},{6,5},{5,6},{8,7},{7,8},{10,... | collective-permute-start | bytes 1130504 | tf_op jit(solution)/shard_map/ppermute | solution.py:287
  5.4 13.3 %collective-permute-start.1 = (f32[736,128]{1,0:T(8,128)S(1)}, f32[736,128]{1,0:T(8,128)S(1)}, u32[]{:S(2)}, u32[]{:S(2)}) collective-permute-start(f32[736,128]{1,0:T(8,128)S(1)} %get-tuple-element.16), channel_id=1, source_target_pairs={{0,1},{1,0},{2,3},{3,2},{4,5},{5,4},{6,7},{7,6},{8,9},{9,8},{10,11... | collective-permute-start | bytes 1130504 | tf_op jit(solution)/shard_map/ppermute | solution.py:288
  18.7 0.0 copy-done.1
  18.7 0.0 copy-done
  18.8 5.3 %inner.1 = (f32[2,32,32,128]{3,2,1,0:T(8,128)S(1)}, f32[32,16,128]{2,1,0:T(8,128)S(1)}, f32[2,2,32,24,128]{4,3,2,1,0:T(8,128)S(1)}, f32[2,32,8,128]{3,2,1,0:T(8,128)S(1)}) custom-call(f32[2,32,4096]{2,1,0:T(8,128)S(1)} %copy-done, f32[32,4096]{1,0:T(8,128)S(1)} %copy-done.1), custom_call_target="tpu_custom_call" | custom-call | flops 2147483648 | bytes 1048576 | tf_op jit(solution)/shard_map/inner/pallas_call | solution.py:291
  24.0 1.9 %collective-permute-start.2 = (f32[32,16,128]{2,1,0:T(8,128)S(1)}, f32[32,16,128]{2,1,0:T(8,128)S(1)}, u32[]{:S(2)}, u32[]{:S(2)}) collective-permute-start(f32[32,16,128]{2,1,0:T(8,128)S(1)} %get-tuple-element.21), channel_id=1, source_target_pairs={{64,0},{128,64},{192,128},{256,192},{320,256},{384,320},{448,384},... | collective-permute-start | bytes 786440 | tf_op jit(solution)/shard_map/ppermute | solution.py:299
  26.0 0.0 collective-permute-done.first
  26.0 0.0 collective-permute-done.1.second
  26.0 0.0 copy-start.2
  26.0 2.6 %edge.1 = (f32[2,32,32,128]{3,2,1,0:T(8,128)S(1)}, f32[32,16,128]{2,1,0:T(8,128)S(1)}) custom-call(f32[736,128]{1,0:T(8,128)S(1)} %collective-permute-done.first, f32[736,128]{1,0:T(8,128)S(1)} %collective-permute-done.1.second, f32[2,2,32,24,128]{4,3,2,1,0:T(8,128)S(1)} %get-tuple-element.17.history, ...), custom_call_target="tpu_custom_call", output_to_operand_aliasing={{0}: (4, {})} | custom-call | flops 2147483648 | bytes 1048576 | tf_op jit(solution)/shard_map/edge/pallas_call | solution.py:301
  28.6 2.1 %collective-permute-start.3 = (f32[32,16,128]{2,1,0:T(8,128)S(1)}, f32[32,16,128]{2,1,0:T(8,128)S(1)}, u32[]{:S(2)}, u32[]{:S(2)}) collective-permute-start(f32[32,16,128]{2,1,0:T(8,128)S(1)} %get-tuple-element.23), channel_id=1, source_target_pairs={{64,0},{128,64},{192,128},{256,192},{320,256},{384,320},{448,384},... | collective-permute-start | bytes 786440 | tf_op jit(solution)/shard_map/ppermute | solution.py:310
  30.7 3.4 %collective-permute-start.4 = (f32[2,32,32,128]{3,2,1,0:T(8,128)S(1)}, f32[2,32,32,128]{3,2,1,0:T(8,128)S(1)}, u32[]{:S(2)}, u32[]{:S(2)}) collective-permute-start(f32[2,32,32,128]{3,2,1,0:T(8,128)S(1)} %get-tuple-element.20.full), channel_id=1, source_target_pairs={{0,64},{64,128},{128,192},{192,256},{256,320},{320,384},{384,448},... | collective-permute-start | bytes 3145736 | tf_op jit(solution)/shard_map/ppermute | solution.py:311
  34.2 0.0 collective-permute-done.2.middle_high
  34.2 0.0 copy-done.2
  34.2 0.7 %local.1 = (f32[48,128]{1,0:T(8,128)S(1)}, f32[2,13,8,128]{3,2,1,0:T(8,128)S(1)}) custom-call(s32[16]{0:T(128)S(1)} %copy-done.2, f32[2,32,32,128]{3,2,1,0:T(8,128)S(1)} %get-tuple-element.20.full, f32[32,16,128]{2,1,0:T(8,128)S(1)} %collective-permute-done.2.middle_high), custom_call_target="tpu_custom_call" | custom-call | flops 268435456 | bytes 1048576 | tf_op jit(solution)/shard_map/local/pallas_call | solution.py:312
  34.9 1.4 %collective-permute-done.3.edges_high = f32[32,16,128]{2,1,0:T(8,128)S(1)} collective-permute-done((f32[32,16,128]{2,1,0:T(8,128)S(1)}, f32[32,16,128]{2,1,0:T(8,128)S(1)}, u32[]{:S(2)}, u32[]{:S(2)}) %collective-permute-start.3) | collective-permute-done | bytes 262176 | tf_op jit(solution)/shard_map/ppermute | solution.py:310
  36.3 0.2 square.1
  36.5 17.9 %all_to_all.10.parts = f32[64,1,128]{2,1,0:T(1,128)S(1)} all-to-all(f32[64,1,128]{2,1,0:T(1,128)S(1)} %square.1), channel_id=1, replica_groups=mesh['image'=8,'slab'=64] {'slab'}, dimensions={0} | all-to-all | bytes 65536 | tf_op jit(solution)/shard_map/all_to_all | solution.py:320
  54.4 0.0 collective-permute-done.4.full_low
  54.4 0.1 total.1
  54.5 9.1 %all_to_all.11.squares = f32[8,1,128]{2,1,0:T(1,128)S(1)} all-to-all(f32[8,1,128]{2,1,0:T(1,128)S(1)} %total.1), channel_id=1, replica_groups=mesh['image'=8,'slab'=64] {'image'}, dimensions={0} | all-to-all | bytes 8192 | tf_op jit(solution)/shard_map/all_to_all | solution.py:322
  63.6 1.2 %mix.1 = f32[2,32,4096]{2,1,0:T(8,128)} custom-call(f32[8,1,128]{2,1,0:T(1,128)S(1)} %all_to_all.11.squares, f32[2,13,8,128]{3,2,1,0:T(8,128)S(1)} %get-tuple-element.24.plan, f32[2,32,32,128]{3,2,1,0:T(8,128)S(1)} %get-tuple-element.20.full, f32[2,32,32,128]{3,2,1,0:T(8,128)S(1)} %collective-permute-done.4.full_low, ...), custom_call_target="tpu_custom_call" | custom-call | bytes 1048576 | tf_op jit(solution)/shard_map/mix/pallas_call | solution.py:324
Async XLA Ops:
  0.0 18.7 %copy-start.1 = (f32[32,4096]{1,0:T(8,128)S(1)}, f32[32,4096]{1,0:T(8,128)}, u32[]{:S(2)}) copy-start(f32[32,4096]{1,0:T(8,128)} %tilt.3) | copy-start | bytes 1572868
  0.0 18.7 %copy-start = (f32[2,32,4096]{2,1,0:T(8,128)S(1)}, f32[2,32,4096]{2,1,0:T(8,128)}, u32[]{:S(2)}) copy-start(f32[2,32,4096]{2,1,0:T(8,128)} %string.3) | copy-start | bytes 3145732
  1.3 24.6 %collective-permute-start = (f32[736,128]{1,0:T(8,128)S(1)}, f32[736,128]{1,0:T(8,128)S(1)}, u32[]{:S(2)}, u32[]{:S(2)}) collective-permute-start(f32[736,128]{1,0:T(8,128)S(1)} %get-tuple-element.15), channel_id=1, source_target_pairs={{0,63},{63,0},{2,1},{1,2},{4,3},{3,4},{6,5},{5,6},{8,7},{7,8},{10,... | collective-permute-start | bytes 1130504 | tf_op jit(solution)/shard_map/ppermute | solution.py:287
  5.4 20.6 %collective-permute-start.1 = (f32[736,128]{1,0:T(8,128)S(1)}, f32[736,128]{1,0:T(8,128)S(1)}, u32[]{:S(2)}, u32[]{:S(2)}) collective-permute-start(f32[736,128]{1,0:T(8,128)S(1)} %get-tuple-element.16), channel_id=1, source_target_pairs={{0,1},{1,0},{2,3},{3,2},{4,5},{5,4},{6,7},{7,6},{8,9},{9,8},{10,11... | collective-permute-start | bytes 1130504 | tf_op jit(solution)/shard_map/ppermute | solution.py:288
  24.0 10.2 %collective-permute-start.2 = (f32[32,16,128]{2,1,0:T(8,128)S(1)}, f32[32,16,128]{2,1,0:T(8,128)S(1)}, u32[]{:S(2)}, u32[]{:S(2)}) collective-permute-start(f32[32,16,128]{2,1,0:T(8,128)S(1)} %get-tuple-element.21), channel_id=1, source_target_pairs={{64,0},{128,64},{192,128},{256,192},{320,256},{384,320},{448,384},... | collective-permute-start | bytes 786440 | tf_op jit(solution)/shard_map/ppermute | solution.py:299
  26.0 8.2 %copy-start.2 = (s32[16]{0:T(128)S(1)}, s32[16]{0:T(128)}, u32[]{:S(2)}) copy-start(s32[16]{0:T(128)} %sources.1) | copy-start | bytes 196
  28.6 7.7 %collective-permute-start.3 = (f32[32,16,128]{2,1,0:T(8,128)S(1)}, f32[32,16,128]{2,1,0:T(8,128)S(1)}, u32[]{:S(2)}, u32[]{:S(2)}) collective-permute-start(f32[32,16,128]{2,1,0:T(8,128)S(1)} %get-tuple-element.23), channel_id=1, source_target_pairs={{64,0},{128,64},{192,128},{256,192},{320,256},{384,320},{448,384},... | collective-permute-start | bytes 786440 | tf_op jit(solution)/shard_map/ppermute | solution.py:310
  30.7 23.7 %collective-permute-start.4 = (f32[2,32,32,128]{3,2,1,0:T(8,128)S(1)}, f32[2,32,32,128]{3,2,1,0:T(8,128)S(1)}, u32[]{:S(2)}, u32[]{:S(2)}) collective-permute-start(f32[2,32,32,128]{3,2,1,0:T(8,128)S(1)} %get-tuple-element.20.full), channel_id=1, source_target_pairs={{0,64},{64,128},{128,192},{192,256},{256,320},{320,384},{384,448},... | collective-permute-start | bytes 3145736 | tf_op jit(solution)/shard_map/ppermute | solution.py:311
